TPU v7x, 32 devices: a whole 2x2x4 slice. The times are simulated.
32 devices in a mesh: dp: 8 (over z, core), fsdp: 4 (over y, x).
Axes of the slice: x: 2, y: 2, z: 4, core: 2. Of those that a mesh axis runs over, the one named last changes fastest.
Arguments:
- tokens: bfloat16 [32768, 768], P(('dp', 'fsdp')), may hold values from -6 to 6
- bucket: int32 [32], P(('dp', 'fsdp')), may hold values from 0 to 1, as said below
- lengths: int32 [32, 8], P(('dp', 'fsdp')), may hold values from 0 to 512, as said below
- cotangent: bfloat16 [32768, 768], P(('dp', 'fsdp')), may hold values from -6 to 6
- query_weight: bfloat16 [768, 768], P('dp', 'fsdp'), may hold values from -0.21875 to 0.21875
- query_bias: bfloat16 [768], P('fsdp'), may hold values from -3 to 3
- key_weight: bfloat16 [768, 768], P('dp', 'fsdp'), may hold values from -0.21875 to 0.21875
- value_weight: bfloat16 [768, 768], P('dp', 'fsdp'), may hold values from -0.21875 to 0.21875
- value_bias: bfloat16 [768], P('fsdp'), may hold values from -0.625 to 0.625
- out_weight: bfloat16 [768, 768], P('dp', 'fsdp'), may hold values from -2.5 to 2.5
- out_bias: bfloat16 [768], P('fsdp'), may hold values from -3 to 3
- norm1_gain: bfloat16 [768], P('fsdp'), may hold values from 0.5 to 1.5
- norm1_bias: bfloat16 [768], P('fsdp'), may hold values from -1.75 to 1.75
- up_weight: bfloat16 [768, 3072], P('dp', 'fsdp'), may hold values from -0.21875 to 0.21875
- up_bias: bfloat16 [3072], P('fsdp'), may hold values from -3 to 3
- down_weight: bfloat16 [3072, 768], P('dp', 'fsdp'), may hold values from -0.109375 to 0.109375
- down_bias: bfloat16 [768], P('fsdp'), may hold values from -3 to 3
- norm2_gain: bfloat16 [768], P('fsdp'), may hold values from 0.5 to 1.5
- norm2_bias: bfloat16 [768], P('fsdp'), may hold values from -1.75 to 1.75
Outputs:
- out_tokens: bfloat16 [32768, 768], P(('dp', 'fsdp'))
- pooled: float32 [256, 768], P(('dp', 'fsdp'))
- input_grad: float32 [32768, 768], P(('dp', 'fsdp'))
- grad_query_weight: float32 [768, 768], P('dp', 'fsdp')
- grad_query_bias: float32 [768], P('fsdp')
- grad_key_weight: float32 [768, 768], P('dp', 'fsdp')
- grad_value_weight: float32 [768, 768], P('dp', 'fsdp')
- grad_value_bias: float32 [768], P('fsdp')
- grad_out_weight: float32 [768, 768], P('dp', 'fsdp')
- grad_out_bias: float32 [768], P('fsdp')
- grad_norm1_gain: float32 [768], P('fsdp')
- grad_norm1_bias: float32 [768], P('fsdp')
- grad_up_weight: float32 [768, 3072], P('dp', 'fsdp')
- grad_up_bias: float32 [3072], P('fsdp')
- grad_down_weight: float32 [3072, 768], P('dp', 'fsdp')
- grad_down_bias: float32 [768], P('fsdp')
- grad_norm2_gain: float32 [768], P('fsdp')
- grad_norm2_bias: float32 [768], P('fsdp')
Inputs may be any that keep to these rules, and one draw needn't show every extreme that they name: `bucket`: both values occur. A device with 1 holds 2 passages of 512 rows, one with 0 holds 8 queries of 128 rows. `lengths`: entry j is the live length of the device's j-th sequence, 1 to 512 for passages and 1 to 128 for queries; entries j >= 2 of a passage device are 0. Some passage has 512 live tokens and some query 128.
All inputs are finite; a program needn't handle non-finite values.
Results may differ from a plain program's by a relative error of at most 0.02.
Values may be sent and summed in bfloat16 or wider, within the bound.
No kernel may reach another device: no remote copies, remote signals or barrier semaphores. Data moves between devices by JAX's collectives and lax.ppermute only.
A program may use at most 192 MiB of HBM per device.

v0:
```python
import jax
import jax.numpy as jnp
from jax import lax
from jax.sharding import PartitionSpec as P

H = 12
HD = 64
PLEN = 512
QLEN = 128


epsilon = 1e-06
masked_score = -1e30


def layer_norm(inputs, norm_gain, norm_shift):
    centred = inputs - jnp.mean(inputs, axis=-1, keepdims=True)
    spread = jnp.mean(centred * centred, axis=-1, keepdims=True)
    return centred * lax.rsqrt(spread + epsilon) * norm_gain + norm_shift


def exact_gelu(hidden):
    return jax.nn.gelu(hidden, approximate=False)


def layout(passage_flag, seq_lengths, row_count):
    row_index = jnp.arange(row_count, dtype=jnp.int32)
    segment = jnp.where(passage_flag == 1, row_index // PLEN, row_index // QLEN)
    position = jnp.where(passage_flag == 1, row_index % PLEN, row_index % QLEN)
    slot_index = jnp.arange(seq_lengths.shape[0], dtype=jnp.int32)
    member = segment[:, None] == slot_index[None, :]
    seq_limit = jnp.sum(jnp.where(member, seq_lengths[None, :], 0), axis=1)
    return (segment, position < seq_limit, member)


def head_view(tensor, seq_span):
    return tensor.reshape(tensor.shape[0] // seq_span, seq_span, H, HD)


def softmax_probs(queries, key_rows, segment, alive_rows, seq_span):
    block_segment = segment.reshape(-1, seq_span)
    block_alive = alive_rows.reshape(-1, seq_span)
    allowed = (block_segment[:, :, None] == block_segment[:, None, :]) & block_alive[:, None, :]
    raw_scores = jnp.einsum(
        "bqhd,bkhd->bhqk",
        head_view(queries, seq_span),
        head_view(key_rows, seq_span),
        preferred_element_type=jnp.float32,
    ) * HD ** (-0.5)
    scores = jnp.where(allowed[:, None], raw_scores, masked_score)
    highest = jnp.max(scores, axis=-1, keepdims=True)
    exponent = jnp.exp(scores - highest)
    return exponent / jnp.sum(exponent, axis=-1, keepdims=True)


def attend(queries, key_rows, values, segment, alive_rows, seq_span):
    probs_low = softmax_probs(queries, key_rows, segment, alive_rows, seq_span).astype(jnp.bfloat16)
    context = jnp.einsum(
        "bhqk,bkhd->bqhd",
        probs_low,
        head_view(values, seq_span),
        preferred_element_type=jnp.float32,
    )
    return context.reshape(queries.shape).astype(jnp.bfloat16)


def attend_back(queries, key_rows, values, segment, alive_rows, grad_context, seq_span):
    probs = softmax_probs(queries, key_rows, segment, alive_rows, seq_span)
    probs_low = probs.astype(jnp.bfloat16)
    grad_heads = head_view(grad_context, seq_span)
    grad_probs = jnp.einsum(
        "bqhd,bkhd->bhqk",
        grad_heads,
        head_view(values, seq_span),
        preferred_element_type=jnp.float32,
    )
    grad_values = jnp.einsum(
        "bhqk,bqhd->bkhd", probs_low, grad_heads, preferred_element_type=jnp.float32
    )
    grad_scores = (
        probs * (grad_probs - jnp.sum(grad_probs * probs, axis=-1, keepdims=True))
    ).astype(jnp.bfloat16)
    grad_queries = jnp.einsum(
        "bhqk,bkhd->bqhd",
        grad_scores,
        head_view(key_rows, seq_span),
        preferred_element_type=jnp.float32,
    ) * HD ** (-0.5)
    grad_keys = jnp.einsum(
        "bhqk,bqhd->bkhd",
        grad_scores,
        head_view(queries, seq_span),
        preferred_element_type=jnp.float32,
    ) * HD ** (-0.5)
    return tuple(
        (
            gradient.reshape(queries.shape).astype(jnp.bfloat16)
            for gradient in (grad_queries, grad_keys, grad_values)
        )
    )


def forward(tokens, passage_flag, segment, alive_rows, attention_set, feed_set):
    (
        query_weight,
        key_weight,
        value_weight,
        out_weight,
        query_bias,
        value_bias,
        out_bias,
        norm1_gain,
        norm1_bias,
    ) = attention_set
    up_weight, down_weight, up_bias, down_bias, norm2_gain, norm2_bias = feed_set
    queries = (
        jnp.dot(tokens, query_weight, preferred_element_type=jnp.float32)
        + query_bias.astype(jnp.float32)
    ).astype(jnp.bfloat16)
    key_rows = jnp.dot(tokens, key_weight, preferred_element_type=jnp.float32).astype(jnp.bfloat16)
    values = (
        jnp.dot(tokens, value_weight, preferred_element_type=jnp.float32)
        + value_bias.astype(jnp.float32)
    ).astype(jnp.bfloat16)
    context = lax.cond(
        passage_flag == 1,
        lambda: attend(queries, key_rows, values, segment, alive_rows, PLEN),
        lambda: attend(queries, key_rows, values, segment, alive_rows, QLEN),
    )
    residual_one = tokens.astype(jnp.float32) + (
        jnp.dot(context, out_weight, preferred_element_type=jnp.float32)
        + out_bias.astype(jnp.float32)
    )
    normed_one = layer_norm(
        residual_one, norm1_gain.astype(jnp.float32), norm1_bias.astype(jnp.float32)
    )
    normed_low = normed_one.astype(jnp.bfloat16)
    hidden = jnp.dot(normed_low, up_weight, preferred_element_type=jnp.float32) + up_bias.astype(
        jnp.float32
    )
    active = exact_gelu(hidden).astype(jnp.bfloat16)
    residual_two = normed_one + (
        jnp.dot(active, down_weight, preferred_element_type=jnp.float32)
        + down_bias.astype(jnp.float32)
    )
    result = layer_norm(
        residual_two, norm2_gain.astype(jnp.float32), norm2_bias.astype(jnp.float32)
    )
    return (
        result,
        (
            queries,
            key_rows,
            values,
            context,
            residual_one,
            normed_low,
            hidden,
            active,
            residual_two,
        ),
    )


def backward(
    tokens, passage_flag, segment, alive_rows, attention_set, feed_set, kept_state, grad_result
):
    (
        query_weight,
        key_weight,
        value_weight,
        out_weight,
        query_bias,
        value_bias,
        out_bias,
        norm1_gain,
        norm1_bias,
    ) = attention_set
    up_weight, down_weight, up_bias, down_bias, norm2_gain, norm2_bias = feed_set
    queries, key_rows, values, context, residual_one, normed_low, hidden, active, residual_two = (
        kept_state
    )
    second_pull = jax.vjp(
        layer_norm, residual_two, norm2_gain.astype(jnp.float32), norm2_bias.astype(jnp.float32)
    )[1]
    grad_mixed, grad_gain_two, grad_shift_two = second_pull(grad_result)
    grad_branch = grad_mixed.astype(jnp.bfloat16)
    grad_down_bias = jnp.sum(grad_branch.astype(jnp.float32), axis=0)
    grad_down_weight = jnp.einsum(
        "tf,td->fd", active, grad_branch, preferred_element_type=jnp.float32
    )
    grad_active = jnp.einsum(
        "td,fd->tf", grad_branch, down_weight, preferred_element_type=jnp.float32
    )
    gelu_pull = jax.vjp(exact_gelu, hidden)[1]
    grad_hidden = gelu_pull(grad_active)[0].astype(jnp.bfloat16)
    grad_up_bias = jnp.sum(grad_hidden.astype(jnp.float32), axis=0)
    grad_up_weight = jnp.einsum(
        "td,tf->df", normed_low, grad_hidden, preferred_element_type=jnp.float32
    )
    grad_normed = grad_mixed + jnp.einsum(
        "tf,df->td", grad_hidden, up_weight, preferred_element_type=jnp.float32
    )
    first_pull = jax.vjp(
        layer_norm, residual_one, norm1_gain.astype(jnp.float32), norm1_bias.astype(jnp.float32)
    )[1]
    grad_inner, grad_gain_one, grad_shift_one = first_pull(grad_normed)
    grad_attended = grad_inner.astype(jnp.bfloat16)
    grad_out_bias = jnp.sum(grad_attended.astype(jnp.float32), axis=0)
    grad_out_weight = jnp.einsum(
        "td,te->de", context, grad_attended, preferred_element_type=jnp.float32
    )
    grad_context = jnp.einsum(
        "te,de->td", grad_attended, out_weight, preferred_element_type=jnp.float32
    ).astype(jnp.bfloat16)
    grad_queries, grad_keys, grad_values = lax.cond(
        passage_flag == 1,
        lambda: attend_back(queries, key_rows, values, segment, alive_rows, grad_context, PLEN),
        lambda: attend_back(queries, key_rows, values, segment, alive_rows, grad_context, QLEN),
    )
    grad_query_bias = jnp.sum(grad_queries.astype(jnp.float32), axis=0)
    grad_value_bias = jnp.sum(grad_values.astype(jnp.float32), axis=0)
    grad_query_weight = jnp.einsum(
        "td,te->de", tokens, grad_queries, preferred_element_type=jnp.float32
    )
    grad_key_weight = jnp.einsum("td,te->de", tokens, grad_keys, preferred_element_type=jnp.float32)
    grad_value_weight = jnp.einsum(
        "td,te->de", tokens, grad_values, preferred_element_type=jnp.float32
    )
    grad_tokens = (
        grad_inner
        + jnp.einsum("te,de->td", grad_queries, query_weight, preferred_element_type=jnp.float32)
        + jnp.einsum("te,de->td", grad_keys, key_weight, preferred_element_type=jnp.float32)
        + jnp.einsum("te,de->td", grad_values, value_weight, preferred_element_type=jnp.float32)
    )
    attention_grads = (
        grad_query_weight,
        grad_key_weight,
        grad_value_weight,
        grad_out_weight,
        grad_query_bias,
        grad_value_bias,
        grad_out_bias,
        grad_gain_one,
        grad_shift_one,
    )
    feed_grads = (
        grad_up_weight,
        grad_down_weight,
        grad_up_bias,
        grad_down_bias,
        grad_gain_two,
        grad_shift_two,
    )
    return (grad_tokens, attention_grads, feed_grads)


def pool_rows(result, member, alive_rows):
    chosen = (member & alive_rows[:, None]).astype(jnp.float32)
    summed = jnp.einsum("tj,td->jd", chosen, result, precision=lax.Precision.HIGHEST)
    counted = jnp.sum(chosen, axis=0)
    return summed / jnp.maximum(counted, 1.0)[:, None]


def shards(
    tokens,
    bucket,
    lengths,
    cotangent,
    query_weight,
    query_bias,
    key_weight,
    value_weight,
    value_bias,
    out_weight,
    out_bias,
    norm1_gain,
    norm1_bias,
    up_weight,
    up_bias,
    down_weight,
    down_bias,
    norm2_gain,
    norm2_bias,
):
    passage_flag = bucket[0]
    segment, alive_rows, member = layout(passage_flag, lengths[0], tokens.shape[0])

    def collect_attention():
        inner_parts = (
            lax.all_gather(query_weight, "fsdp", axis=1, tiled=True),
            lax.all_gather(key_weight, "fsdp", axis=1, tiled=True),
            lax.all_gather(value_weight, "fsdp", axis=1, tiled=True),
            lax.all_gather(out_weight, "fsdp", axis=1, tiled=True),
            lax.all_gather(query_bias, "fsdp", axis=0, tiled=True),
            lax.all_gather(value_bias, "fsdp", axis=0, tiled=True),
            lax.all_gather(out_bias, "fsdp", axis=0, tiled=True),
            lax.all_gather(norm1_gain, "fsdp", axis=0, tiled=True),
            lax.all_gather(norm1_bias, "fsdp", axis=0, tiled=True),
        )
        matrices = (
            lax.all_gather(inner_parts[0], "dp", axis=0, tiled=True),
            lax.all_gather(inner_parts[1], "dp", axis=0, tiled=True),
            lax.all_gather(inner_parts[2], "dp", axis=0, tiled=True),
            lax.all_gather(inner_parts[3], "dp", axis=0, tiled=True),
        )
        return tuple(matrices) + tuple(inner_parts[4:])

    def collect_feed():
        inner_parts = (
            lax.all_gather(up_weight, "fsdp", axis=1, tiled=True),
            lax.all_gather(down_weight, "fsdp", axis=1, tiled=True),
            lax.all_gather(up_bias, "fsdp", axis=0, tiled=True),
            lax.all_gather(down_bias, "fsdp", axis=0, tiled=True),
            lax.all_gather(norm2_gain, "fsdp", axis=0, tiled=True),
            lax.all_gather(norm2_bias, "fsdp", axis=0, tiled=True),
        )
        matrices = (
            lax.all_gather(inner_parts[0], "dp", axis=0, tiled=True),
            lax.all_gather(inner_parts[1], "dp", axis=0, tiled=True),
        )
        return tuple(matrices) + tuple(inner_parts[2:])

    attention_set = collect_attention()
    feed_set = collect_feed()
    result, kept_state = forward(tokens, passage_flag, segment, alive_rows, attention_set, feed_set)
    attention_again = collect_attention()
    feed_again = collect_feed()
    kept_state = forward(tokens, passage_flag, segment, alive_rows, attention_again, feed_again)[1]
    grad_tokens, attention_grads, feed_grads = backward(
        tokens,
        passage_flag,
        segment,
        alive_rows,
        attention_again,
        feed_again,
        kept_state,
        cotangent.astype(jnp.float32),
    )
    feed_rows = (
        lax.psum_scatter(
            feed_grads[0].astype(jnp.bfloat16), "dp", scatter_dimension=0, tiled=True
        ).astype(jnp.float32),
        lax.psum_scatter(
            feed_grads[1].astype(jnp.bfloat16), "dp", scatter_dimension=0, tiled=True
        ).astype(jnp.float32),
    )
    feed_cols = (
        lax.psum_scatter(
            feed_rows[0].astype(jnp.bfloat16), "fsdp", scatter_dimension=1, tiled=True
        ).astype(jnp.float32),
        lax.psum_scatter(
            feed_rows[1].astype(jnp.bfloat16), "fsdp", scatter_dimension=1, tiled=True
        ).astype(jnp.float32),
        lax.psum_scatter(
            feed_grads[2].astype(jnp.bfloat16), "fsdp", scatter_dimension=0, tiled=True
        ).astype(jnp.float32),
        lax.psum_scatter(
            feed_grads[3].astype(jnp.bfloat16), "fsdp", scatter_dimension=0, tiled=True
        ).astype(jnp.float32),
        lax.psum_scatter(
            feed_grads[4].astype(jnp.bfloat16), "fsdp", scatter_dimension=0, tiled=True
        ).astype(jnp.float32),
        lax.psum_scatter(
            feed_grads[5].astype(jnp.bfloat16), "fsdp", scatter_dimension=0, tiled=True
        ).astype(jnp.float32),
    )
    attention_rows = (
        lax.psum_scatter(
            attention_grads[0].astype(jnp.bfloat16), "dp", scatter_dimension=0, tiled=True
        ).astype(jnp.float32),
        lax.psum_scatter(
            attention_grads[1].astype(jnp.bfloat16), "dp", scatter_dimension=0, tiled=True
        ).astype(jnp.float32),
        lax.psum_scatter(
            attention_grads[2].astype(jnp.bfloat16), "dp", scatter_dimension=0, tiled=True
        ).astype(jnp.float32),
        lax.psum_scatter(
            attention_grads[3].astype(jnp.bfloat16), "dp", scatter_dimension=0, tiled=True
        ).astype(jnp.float32),
    )
    attention_cols = (
        lax.psum_scatter(
            attention_rows[0].astype(jnp.bfloat16), "fsdp", scatter_dimension=1, tiled=True
        ).astype(jnp.float32),
        lax.psum_scatter(
            attention_rows[1].astype(jnp.bfloat16), "fsdp", scatter_dimension=1, tiled=True
        ).astype(jnp.float32),
        lax.psum_scatter(
            attention_rows[2].astype(jnp.bfloat16), "fsdp", scatter_dimension=1, tiled=True
        ).astype(jnp.float32),
        lax.psum_scatter(
            attention_rows[3].astype(jnp.bfloat16), "fsdp", scatter_dimension=1, tiled=True
        ).astype(jnp.float32),
        lax.psum_scatter(
            attention_grads[4].astype(jnp.bfloat16), "fsdp", scatter_dimension=0, tiled=True
        ).astype(jnp.float32),
        lax.psum_scatter(
            attention_grads[5].astype(jnp.bfloat16), "fsdp", scatter_dimension=0, tiled=True
        ).astype(jnp.float32),
        lax.psum_scatter(
            attention_grads[6].astype(jnp.bfloat16), "fsdp", scatter_dimension=0, tiled=True
        ).astype(jnp.float32),
        lax.psum_scatter(
            attention_grads[7].astype(jnp.bfloat16), "fsdp", scatter_dimension=0, tiled=True
        ).astype(jnp.float32),
        lax.psum_scatter(
            attention_grads[8].astype(jnp.bfloat16), "fsdp", scatter_dimension=0, tiled=True
        ).astype(jnp.float32),
    )
    summed_vectors = lax.psum(
        (
            attention_cols[4],
            attention_cols[5],
            attention_cols[6],
            attention_cols[7],
            attention_cols[8],
            feed_cols[2],
            feed_cols[3],
            feed_cols[4],
            feed_cols[5],
        ),
        "dp",
    )
    pooled = pool_rows(result, member, alive_rows)
    return (
        result.astype(jnp.bfloat16),
        pooled,
        grad_tokens,
        attention_cols[0],
        summed_vectors[0],
        attention_cols[1],
        attention_cols[2],
        summed_vectors[1],
        attention_cols[3],
        summed_vectors[2],
        summed_vectors[3],
        summed_vectors[4],
        feed_cols[0],
        summed_vectors[5],
        feed_cols[1],
        summed_vectors[6],
        summed_vectors[7],
        summed_vectors[8],
    )


def solution(mesh):
    in_specs = (
        P(("dp", "fsdp"), None),
        P(("dp", "fsdp")),
        P(("dp", "fsdp"), None),
        P(("dp", "fsdp"), None),
        P("dp", "fsdp"),
        P("fsdp"),
        P("dp", "fsdp"),
        P("dp", "fsdp"),
        P("fsdp"),
        P("dp", "fsdp"),
        P("fsdp"),
        P("fsdp"),
        P("fsdp"),
        P("dp", "fsdp"),
        P("fsdp"),
        P("dp", "fsdp"),
        P("fsdp"),
        P("fsdp"),
        P("fsdp"),
    )
    out_specs = (
        P(("dp", "fsdp"), None),
        P(("dp", "fsdp"), None),
        P(("dp", "fsdp"), None),
        P("dp", "fsdp"),
        P("fsdp"),
        P("dp", "fsdp"),
        P("dp", "fsdp"),
        P("fsdp"),
        P("dp", "fsdp"),
        P("fsdp"),
        P("fsdp"),
        P("fsdp"),
        P("dp", "fsdp"),
        P("fsdp"),
        P("dp", "fsdp"),
        P("fsdp"),
        P("fsdp"),
        P("fsdp"),
    )
    return jax.shard_map(shards, mesh=mesh, in_specs=in_specs, out_specs=out_specs, check_vma=False)
```

profile of v0, /device:TPU:0, one launch (start us, length us, event | category | flops | bytes accessed | tf_op | source)
XLA Modules:
  0.0 774.3 jit_solution(2931653193813368939)
XLA Ops:
  8.4 10.2 %all_gather.86 = bf16[96,768]{0,1:T(8,128)(2,1)S(1)} all-gather(bf16[96,192]{0,1:T(8,128)(2,1)S(1)} %copy.314), channel_id=1, replica_groups=mesh['dp'=8,'fsdp'=4] {'fsdp'}, dimensions={1}, use_global_device_ids=true | all-gather | bytes 184320 | tf_op jit(solution)/shard_map/all_gather | solution.py:292
  20.4 8.7 %all_gather.83 = bf16[96,768]{0,1:T(8,128)(2,1)S(1)} all-gather(bf16[96,192]{0,1:T(8,128)(2,1)S(1)} %copy.312), channel_id=1, replica_groups=mesh['dp'=8,'fsdp'=4] {'fsdp'}, dimensions={1}, use_global_device_ids=true | all-gather | bytes 184320 | tf_op jit(solution)/shard_map/all_gather | solution.py:291
  30.9 7.8 %all_gather.88 = bf16[96,768]{0,1:T(8,128)(2,1)S(1)} all-gather(bf16[96,192]{0,1:T(8,128)(2,1)S(1)} %copy.316), channel_id=1, replica_groups=mesh['dp'=8,'fsdp'=4] {'fsdp'}, dimensions={1}, use_global_device_ids=true | all-gather | bytes 184320 | tf_op jit(solution)/shard_map/all_gather | solution.py:293
  40.4 8.7 %all_gather.91 = bf16[96,768]{0,1:T(8,128)(2,1)S(1)} all-gather(bf16[96,192]{0,1:T(8,128)(2,1)S(1)} %copy.324), channel_id=1, replica_groups=mesh['dp'=8,'fsdp'=4] {'fsdp'}, dimensions={1}, use_global_device_ids=true | all-gather | bytes 184320 | tf_op jit(solution)/shard_map/all_gather | solution.py:294
  50.0 12.1 %all_gather.96 = bf16[96,3072]{1,0:T(8,128)(2,1)} all-gather(bf16[96,768]{1,0:T(8,128)(2,1)S(1)} %copy-done.40), channel_id=1, replica_groups=mesh['dp'=8,'fsdp'=4] {'fsdp'}, dimensions={1}, use_global_device_ids=true | all-gather | bytes 737280 | tf_op jit(solution)/shard_map/all_gather | solution.py:311
  62.2 10.9 %all_gather.99 = bf16[384,768]{0,1:T(8,128)(2,1)} all-gather(bf16[384,192]{0,1:T(8,128)(2,1)S(1)} %copy-done.41), channel_id=1, replica_groups=mesh['dp'=8,'fsdp'=4] {'fsdp'}, dimensions={1}, use_global_device_ids=true | all-gather | bytes 737280 | tf_op jit(solution)/shard_map/all_gather | solution.py:312
  76.8 15.1 %all-reduce.19 = (bf16[768]{0:T(1024)(128)(2,1)S(1)}, bf16[768]{0:T(1024)(128)(2,1)S(1)}, bf16[768]{0:T(1024)(128)(2,1)S(1)}, bf16[768]{0:T(1024)(128)(2,1)S(1)}...) all-reduce(bf16[768]{0:T(1024)(128)(2,1)S(1)} %dynamic-update-slice, ...), channel_id=1, replica_groups=mesh['dp'=8,'fsdp'=4] {'fsdp'}, use_global_device_ids=true, to_apply=%add | all-reduce | flops 5376 | bytes 21504
  93.2 7.3 all-gather
  106.4 3.7 add_convert_fusion.2
  110.2 4.9 add_convert_fusion.1
  115.1 51.7 %conditional.6 = (bf16[1024,768]{0,1:T(8,128)(2,1)S(1)}) conditional(s32[]{:T(128)} %convert_element_type.271, (s32[1024]{0:T(1024)S(1)}, pred[1024]{0:T(1024)(128)(4,1)S(1)}, bf16[1024,768]{1,0:T(8,128)(2,1)S(1)}, bf16[1024,768]{1,0:T(8,128)(2,1)S(1)}, bf16[1024,768]{1,0:T(8,128)(2,1)}) %tuple.44, (s32[1024]{0:T(1024)S(1)}, ...), branch_computations={%region_1.4_spmd, %region_4.7_spmd} | conditional | flops 1650196992 | bytes 95534144
  126.9 3.8 reshape.261
  133.6 3.9 reshape.260
  140.7 14.3 %fusion.152 = (f32[2,12,512]{2,1,0:T(8,128)S(1)}, f32[2,12,512,512]{2,3,1,0:T(8,128)}) fusion(pred[2,512,512]{1,2,0:T(8,128)(4,1)} %compare_and_fusion.1, bf16[2,512,12,64]{1,0,3,2:T(2,128)(2,1)S(1)} %copy-done.26, bf16[2,512,12,64]{1,0,3,2:T(2,128)(2,1)} %reshape.259), kind=kOutput, calls=%fused_computation.222 | convolution fusion | flops 830472704 | bytes 28884992 | tf_op jit(solution)/shard_map/cond/branch_1_fun/sub | solution.py:52
  155.0 9.8 %fusion.26 = bf16[2,512,12,64]{1,3,2,0:T(8,128)(2,1)S(1)} fusion(f32[2,12,512,512]{2,3,1,0:T(8,128)} %get-tuple-element.344, f32[2,12,512]{2,1,0:T(8,128)S(1)} %get-tuple-element.343, bf16[2,512,12,64]{1,0,3,2:T(2,128)(2,1)S(1)} %copy-done.23), kind=kOutput, calls=%fused_computation.32 | convolution fusion | flops 818675712 | bytes 28360704 | tf_op jit(solution)/shard_map/cond/branch_1_fun/bhqk,bkhd->bqhd/dot_general | solution.py:58
  168.0 3.8 fusion.172
  172.3 38.3 %multiply_convert_fusion.4 = (bf16[1024,3072]{1,0:T(8,128)(2,1)}, f32[1024,3072]{1,0:T(8,128)}, f32[1024,3072]{1,0:T(8,128)}) fusion(f32[3072]{0:T(1024)S(1)} %bitcast.208, bf16[768,3072]{1,0:T(8,128)(2,1)} %all-gather.16.cloned.1.call-done, f32[1024,768]{0,1:T(8,128)S(1)} %get-tuple-element.360, f32[768]{0:T(1024)S(1)} %convert_element_type.279, ...), kind=kOutput, calls=%fused_computation.105 | convolution fusion | flops 5043388416 | bytes 39348224 | tf_op jit(solution)/shard_map/dot_general | solution.py:138
  210.6 10.0 %all-gather.18.cloned.1.call-done = bf16[3072,768]{0,1:T(8,128)(2,1)} async-done(((bf16[384,768]{0,1:T(8,128)(2,1)}), bf16[3072,768]{0,1:T(8,128)(2,1)}) %all-gather.18.cloned.1.call-update) | async-done | bytes 4718608 | tf_op jit(solution)/shard_map/all_gather | solution.py:320
  220.7 9.3 %fusion.173 = (f32[1024]{0:T(1024)S(1)}, f32[1024,768]{0,1:T(8,128)S(1)}) fusion(f32[768]{0:T(1024)S(1)} %copy-done.60, bf16[1024,3072]{1,0:T(8,128)(2,1)} %get-tuple-element.339, bf16[3072,768]{0,1:T(8,128)(2,1)} %all-gather.18.cloned.1.call-done, f32[768]{0:T(1024)S(1)} %convert_element_type.279, f32[768]{0:T(1024)S(1)} %convert_element_type.278, ...), kind=kOutput, calls=%fused_computation.227 | convolution fusion | flops 4837342208 | bytes 17323008 | tf_op jit(solution)/shard_map/dot_general | solution.py:143
  234.8 19.1 %fusion.174 = (bf16[3072]{0:T(1024)(128)(2,1)}, bf16[1024,3072]{1,0:T(8,128)(2,1)}) fusion(f32[1024,3072]{1,0:T(8,128)} %get-tuple-element.340, bf16[1024,768]{0,1:T(8,128)(2,1)S(1)} %get-tuple-element.334, bf16[3072,768]{0,1:T(8,128)(2,1)} %all-gather.18.cloned.1.call-done, f32[1024,3072]{1,0:T(8,128)} %get-tuple-element.361, f32[3072]{0:T(1024)S(1)} %bitcast.209), kind=kOutput, calls=%fused_computation.228 | convolution fusion | flops 4882166784 | bytes 37767168 | tf_op jit(solution)/shard_map/td,fd->tf/dot_general | solution.py:192
  253.9 10.9 %multiply_reduce_fusion.2 = (bf16[768]{0:T(1024)(128)(2,1)}, f32[1024]{0:T(1024)S(1)}, bf16[768]{0:T(1024)(128)(2,1)}, f32[1024,768]{0,1:T(8,128)S(1)}) fusion(f32[1024,768]{0,1:T(8,128)S(1)} %get-tuple-element.360, f32[1024]{0:T(1024)S(1)} %fusion.136, f32[1024]{0:T(1024)S(1)} %broadcast_multiply_fusion.1, f32[768]{0:T(1024)S(1)} %convert_element_type.278, ...), kind=kOutput, calls=%fused_computation.129 | convolution fusion | flops 4845204480 | bytes 22057984 | tf_op jit(solution)/shard_map/tf,df->td/dot_general | solution.py:201
  272.2 4.5 convolution_convert_fusion.2
  276.7 112.1 %conditional.7 = (bf16[1024,768]{0,1:T(8,128)(2,1)}, bf16[1024,768]{0,1:T(8,128)(2,1)}, bf16[1024,768]{0,1:T(8,128)(2,1)S(1)}) conditional(s32[]{:T(128)} %convert_element_type.271, (s32[1024]{0:T(1024)S(1)}, pred[1024]{0:T(1024)(128)(4,1)S(1)}, bf16[1024,768]{1,0:T(8,128)(2,1)S(1)}, bf16[1024,768]{1,0:T(8,128)(2,1)S(1)}, ...), branch_computations={%region_16.20_spmd, %region_20.24_spmd} | conditional | flops 4112503296 | bytes 275037344
  279.8 3.8 reshape.271
  287.4 3.9 reshape.270
  300.3 14.8 %fusion.162 = (f32[2,12,512]{2,1,0:T(8,128)S(1)}, f32[2,12,512,512]{2,3,1,0:T(8,128)}) fusion(pred[2,512,512]{1,2,0:T(8,128)(4,1)} %compare_and_fusion.3, bf16[2,512,12,64]{1,0,3,2:T(2,128)(2,1)S(1)} %reshape.269, bf16[2,512,12,64]{1,0,3,2:T(2,128)(2,1)S(1)} %reshape.268), kind=kOutput, calls=%fused_computation.224 | convolution fusion | flops 830472704 | bytes 28884992 | tf_op jit(solution)/shard_map/cond/branch_1_fun/sub | solution.py:52
  315.1 10.7 %fusion.73 = bf16[2,512,12,64]{1,3,2,0:T(8,128)(2,1)S(1)} fusion(bf16[2,512,12,64]{1,0,3,2:T(2,128)(2,1)} %reshape.270, f32[2,12,512,512]{2,3,1,0:T(8,128)} %get-tuple-element.352, f32[2,12,512]{2,1,0:T(8,128)S(1)} %get-tuple-element.351), kind=kOutput, calls=%fused_computation.87 | convolution fusion | flops 817889280 | bytes 28360704 | tf_op jit(solution)/shard_map/cond/branch_1_fun/bhqk,bqhd->bkhd/dot_general | solution.py:77
  329.0 16.7 %multiply_reduce_fusion.1 = (f32[2,12,512]{2,1,0:T(8,128)S(1)}, f32[2,12,512,512]{2,3,1,0:T(8,128)}) fusion(f32[2,12,512,512]{2,3,1,0:T(8,128)} %get-tuple-element.352, f32[2,12,512]{2,1,0:T(8,128)S(1)} %get-tuple-element.351, bf16[2,512,12,64]{1,0,3,2:T(2,128)(2,1)S(1)} %copy-done.18, bf16[2,512,12,64]{1,0,3,2:T(2,128)(2,1)} %reshape.270), kind=kOutput, calls=%fused_computation.73 | convolution fusion | flops 824168448 | bytes 53575680 | tf_op jit(solution)/shard_map/cond/branch_1_fun/bqhd,bkhd->bhqk/dot_general | solution.py:71
  345.6 21.4 %multiply_convert_fusion.2 = bf16[2,12,512,512]{2,3,1,0:T(8,128)(2,1)} fusion(f32[2,12,512,512]{2,3,1,0:T(8,128)} %get-tuple-element.354, f32[2,12,512]{2,1,0:T(8,128)S(1)} %get-tuple-element.353, f32[2,12,512,512]{2,3,1,0:T(8,128)} %get-tuple-element.352, f32[2,12,512]{2,1,0:T(8,128)S(1)} %get-tuple-element.351), kind=kLoop, calls=%fused_computation.72 | loop fusion | flops 25165824 | bytes 63012864 | tf_op jit(solution)/shard_map/cond/branch_1_fun/convert_element_type | solution.py:82
  367.0 9.7 %fusion.78 = bf16[2,512,12,64]{1,3,2,0:T(8,128)(2,1)} fusion(bf16[2,12,512,512]{2,3,1,0:T(8,128)(2,1)} %multiply_convert_fusion.2, bf16[2,512,12,64]{1,0,3,2:T(2,128)(2,1)S(1)} %copy-done.21), kind=kOutput, calls=%fused_computation.90 | convolution fusion | flops 806879232 | bytes 15728640 | tf_op jit(solution)/shard_map/cond/branch_1_fun/bhqk,bqhd->bkhd/dot_general | solution.py:89
  376.6 6.7 multiply_bitcast_fusion.1
  403.1 9.8 %convolution_convert_fusion = bf16[3072,768]{1,0:T(8,128)(2,1)} fusion(bf16[1024,3072]{1,0:T(8,128)(2,1)} %get-tuple-element.339, bf16[1024,768]{0,1:T(8,128)(2,1)S(1)} %copy-done.32), kind=kOutput, calls=%fused_computation.119 | convolution fusion | flops 4834197504 | bytes 12582912 | tf_op jit(solution)/shard_map/tf,td->fd/dot_general | solution.py:189
  414.8 9.8 %convolution_convert_fusion.1 = bf16[768,3072]{1,0:T(8,128)(2,1)} fusion(bf16[1024,3072]{1,0:T(8,128)(2,1)} %get-tuple-element.366, f32[1024,768]{0,1:T(8,128)S(1)} %copy-done.10, f32[768]{0:T(1024)S(1)} %copy-done.59, f32[768]{0:T(1024)S(1)} %copy-done.51, f32[1024]{0:T(1024)S(1)} %copy-done.53, f32[1024]{0:T(1024)S(1)} %copy-done.49), kind=kOutput, calls=%fused_computation.120 | convolution fusion | flops 4838129664 | bytes 14170112 | tf_op jit(solution)/shard_map/td,tf->df/dot_general | solution.py:198
  428.6 30.8 %reduce-scatter.37.cloned.1.call-done = bf16[96,768]{1,0:T(8,128)(2,1)} async-done(((bf16[768,768]{1,0:T(8,128)(2,1)}), bf16[96,768]{1,0:T(8,128)(2,1)}) %reduce-scatter.37.cloned.1.call-update) | async-done | bytes 147472
  463.0 29.5 %reduce-scatter.41.cloned.1.call-done = bf16[96,768]{1,0:T(8,128)(2,1)} async-done(((bf16[768,768]{1,0:T(8,128)(2,1)}), bf16[96,768]{1,0:T(8,128)(2,1)}) %reduce-scatter.41.cloned.1.call-update) | async-done | bytes 147472
  494.5 53.4 %reduce-scatter.35.cloned.1.call-done = bf16[384,768]{1,0:T(8,128)(2,1)} async-done(((bf16[3072,768]{1,0:T(8,128)(2,1)}), bf16[384,768]{1,0:T(8,128)(2,1)}) %reduce-scatter.35.cloned.1.call-update) | async-done | bytes 589840 | tf_op jit(solution)/shard_map/reduce_scatter | solution.py:344
  550.2 4.3 fusion.175
  558.1 16.6 %all-reduce.18 = (bf16[768]{0:T(1024)(128)(2,1)S(1)}, bf16[768]{0:T(1024)(128)(2,1)S(1)}, bf16[768]{0:T(1024)(128)(2,1)S(1)}, bf16[768]{0:T(1024)(128)(2,1)S(1)}...) all-reduce(bf16[768]{0:T(1024)(128)(2,1)S(1)} %dynamic-update-slice, ...), channel_id=1, replica_groups=mesh['dp'=8,'fsdp'=4] {'fsdp'}, use_global_device_ids=true, to_apply=%add.7 | all-reduce | flops 9984 | bytes 39936
  574.7 3.0 fusion.176
  578.4 4.7 add_add_fusion.2
  583.1 20.4 %reduce-scatter.31.cloned.1.call-done = bf16[96,3072]{1,0:T(8,128)(2,1)} async-done(((bf16[768,3072]{1,0:T(8,128)(2,1)}), bf16[96,3072]{1,0:T(8,128)(2,1)}) %reduce-scatter.31.cloned.1.call-update) | async-done | bytes 589840 | tf_op jit(solution)/shard_map/reduce_scatter | solution.py:341
  607.7 3.5 copy.340
  611.6 25.9 %all-reduce.17 = (f32[192]{0:T(256)}, f32[192]{0:T(256)}, f32[192]{0:T(256)}, f32[192]{0:T(256)}, f32[192]{0:T(256)}, /*index=5*/f32[768]{0:T(1024)}, f32[192]{0:T(256)}, f32[192]{0:T(256)}, f32[192]{0:T(256)}) all-reduce(f32[192]{0:T(256)S(1)} %get-tuple-element.374, ...), channel_id=1, replica_groups=mesh['dp'=8,'fsdp'=4] {'dp'}, use_global_device_ids=true, to_apply=%region_28.29 | all-reduce | flops 2304 | bytes 18432 | tf_op jit(solution)/shard_map/psum | solution.py:411
  641.7 14.1 %reduce-scatter.25.cloned.1.call-done = bf16[96,192]{0,1:T(8,128)(2,1)} async-done(((bf16[96,768]{0,1:T(8,128)(2,1)}), bf16[96,192]{0,1:T(8,128)(2,1)}) %reduce-scatter.25.cloned.1.call-update) | async-done | bytes 36880 | tf_op jit(solution)/shard_map/reduce_scatter | solution.py:386
  657.3 25.7 %reduce-scatter.23.cloned.1.call-done = bf16[96,192]{0,1:T(8,128)(2,1)} async-done(((bf16[96,768]{0,1:T(8,128)(2,1)}), bf16[96,192]{0,1:T(8,128)(2,1)}) %reduce-scatter.23.cloned.1.call-update) | async-done | bytes 36880 | tf_op jit(solution)/shard_map/reduce_scatter | solution.py:383
  684.5 25.1 %reduce-scatter.27.cloned.1.call-done = bf16[96,192]{0,1:T(8,128)(2,1)} async-done(((bf16[96,768]{0,1:T(8,128)(2,1)}), bf16[96,192]{0,1:T(8,128)(2,1)}) %reduce-scatter.27.cloned.1.call-update) | async-done | bytes 36880 | tf_op jit(solution)/shard_map/reduce_scatter | solution.py:389
  711.1 26.3 %reduce-scatter.45.cloned.1.call-done = bf16[192,384]{1,0:T(8,128)(2,1)} async-done(((bf16[768,384]{1,0:T(8,128)(2,1)}), bf16[192,384]{1,0:T(8,128)(2,1)}) %reduce-scatter.45.cloned.1.call-update) | async-done | bytes 147472
  739.3 26.2 %reduce-scatter.33.cloned.1.call-done = bf16[96,768]{1,0:T(8,128)(2,1)} async-done(((bf16[96,3072]{1,0:T(8,128)(2,1)}), bf16[96,768]{1,0:T(8,128)(2,1)}) %reduce-scatter.33.cloned.1.call-update) | async-done | bytes 147472 | tf_op jit(solution)/shard_map/reduce_scatter | solution.py:349
  (297 shorter events, 112.6 us)
Async XLA Ops:
  7.2 66.6 %copy-start.63 = (u32[32]{0:T(128)S(1)}, u32[32]{0:T(128)}, u32[]{:S(2)}) copy-start(u32[32]{0:T(128)} %constant.199) | copy-start | bytes 388
  7.2 42.8 %copy-start.40 = (bf16[96,768]{1,0:T(8,128)(2,1)S(1)}, bf16[96,768]{1,0:T(8,128)(2,1)}, u32[]{:S(2)}) copy-start(bf16[96,768]{1,0:T(8,128)(2,1)} %param.36) | copy-start | bytes 442372
  7.2 54.9 %copy-start.41 = (bf16[384,192]{0,1:T(8,128)(2,1)S(1)}, bf16[384,192]{0,1:T(8,128)(2,1)}, u32[]{:S(2)}) copy-start(bf16[384,192]{0,1:T(8,128)(2,1)} %param.38) | copy-start | bytes 442372
  7.2 67.9 %copy-start.67 = (bf16[192]{0:T(256)(128)(2,1)S(1)}, bf16[192]{0:T(256)(128)(2,1)}, u32[]{:S(2)}) copy-start(bf16[192]{0:T(256)(128)(2,1)} %param.40) | copy-start | bytes 1156
  7.2 68.1 %copy-start.68 = (bf16[192]{0:T(256)(128)(2,1)S(1)}, bf16[192]{0:T(256)(128)(2,1)}, u32[]{:S(2)}) copy-start(bf16[192]{0:T(256)(128)(2,1)} %param.39) | copy-start | bytes 1156
  7.2 68.3 %copy-start.69 = (bf16[192]{0:T(256)(128)(2,1)S(1)}, bf16[192]{0:T(256)(128)(2,1)}, u32[]{:S(2)}) copy-start(bf16[192]{0:T(256)(128)(2,1)} %param.34) | copy-start | bytes 1156
  7.3 68.6 %copy-start.70 = (bf16[192]{0:T(256)(128)(2,1)S(1)}, bf16[192]{0:T(256)(128)(2,1)}, u32[]{:S(2)}) copy-start(bf16[192]{0:T(256)(128)(2,1)} %param.35) | copy-start | bytes 1156
  7.3 68.8 %copy-start.71 = (bf16[192]{0:T(256)(128)(2,1)S(1)}, bf16[192]{0:T(256)(128)(2,1)}, u32[]{:S(2)}) copy-start(bf16[192]{0:T(256)(128)(2,1)} %param.33) | copy-start | bytes 1156
  7.3 69.0 %copy-start.72 = (bf16[192]{0:T(256)(128)(2,1)S(1)}, bf16[192]{0:T(256)(128)(2,1)}, u32[]{:S(2)}) copy-start(bf16[192]{0:T(256)(128)(2,1)} %param.31) | copy-start | bytes 1156
  7.3 69.2 %copy-start.73 = (bf16[192]{0:T(256)(128)(2,1)S(1)}, bf16[192]{0:T(256)(128)(2,1)}, u32[]{:S(2)}) copy-start(bf16[192]{0:T(256)(128)(2,1)} %param.28) | copy-start | bytes 1156
  7.3 84.5 %copy-start.64 = (bf16[768]{0:T(1024)(128)(2,1)S(1)}, bf16[768]{0:T(1024)(128)(2,1)}, u32[]{:S(2)}) copy-start(bf16[768]{0:T(1024)(128)(2,1)} %param.37) | copy-start | bytes 4612
  7.3 85.1 %copy-start.65 = (s32[1,8]{1,0:T(1,128)S(1)}, s32[1,8]{1,0:T(1,128)}, u32[]{:S(2)}) copy-start(s32[1,8]{1,0:T(1,128)} %param.25) | copy-start | bytes 100
  7.3 93.2 %copy-start.11 = (bf16[1024,768]{1,0:T(8,128)(2,1)S(1)}, bf16[1024,768]{1,0:T(8,128)(2,1)}, u32[]{:S(2)}) copy-start(bf16[1024,768]{1,0:T(8,128)(2,1)} %param.26) | copy-start | bytes 4718596
  7.3 96.4 %all-gather.10.cloned.1.call-start = ((), (), s32[]{:S(2)}) async-start(), calls=%async_computation.13 | async-start | bytes 1327104 | tf_op jit(solution)/shard_map/all_gather | solution.py:303
  19.4 87.0 %all-gather.8.cloned.1.call-start = ((), (), s32[]{:S(2)}) async-start(), calls=%async_computation.12 | async-start | bytes 1327104 | tf_op jit(solution)/shard_map/all_gather | solution.py:302
  29.9 80.3 %all-gather.12.cloned.1.call-start = ((), (), s32[]{:S(2)}) async-start(), calls=%async_computation.14 | async-start | bytes 1327104 | tf_op jit(solution)/shard_map/all_gather | solution.py:304
  39.4 128.5 %all-gather.14.cloned.1.call-start = ((), (), s32[]{:S(2)}) async-start(), calls=%async_computation.15 | async-start | bytes 1327104 | tf_op jit(solution)/shard_map/all_gather | solution.py:305
  49.9 52.2 %copy-start.16 = (bf16[1024,768]{1,0:T(8,128)(2,1)S(1)}, bf16[1024,768]{1,0:T(8,128)(2,1)}, u32[]{:S(2)}) copy-start(bf16[1024,768]{1,0:T(8,128)(2,1)} %param.23) | copy-start | bytes 4718596
  49.9 122.3 %all-gather.16.cloned.1.call-start = ((), (), s32[]{:S(2)}) async-start(), calls=%async_computation.16 | async-start | bytes 5308416 | tf_op jit(solution)/shard_map/all_gather | solution.py:319
  62.1 158.5 %all-gather.18.cloned.1.call-start = ((), (), s32[]{:S(2)}) async-start(), calls=%async_computation.17 | async-start | bytes 5308416 | tf_op jit(solution)/shard_map/all_gather | solution.py:320
  73.1 351.7 %reduce-scatter.29.cloned.1.call-start = ((), (), s32[]{:S(2)}) async-start(), calls=%async_computation.21 | async-start | bytes 1327104 | tf_op jit(solution)/shard_map/reduce_scatter | solution.py:378
  73.8 41.2 %copy-start.34 = (s32[1024]{0:T(1024)}, s32[1024]{0:T(1024)S(1)}, u32[]{:S(2)}) copy-start(s32[1024]{0:T(1024)S(1)} %fusion.132) | copy-start | bytes 12292
  92.4 172.5 %copy-start.50 = (f32[768]{0:T(1024)}, f32[768]{0:T(1024)S(1)}, u32[]{:S(2)}) copy-start(f32[768]{0:T(1024)S(1)} %convert_element_type.278) | copy-start | bytes 9220
  92.4 128.2 %copy-start.58 = (f32[768]{0:T(1024)}, f32[768]{0:T(1024)S(1)}, u32[]{:S(2)}) copy-start(f32[768]{0:T(1024)S(1)} %convert_element_type.279) | copy-start | bytes 9220
  171.8 93.1 %copy-start.9 = (f32[1024,768]{0,1:T(8,128)}, f32[1024,768]{0,1:T(8,128)S(1)}, u32[]{:S(2)}) copy-start(f32[1024,768]{0,1:T(8,128)S(1)} %get-tuple-element.360) | copy-start | bytes 9437188
  171.8 93.1 %copy-start.48 = (f32[1024]{0:T(1024)}, f32[1024]{0:T(1024)S(1)}, u32[]{:S(2)}) copy-start(f32[1024]{0:T(1024)S(1)} %broadcast_multiply_fusion.1) | copy-start | bytes 12292
  172.2 92.7 %copy-start.52 = (f32[1024]{0:T(1024)}, f32[1024]{0:T(1024)S(1)}, u32[]{:S(2)}) copy-start(f32[1024]{0:T(1024)S(1)} %fusion.136) | copy-start | bytes 12292
  172.3 48.4 %copy-start.60 = (f32[768]{0:T(1024)S(1)}, f32[768]{0:T(1024)}, u32[]{:S(2)}) copy-start(f32[768]{0:T(1024)} %convert_element_type.283) | copy-start | bytes 9220
  229.9 24.0 %copy-start = (f32[1024,768]{0,1:T(8,128)}, f32[1024,768]{0,1:T(8,128)S(1)}, u32[]{:S(2)}) copy-start(f32[1024,768]{0,1:T(8,128)S(1)} %get-tuple-element.363) | copy-start | bytes 9437188
  230.0 24.0 %copy-start.38 = (f32[1024]{0:T(1024)}, f32[1024]{0:T(1024)S(1)}, u32[]{:S(2)}) copy-start(f32[1024]{0:T(1024)S(1)} %broadcast_multiply_fusion) | copy-start | bytes 12292
  272.1 154.6 %reduce-scatter.39.cloned.1.call-start = ((), (), s32[]{:S(2)}) async-start(), calls=%async_computation.26 | async-start | bytes 1327104
  394.3 65.1 %reduce-scatter.37.cloned.1.call-start = ((), (), s32[]{:S(2)}) async-start(), calls=%async_computation.25 | async-start | bytes 1327104
  398.6 93.9 %reduce-scatter.41.cloned.1.call-start = ((), (), s32[]{:S(2)}) async-start(), calls=%async_computation.27 | async-start | bytes 1327104
  403.0 144.9 %reduce-scatter.35.cloned.1.call-start = ((), (), s32[]{:S(2)}) async-start(), calls=%async_computation.24 | async-start | bytes 5308416 | tf_op jit(solution)/shard_map/reduce_scatter | solution.py:344
  413.0 190.5 %reduce-scatter.31.cloned.1.call-start = ((), (), s32[]{:S(2)}) async-start(), calls=%async_computation.22 | async-start | bytes 5308416 | tf_op jit(solution)/shard_map/reduce_scatter | solution.py:341
  424.7 37.8 %copy-start.12 = (bf16[1024,768]{1,0:T(8,128)(2,1)S(1)}, bf16[1024,768]{1,0:T(8,128)(2,1)}, u32[]{:S(2)}) copy-start(bf16[1024,768]{1,0:T(8,128)(2,1)} %param.26) | copy-start | bytes 4718596
  424.7 38.1 %copy-start.74 = (bf16[192]{0:T(256)(128)(2,1)S(1)}, bf16[192]{0:T(256)(128)(2,1)}, u32[]{:S(2)}) copy-start(bf16[192]{0:T(256)(128)(2,1)} %param.41) | copy-start | bytes 1156
  424.7 125.5 %copy-start.28 = (bf16[1024,768]{0,1:T(8,128)(2,1)S(1)}, bf16[1024,768]{0,1:T(8,128)(2,1)}, u32[]{:S(2)}) copy-start(bf16[1024,768]{0,1:T(8,128)(2,1)} %copy-done.27) | copy-start | bytes 4718596
  424.7 215.5 %reduce-scatter.43.cloned.1.call-start = ((), (), s32[]{:S(2)}) async-start(), calls=%async_computation.28 | async-start | bytes 245760
  426.7 229.1 %reduce-scatter.25.cloned.1.call-start = ((), (), s32[]{:S(2)}) async-start(), calls=%async_computation.19 | async-start | bytes 245760 | tf_op jit(solution)/shard_map/reduce_scatter | solution.py:386
  428.5 254.4 %reduce-scatter.23.cloned.1.call-start = ((), (), s32[]{:S(2)}) async-start(), calls=%async_computation.18 | async-start | bytes 245760 | tf_op jit(solution)/shard_map/reduce_scatter | solution.py:383
  461.1 248.4 %reduce-scatter.27.cloned.1.call-start = ((), (), s32[]{:S(2)}) async-start(), calls=%async_computation.20 | async-start | bytes 245760 | tf_op jit(solution)/shard_map/reduce_scatter | solution.py:389
  494.3 243.1 %reduce-scatter.45.cloned.1.call-start = ((), (), s32[]{:S(2)}) async-start(), calls=%async_computation.29 | async-start | bytes 737280
  550.1 215.4 %reduce-scatter.33.cloned.1.call-start = ((), (), s32[]{:S(2)}) async-start(), calls=%async_computation.23 | async-start | bytes 737280 | tf_op jit(solution)/shard_map/reduce_scatter | solution.py:349
  578.4 25.1 %copy-start.1 = (f32[1024,768]{0,1:T(8,128)S(1)}, f32[1024,768]{0,1:T(8,128)}, u32[]{:S(2)}) copy-start(f32[1024,768]{0,1:T(8,128)} %copy-done) | copy-start | bytes 9437188
  578.4 25.1 %copy-start.37 = (f32[768]{0:T(1024)S(1)}, f32[768]{0:T(1024)}, u32[]{:S(2)}) copy-start(f32[768]{0:T(1024)} %convert_element_type.284) | copy-start | bytes 9220
  578.4 25.1 %copy-start.39 = (f32[1024]{0:T(1024)S(1)}, f32[1024]{0:T(1024)}, u32[]{:S(2)}) copy-start(f32[1024]{0:T(1024)} %copy-done.38) | copy-start | bytes 12292
  578.4 25.1 %copy-start.43 = (f32[1024]{0:T(1024)S(1)}, f32[1024]{0:T(1024)}, u32[]{:S(2)}) copy-start(f32[1024]{0:T(1024)} %copy-done.42) | copy-start | bytes 12292
  (41 other events, 254.1 us)
Sparse Core Ops, SparseCore 0:
  19.5 22.9 all-gather.9
  44.7 22.4 all-gather.7
  69.4 22.4 all-gather.11
  93.4 22.4 all-gather.13
  117.3 51.4 all-gather.15
  170.3 50.2 all-gather.17
  272.2 31.5 reduce-scatter.28
  394.4 31.5 reduce-scatter.38
  428.3 31.0 reduce-scatter.36
  461.5 30.9 reduce-scatter.40
  494.8 53.0 reduce-scatter.34
  550.0 53.3 reduce-scatter.30
  606.2 22.3 reduce-scatter.42
  631.8 23.9 reduce-scatter.24
  658.9 23.9 reduce-scatter.22
  685.6 23.9 reduce-scatter.26
  712.3 25.0 reduce-scatter.44
  740.4 25.0 reduce-scatter.32
where the time goes:
time: 783 us; the launch traced here: 774 us
  waiting for transfers between devices  262 us (33%)
  matrix products  225 us (29%)
  blocking collectives  123 us (16%)
  local copies, waits for them, and re-layouts  95.2 us (12%)
  other arithmetic  40.4 us (5%)
  between operations  18.1 us (2%)
  loops' own time  9.95 us (1%)
    unnamed x23, waiting for transfers between devices  86.9 us
    reduce_scatter x1, waiting for transfers between devices, shards(): lax.psum_scatter(feed_grads[1].astype(jnp.bfloat16), 'dp', scatter_dimens...  53.4 us
    unnamed x170, local copies, waits for them, and re-layouts  44.4 us
    dot_general x1, matrix products, forward(): jnp.dot(normed_low, up_weight, preferred_element_type=jnp.float32)  38.3 us
    unnamed x2, blocking collectives  31.7 us
    sub x2, matrix products, softmax_probs(): exponent = jnp.exp(scores - highest)  29.1 us
    reduce_scatter x1, waiting for transfers between devices, shards(): lax.psum_scatter(feed_rows[0].astype(jnp.bfloat16), 'fsdp', scatter_dimen...  26.2 us
    psum x1, blocking collectives, shards(): lax.psum((attention_cols[4], attention_cols[5], attention_cols[6], attent...  25.9 us
  transfers between devices with their start and end apart: 18, of which 10 were waited for; matrix products, arithmetic and copies ran while one was open for 39% of the time, Pallas kernels for 0%

commit v1 on v0

v1 whole, which is shorter than its diff:
```python
import functools

import jax
import jax.numpy as jnp
from jax import lax
from jax.experimental import pallas as pl
from jax.experimental.pallas import tpu as pltpu
from jax.sharding import PartitionSpec as P

H = 12
HD = 64
PLEN = 512
QLEN = 128
PAIR = 2 * HD
ROWS = 256

epsilon = 1e-06
masked_score = -1e30
f32 = jnp.float32
bf16 = jnp.bfloat16
LIMIT = 60 * 1024 * 1024


def dot(left, right):
    return jnp.dot(left, right, preferred_element_type=f32)


def dot_nt(left, right):
    return lax.dot_general(left, right, (((1,), (1,)), ((), ())), preferred_element_type=f32)


def dot_tn(left, right):
    return lax.dot_general(left, right, (((0,), (0,)), ((), ())), preferred_element_type=f32)


def call(kernel, name, grid, in_specs, out_specs, out_shape, scratch=(), prefetch=0, cost=None):
    return pl.pallas_call(
        kernel,
        name=name,
        grid_spec=pltpu.PrefetchScalarGridSpec(
            num_scalar_prefetch=prefetch,
            grid=grid,
            in_specs=in_specs,
            out_specs=out_specs,
            scratch_shapes=list(scratch),
        ),
        out_shape=out_shape,
        compiler_params=pltpu.CompilerParams(
            vmem_limit_bytes=LIMIT, dimension_semantics=("arbitrary",) * len(grid)
        ),
        cost_estimate=cost,
    )


def whole(shape):
    return pl.BlockSpec(shape, lambda *_: (0,) * len(shape))


def sds(shape, dtype):
    return jax.ShapeDtypeStruct(shape, dtype)


def guess(flops, nbytes):
    return pl.CostEstimate(flops=int(flops), bytes_accessed=int(nbytes), transcendentals=0)


def segment_lanes(bucket, lengths, queries_ext, keys_ext):
    row_count = queries_ext.shape[0]
    slots = lengths.shape[0]
    shape = (row_count, PAIR)
    row = lax.broadcasted_iota(jnp.int32, shape, 0)
    lane = lax.broadcasted_iota(jnp.int32, shape, 1) % HD
    passage = bucket[0] == 1
    segment = jnp.where(passage, row // PLEN, row // QLEN)
    position = jnp.where(passage, row % PLEN, row % QLEN)
    limit = jnp.zeros(shape, jnp.int32)
    for s in range(slots):
        limit = jnp.where(segment == s, lengths[s], limit)
    alive = position < limit
    same = segment == lane
    queries_ext[...] = jnp.where(same, 1.0, 0.0).astype(bf16)
    keys_ext[...] = jnp.where((lane < slots) & ~(same & alive), masked_score, 0.0).astype(bf16)


def attend_kernel(
    bucket, lengths, x, qw, kw, vw, qb, vb,
    q_out, k_out, v_out, context_out, lse_out,
    queries_ext, keys_ext, lse_all,
):
    pair = pl.program_id(0)
    row_count = x.shape[0]

    @pl.when(pair == 0)
    def _():
        segment_lanes(bucket, lengths, queries_ext, keys_ext)
        lse_all[...] = jnp.zeros_like(lse_all)

    weights = jnp.concatenate([qw[0], kw[0], vw[0]], axis=1)
    qb_row = qb[...]
    vb_row = vb[...]
    low_half = lax.broadcasted_iota(jnp.int32, (PLEN, PAIR), 1) < HD
    lane = lax.broadcasted_iota(jnp.int32, (PLEN, PAIR), 1)

    def block(b, carry):
        rows = pl.ds(pl.multiple_of(b * PLEN, PLEN), PLEN)
        qkv = dot(x[rows, :], weights)
        queries = ((qkv[:, :PAIR] + qb_row).astype(bf16).astype(f32) * HD ** (-0.5)).astype(bf16)
        keys = qkv[:, PAIR:2 * PAIR].astype(bf16)
        values = (qkv[:, 2 * PAIR:] + vb_row).astype(bf16)
        q_out[rows, :] = queries
        k_out[rows, :] = keys
        v_out[rows, :] = values
        q_ext = queries_ext[rows, :]
        k_ext = keys_ext[rows, :]
        ones = jnp.ones_like(values)
        sums, tops = [], []
        for half in range(2):
            mine = low_half if half == 0 else ~low_half
            scores = dot_nt(jnp.where(mine, queries, q_ext), jnp.where(mine, keys, k_ext))
            top = jnp.max(scores, axis=-1, keepdims=True)
            weight = jnp.exp(scores - top).astype(bf16)
            sums.append(dot(weight, jnp.where(mine, values, ones)))
            tops.append(top)
        numer = jnp.where(low_half, sums[0], sums[1])
        denom = pltpu.roll(jnp.where(low_half, sums[1], sums[0]), HD, 1)
        context_out[rows, :] = (numer / denom).astype(bf16)
        lse = jnp.where(low_half, tops[0], tops[1]) + jnp.log(denom)
        mine = (lane % HD) == pair
        lse_all[rows, :] = jnp.where(mine, lse, lse_all[rows, :])
        return carry

    lax.fori_loop(0, row_count // PLEN, block, 0)

    @pl.when(pair == pl.num_programs(0) - 1)
    def _():
        lse_out[...] = lse_all[...].T


def attend(bucket, lengths, x, weights, qb, vb):
    t, d = x.shape
    pairs = d // PAIR
    column = lambda m: pl.BlockSpec((1, d, PAIR), lambda p, *_: (m, 0, p))
    vector = pl.BlockSpec((1, PAIR), lambda p, *_: (0, p))
    tall = pl.BlockSpec((t, PAIR), lambda p, *_: (0, p))
    return call(
        attend_kernel, "attend", (pairs,),
        [whole((t, d)), column(0), column(1), column(2), vector, vector],
        [tall, tall, tall, tall, whole((PAIR, t))],
        [sds((t, d), bf16)] * 4 + [sds((PAIR, t), f32)],
        [pltpu.VMEM((t, PAIR), bf16), pltpu.VMEM((t, PAIR), bf16), pltpu.VMEM((t, PAIR), f32)],
        prefetch=2, cost=guess(15e9, 12e6),
    )(bucket, lengths, x, weights, weights, weights, qb, vb)


def attend_back_kernel(
    bucket, lengths, x_t, q, k, v, grad_context, lse, delta, qw, kw, vw, grad_inner,
    gqw, gkw, gvw, gqb, gvb, input_grad,
    queries_ext, keys_ext, grads,
):
    pair = pl.program_id(0)
    row_count = q.shape[0]

    @pl.when(pair == 0)
    def _():
        segment_lanes(bucket, lengths, queries_ext, keys_ext)

    low_half = lax.broadcasted_iota(jnp.int32, (PLEN, PAIR), 1) < HD

    def block(b, carry):
        rows = pl.ds(pl.multiple_of(b * PLEN, PLEN), PLEN)
        queries, keys, values, grad_ctx = q[rows, :], k[rows, :], v[rows, :], grad_context[rows, :]
        q_ext, k_ext = queries_ext[rows, :], keys_ext[rows, :]
        nothing = jnp.zeros_like(values)
        got = []
        for half in range(2):
            mine = low_half if half == 0 else ~low_half
            lse_row = lse[pl.ds(half * HD + pair, 1), rows]
            delta_row = delta[pl.ds(half * HD + pair, 1), rows]
            scores = dot_nt(jnp.where(mine, keys, k_ext), jnp.where(mine, queries, q_ext))
            probs = jnp.exp(scores - lse_row)
            grad_probs = dot_nt(jnp.where(mine, values, nothing), grad_ctx)
            grad_scores = (probs * (grad_probs - delta_row)).astype(bf16)
            grad_v = dot(probs.astype(bf16), grad_ctx)
            grad_k = dot(grad_scores, queries)
            grad_q = dot_tn(grad_scores, keys)
            got.append((grad_q, grad_k, grad_v))
        gq = (jnp.where(low_half, got[0][0], got[1][0]) * HD ** (-0.5)).astype(bf16)
        gk = jnp.where(low_half, got[0][1], got[1][1]).astype(bf16)
        gv = jnp.where(low_half, got[0][2], got[1][2]).astype(bf16)
        grads[rows, :PAIR] = gq
        grads[rows, PAIR:2 * PAIR] = gk
        grads[rows, 2 * PAIR:] = gv
        sum_q = jnp.sum(gq.astype(f32), axis=0, keepdims=True)
        sum_v = jnp.sum(gv.astype(f32), axis=0, keepdims=True)
        return (carry[0] + sum_q, carry[1] + sum_v)

    start = jnp.zeros((1, PAIR), f32)
    gqb[...], gvb[...] = lax.fori_loop(0, row_count // PLEN, block, (start, start))

    columns = grads[...]
    weight_grads = dot(x_t[...], columns)
    gqw[...] = weight_grads[:, :PAIR].astype(gqw.dtype)
    gkw[...] = weight_grads[:, PAIR:2 * PAIR].astype(gkw.dtype)
    gvw[...] = weight_grads[:, 2 * PAIR:].astype(gvw.dtype)

    @pl.when(pair == 0)
    def _():
        input_grad[...] = grad_inner[...]

    weights = jnp.concatenate([qw[0], kw[0], vw[0]], axis=1)
    input_grad[...] += dot_nt(columns, weights)


def attend_back(bucket, lengths, x_t, q, k, v, grad_context, lse, delta, weights, grad_inner):
    t, d = q.shape
    pairs = d // PAIR
    column = lambda m: pl.BlockSpec((1, d, PAIR), lambda p, *_: (m, 0, p))
    vector = pl.BlockSpec((1, PAIR), lambda p, *_: (0, p))
    tall = pl.BlockSpec((t, PAIR), lambda p, *_: (0, p))
    made = pl.BlockSpec((d, PAIR), lambda p, *_: (0, p))
    return call(
        attend_back_kernel, "attend_back", (pairs,),
        [whole((d, t)), tall, tall, tall, tall, whole((PAIR, t)), whole((PAIR, t)),
         column(0), column(1), column(2), whole((t, d))],
        [made, made, made, vector, vector, whole((t, d))],
        [sds((d, d), bf16)] * 3 + [sds((1, d), f32)] * 2 + [sds((t, d), f32)],
        [pltpu.VMEM((t, PAIR), bf16), pltpu.VMEM((t, PAIR), bf16), pltpu.VMEM((t, 3 * PAIR), bf16)],
        prefetch=2, cost=guess(30e9, 25e6),
    )(bucket, lengths, x_t, q, k, v, grad_context, lse, delta, weights, weights, weights, grad_inner)


def normed(v):
    centred = v - jnp.mean(v, axis=-1, keepdims=True)
    r = lax.rsqrt(jnp.mean(centred * centred, axis=-1, keepdims=True) + epsilon)
    return centred * r, r


def norm_back(dy, n, r, gain):
    dn = dy * gain
    return r * (dn - jnp.mean(dn, axis=-1, keepdims=True) - n * jnp.mean(dn * n, axis=-1, keepdims=True))


def gelu_parts(u):
    size = jnp.abs(u)
    below = 1.0 + (0.3275911 * 0.7071067811865476) * size
    t = pl.reciprocal(below, approx=True)
    t = t * (2.0 - below * t)
    poly = 0.5 * 1.061405429
    for c in (-1.453152027, 1.421413741, -0.284496736, 0.254829592):
        poly = poly * t + 0.5 * c
    bell = jnp.exp(u * u * -0.5)
    tail = poly * t * bell
    phi = jnp.where(u >= 0, 1.0 - tail, tail)
    return u * phi, phi + u * bell * 0.3989422804014327


def up_kernel(x, context, ow, ob, g1, b1, uw, ub, n1_out, r1_out, low_out, act_out, slope_out):
    parts, _, wide = act_out.shape
    attended = dot(context[...], ow[0]) + ob[...]
    n1, r1 = normed(x[...].astype(f32) + attended)
    n1_out[...] = n1
    r1_out[...] = jnp.broadcast_to(r1, r1_out.shape)
    low = (n1 * g1[...] + b1[...]).astype(bf16)
    low_out[...] = low
    each = uw.shape[2] // wide
    for j in range(uw.shape[0]):
        hidden = dot(low, uw[j]) + ub[j:j + 1, :]
        active, slope = gelu_parts(hidden)
        active, slope = active.astype(bf16), slope.astype(bf16)
        for c in range(each):
            act_out[j * each + c] = active[:, c * wide:(c + 1) * wide]
            slope_out[j * each + c] = slope[:, c * wide:(c + 1) * wide]


def up(x, context, weights, ob, g1, b1, uw, ub, parts):
    t, d = x.shape
    f, _, wide = uw.shape
    narrow = f * wide // parts
    rows = pl.BlockSpec((ROWS, d), lambda r: (r, 0))
    tall = pl.BlockSpec((parts, ROWS, narrow), lambda r: (0, r, 0))
    return call(
        up_kernel, "up", (t // ROWS,),
        [rows, rows, pl.BlockSpec((1, d, d), lambda r: (3, 0, 0)), whole((1, d)), whole((1, d)), whole((1, d)),
         whole(uw.shape), whole(ub.shape)],
        [rows, pl.BlockSpec((ROWS, 128), lambda r: (r, 0)), rows, tall, tall],
        [sds((t, d), f32), sds((t, 128), f32), sds((t, d), bf16), sds((parts, t, narrow), bf16),
         sds((parts, t, narrow), bf16)],
        cost=guess(12e9, 26e6),
    )(x, context, weights, ob, g1, b1, uw, ub)


def down_kernel(
    bucket, lengths, act_rows, n1, g1, b1, dw, db, g2, b2, cotangent, act_part,
    out, pooled, mixed_out, branch_out, gdb, gg2, gb2, gdw,
    branch_t, counts,
):
    step = pl.program_id(0)
    tiles = branch_t.shape[1] // ROWS
    parts = dw.shape[0]

    @pl.when(step == 0)
    def _():
        pooled[...] = jnp.zeros_like(pooled)
        counts[...] = jnp.zeros_like(counts)
        gdb[...] = jnp.zeros_like(gdb)
        gg2[...] = jnp.zeros_like(gg2)
        gb2[...] = jnp.zeros_like(gb2)

    @pl.when(step < tiles)
    def _():
        branch = dot_nt(act_rows[0], dw[0])
        for i in range(1, parts):
            branch += dot_nt(act_rows[i], dw[i])
        residual = n1[...] * g1[...] + b1[...] + (branch + db[...])
        n2, r2 = normed(residual)
        result = n2 * g2[...] + b2[...]
        out[...] = result.astype(bf16)
        slots = pooled.shape[0]
        shape = (slots, ROWS)
        slot = lax.broadcasted_iota(jnp.int32, shape, 0)
        row = lax.broadcasted_iota(jnp.int32, shape, 1) + step * ROWS
        passage = bucket[0] == 1
        segment = jnp.where(passage, row // PLEN, row // QLEN)
        position = jnp.where(passage, row % PLEN, row % QLEN)
        limit = jnp.zeros(shape, jnp.int32)
        for s in range(slots):
            limit = jnp.where(slot == s, lengths[s], limit)
        chosen = jnp.where((segment == slot) & (position < limit), 1.0, 0.0)
        picked = chosen.astype(bf16)
        high = result.astype(bf16)
        rest = result - high.astype(f32)
        middle = rest.astype(bf16)
        last = (rest - middle.astype(f32)).astype(bf16)
        pooled[...] += dot(picked, high) + dot(picked, middle) + dot(picked, last)
        counts[...] += jnp.broadcast_to(jnp.sum(chosen, axis=1, keepdims=True), counts.shape)
        dy = cotangent[...].astype(f32)
        gg2[...] += jnp.sum(dy * n2, axis=0, keepdims=True)
        gb2[...] += jnp.sum(dy, axis=0, keepdims=True)
        mixed = norm_back(dy, n2, r2, g2[...])
        mixed_out[...] = mixed
        low = mixed.astype(bf16)
        branch_out[...] = low
        gdb[...] += jnp.sum(low.astype(f32), axis=0, keepdims=True)
        for tile in range(tiles):
            @pl.when(step == tile)
            def _():
                branch_t[:, tile * ROWS:(tile + 1) * ROWS] = low.T

    @pl.when(step == tiles - 1)
    def _():
        pooled[...] = pooled[...] / jnp.maximum(counts[...], 1.0)[:, :1]

    @pl.when(step >= tiles)
    def _():
        gdw[0] = dot(branch_t[...], act_part[0]).astype(bf16)


def down(bucket, lengths, active, n1, g1, b1, dw, db, g2, b2, cotangent):
    parts, t, narrow = active.shape
    d = n1.shape[1]
    tiles = t // ROWS
    slots = lengths.shape[0]
    early = lambda s: jnp.minimum(s, tiles - 1)
    late = lambda s: jnp.maximum(s - tiles, 0)
    rows = pl.BlockSpec((ROWS, d), lambda s, *_: (early(s), 0))
    vector = whole((1, d))
    return call(
        down_kernel, "down", (tiles + parts,),
        [pl.BlockSpec((parts, ROWS, narrow), lambda s, *_: (0, early(s), 0)), rows, vector, vector,
         whole(dw.shape), vector, vector, vector, rows,
         pl.BlockSpec((1, t, narrow), lambda s, *_: (late(s), 0, 0))],
        [rows, whole((slots, d)), rows, rows, vector, vector, vector,
         pl.BlockSpec((1, d, narrow), lambda s, *_: (late(s), 0, 0))],
        [sds((t, d), bf16), sds((slots, d), f32), sds((t, d), f32), sds((t, d), bf16)]
        + [sds((1, d), f32)] * 3 + [sds((parts, d, narrow), bf16)],
        [pltpu.VMEM((d, t), bf16), pltpu.VMEM((slots, 128), f32)],
        prefetch=2, cost=guess(12e9, 30e6),
    )(bucket, lengths, active, n1, g1, b1, dw, db, g2, b2, cotangent, active)


def feed_back_kernel(
    branch, slope, dw, uw, low_t, mixed, n1, r1, g1, context, ow,
    guw, gub, inner_out, gg1, gb1, gob, gow, grad_context, delta_out,
    hidden, grad_normed, attended,
):
    j = pl.program_id(0)
    each, t, narrow = slope.shape
    d = branch.shape[1]
    tiles = t // ROWS

    def gelu_rows(r, sums):
        rows = pl.ds(pl.multiple_of(r * ROWS, ROWS), ROWS)
        found = []
        for c in range(each):
            grad = (slope[c, rows, :].astype(f32) * dot(branch[rows, :], dw[c])).astype(bf16)
            hidden[rows, c * narrow:(c + 1) * narrow] = grad
            found.append(sums[c] + jnp.sum(grad.astype(f32), axis=0, keepdims=True))
        return tuple(found)

    sums = lax.fori_loop(0, tiles, gelu_rows, (jnp.zeros((1, narrow), f32),) * each)
    for c in range(each):
        gub[0, :, c * narrow:(c + 1) * narrow] = sums[c]
    guw[0] = dot(low_t[...], hidden[...]).astype(bf16)

    @pl.when(j == 0)
    def _():
        grad_normed[...] = mixed[...]

    def normed_rows(r, carry):
        rows = pl.ds(pl.multiple_of(r * ROWS, ROWS), ROWS)
        grad_normed[rows, :] += dot_nt(hidden[rows, :], uw[0])
        return carry

    lax.fori_loop(0, tiles, normed_rows, 0)

    @pl.when(j == pl.num_programs(0) - 1)
    def _():
        feature = lax.broadcasted_iota(jnp.int32, (128, d), 1)
        slot = lax.broadcasted_iota(jnp.int32, (128, d), 0)
        head = jnp.where(slot < HD, 2 * slot, 2 * (slot - HD) + 1)
        pick = jnp.where(feature // HD == head, 1.0, 0.0).astype(bf16)

        def inner_rows(r, sums):
            rows = pl.ds(pl.multiple_of(r * ROWS, ROWS), ROWS)
            dy, n = grad_normed[rows, :], n1[rows, :]
            inner = norm_back(dy, n, r1[rows, :1], g1[...])
            inner_out[rows, :] = inner
            low = inner.astype(bf16)
            attended[rows, :] = low
            grad_ctx = dot_nt(low, ow[0]).astype(bf16)
            grad_context[rows, :] = grad_ctx
            both = grad_ctx.astype(f32) * context[rows, :].astype(f32)
            high = both.astype(bf16)
            rest = (both - high.astype(f32)).astype(bf16)
            delta_out[:, rows] = dot_nt(pick, high) + dot_nt(pick, rest)
            return (
                sums[0] + jnp.sum(dy * n, axis=0, keepdims=True),
                sums[1] + jnp.sum(dy, axis=0, keepdims=True),
                sums[2] + jnp.sum(low.astype(f32), axis=0, keepdims=True),
            )

        gg1[...], gb1[...], gob[...] = lax.fori_loop(0, tiles, inner_rows, (jnp.zeros((1, d), f32),) * 3)
        gow[...] = dot_tn(context[...], attended[...]).astype(bf16)


def feed_back(branch, slope, dw, uw, low_t, mixed, n1, r1, g1, context, weights):
    parts, t, narrow = slope.shape
    f, d, wide = uw.shape
    each = parts // f
    vector = whole((1, d))
    return call(
        feed_back_kernel, "feed_back", (f,),
        [whole((t, d)), pl.BlockSpec((each, t, narrow), lambda j: (j, 0, 0)),
         pl.BlockSpec((each, d, narrow), lambda j: (j, 0, 0)), pl.BlockSpec((1, d, wide), lambda j: (j, 0, 0)),
         whole((d, t)), whole((t, d)), whole((t, d)), whole((t, 128)), vector, whole((t, d)),
         pl.BlockSpec((1, d, d), lambda j: (3, 0, 0))],
        [pl.BlockSpec((1, d, wide), lambda j: (j, 0, 0)), pl.BlockSpec((1, 1, wide), lambda j: (j, 0, 0)),
         whole((t, d)), vector, vector, vector, whole((d, d)), whole((t, d)), whole((128, t))],
        [sds((f, d, wide), bf16), sds((f, 1, wide), f32), sds((t, d), f32)] + [sds((1, d), f32)] * 3
        + [sds((d, d), bf16), sds((t, d), bf16), sds((128, t), f32)],
        [pltpu.VMEM((t, wide), bf16), pltpu.VMEM((t, d), f32), pltpu.VMEM((t, d), bf16)],
        cost=guess(18e9, 45e6),
    )(branch, slope, dw, uw, low_t, mixed, n1, r1, g1, context, weights)


def shards(
    tokens, bucket, lengths, cotangent,
    query_weight, query_bias, key_weight, value_weight, value_bias, out_weight, out_bias,
    norm1_gain, norm1_bias, up_weight, up_bias, down_weight, down_bias, norm2_gain, norm2_bias,
):
    t, d = tokens.shape
    dp, fsdp = lax.axis_size("dp"), lax.axis_size("fsdp")
    lengths = lengths[0]

    def gather(v, axis, dim, tiled=True):
        return lax.all_gather(v, axis, axis=dim, tiled=tiled)

    stack = jnp.stack([query_weight, key_weight, value_weight, out_weight])
    weights = gather(gather(stack, "fsdp", 2), "dp", 1)
    uw = gather(gather(up_weight, "dp", 0), "fsdp", 0, False)
    dw = gather(gather(down_weight.T, "fsdp", 0), "dp", 0, False)
    vectors = jnp.stack([query_bias, value_bias, out_bias, norm1_gain, norm1_bias, down_bias, norm2_gain, norm2_bias])
    vectors = gather(vectors, "fsdp", 1).astype(f32)
    qb, vb, ob, g1, b1, db, g2, b2 = (vectors[n:n + 1] for n in range(8))
    ub = gather(up_bias, "fsdp", 0, False).astype(f32)

    q, k, v, context, lse = attend(bucket, lengths, tokens, weights, qb, vb)
    n1, r1, low, active, slope = up(tokens, context, weights, ob, g1, b1, uw, ub, dp)
    out, pooled, mixed, branch, gdb, gg2, gb2, gdw = down(
        bucket, lengths, active, n1, g1, b1, dw, db, g2, b2, cotangent
    )
    guw, gub, inner, gg1, gb1, gob, gow, grad_context, delta = feed_back(
        branch, slope, dw, uw, low.T, mixed, n1, r1, g1, context, weights
    )
    gqw, gkw, gvw, gqb, gvb, input_grad = attend_back(
        bucket, lengths, tokens.T, q, k, v, grad_context, lse, delta, weights, inner
    )

    def scatter(g, axis, dim, tiled=True):
        return lax.psum_scatter(g, axis, scatter_dimension=dim, tiled=tiled)

    made_u = scatter(scatter(guw, "fsdp", 0, False), "dp", 0).astype(f32)
    made_d = scatter(scatter(gdw, "dp", 0, False), "fsdp", 0).T.astype(f32)
    made = [scatter(scatter(g, "dp", 0), "fsdp", 1).astype(f32) for g in (gqw, gkw, gvw, gow)]
    rows = jnp.concatenate([gqb, gvb, gob, gg1, gb1, gdb, gg2, gb2], axis=0)
    rows = lax.psum(scatter(rows, "fsdp", 1), "dp")
    gub = lax.psum(scatter(gub.reshape(-1), "fsdp", 0), "dp")
    return (
        out, pooled, input_grad, made[0], rows[0], made[1], made[2], rows[1], made[3], rows[2], rows[3], rows[4],
        made_u, gub, made_d, rows[5], rows[6], rows[7],
    )


def solution(mesh):
    tall, square, vector = P(("dp", "fsdp"), None), P("dp", "fsdp"), P("fsdp")
    in_specs = (
        tall, P(("dp", "fsdp")), tall, tall, square, vector, square, square, vector, square, vector,
        vector, vector, square, vector, square, vector, vector, vector,
    )
    out_specs = (
        tall, tall, tall, square, vector, square, square, vector, square, vector, vector, vector,
        square, vector, square, vector, vector, vector,
    )
    return jax.shard_map(shards, mesh=mesh, in_specs=in_specs, out_specs=out_specs, check_vma=False)
```

time: 783 us -> 757 us (0.967); the launches traced: 774 us -> 756 us
  matrix products: 225 us -> 0 us
  waiting for transfers between devices: 262 us -> 476 us
  Pallas kernels: 0 us -> 153 us
  local copies, waits for them, and re-layouts: 95.2 us -> 20.3 us
  blocking collectives: 123 us -> 83.1 us
  other arithmetic: 40.4 us -> 7.4 us
  loops' own time: 9.95 us -> 0 us
    dot_general x24 -> x0, matrix products: 196 us -> none  [the longest x1 38.3 us: forward(): jnp.dot(normed_low, up_weight, preferred_element_type=jnp.float32)]
    pallas_call x0 -> x5, Pallas kernels: none -> 153 us  [the longest x1 39.8 us: feed_back(): call(feed_back_kernel, 'feed_back', (f,), [whole((t, d)), pl.BlockSpec((e...]
    all_gather x6 -> x4, waiting for transfers between devices: 10.1 us -> 95.4 us  [gather(): return lax.all_gather(v, axis, axis=dim, tiled=tiled)]
    reduce_scatter x7, waiting for transfers between devices: 165 us -> 234 us  [scatter(): return lax.psum_scatter(g, axis, scatter_dimension=dim, tiled=tiled)]
    unnamed x23, waiting for transfers between devices: 86.9 us -> 146 us
    unnamed x170 -> x56, local copies, waits for them, and re-layouts: 44.4 us -> 14.9 us
    sub x2 -> x0, matrix products: 29.1 us -> none  [softmax_probs(): exponent = jnp.exp(scores - highest)]
    all_gather x7 -> x4, blocking collectives: 65.6 us -> 39.9 us  [gather(): return lax.all_gather(v, axis, axis=dim, tiled=tiled)]
  transfers between devices with their start and end apart: 18 -> 17, of which waited for: 10 -> 16; matrix products, arithmetic and copies ran while one was open for 39% -> 3% of each run, Pallas kernels for 0% -> 6%
where the time goes in v1:
time: 757 us; the launch traced here: 756 us
  waiting for transfers between devices  476 us (63%)
  Pallas kernels  153 us (20%)
  blocking collectives  83.1 us (11%)
  local copies, waits for them, and re-layouts  20.3 us (3%)
  between operations  15.7 us (2%)
    reduce_scatter x7, waiting for transfers between devices, scatter(): return lax.psum_scatter(g, axis, scatter_dimension=dim, tiled=tiled)  234 us
    unnamed x23, waiting for transfers between devices  146 us
    all_gather x4, waiting for transfers between devices, gather(): return lax.all_gather(v, axis, axis=dim, tiled=tiled)  95.4 us
    all_gather x4, blocking collectives, gather(): return lax.all_gather(v, axis, axis=dim, tiled=tiled)  39.9 us
    pallas_call x1, Pallas kernels, feed_back(): call(feed_back_kernel, 'feed_back', (f,), [whole((t, d)), pl.BlockSpec((e...  39.8 us
    pallas_call x1, Pallas kernels, attend_back(): call(attend_back_kernel, 'attend_back', (pairs,), [whole((d, t)), tall, t...  37.7 us
    psum x1, blocking collectives, shards(): rows = lax.psum(scatter(rows, 'fsdp', 1), 'dp')  28.2 us
    pallas_call x1, Pallas kernels, down(): call(down_kernel, 'down', (tiles + parts,), [pl.BlockSpec((parts, ROWS, n...  28 us
  transfers between devices with their start and end apart: 17, of which 16 were waited for; matrix products, arithmetic and copies ran while one was open for 3% of the time, Pallas kernels for 6%

profile of v1, /device:TPU:0, one launch (start us, length us, event | category | flops | bytes accessed | tf_op | source)
XLA Modules:
  0.0 756.4 jit_solution(17304406500512742404)
XLA Ops:
  7.2 0.7 all-gather.12.cloned.1.call-update
  8.0 0.9 pad_maximum_fusion
  9.1 12.7 %all_gather.33 = bf16[4,96,768]{1,0,2:T(4,128)(2,1)S(1)} all-gather(bf16[4,96,192]{1,0,2:T(4,128)(2,1)S(1)} %copy.51), channel_id=1, replica_groups=mesh['dp'=8,'fsdp'=4] {'fsdp'}, dimensions={2}, use_global_device_ids=true | all-gather | bytes 737280 | tf_op jit(solution)/shard_map/all_gather | solution.py:476
  21.7 1.2 copy.52
  23.1 12.0 %all-gather.12.cloned.1.call-done = bf16[768,768]{1,0:T(8,128)(2,1)} async-done(((bf16[96,768]{1,0:T(8,128)(2,1)}), bf16[768,768]{1,0:T(8,128)(2,1)}) %all-gather.12.cloned.1.call-update) | async-done | bytes 1179664 | tf_op jit(solution)/shard_map/all_gather | solution.py:476
  35.1 11.9 %all_gather.41 = bf16[768,384]{1,0:T(8,128)(2,1)} all-gather(bf16[192,384]{1,0:T(8,128)(2,1)S(1)} %bitcast.52), channel_id=1, replica_groups=mesh['dp'=8,'fsdp'=4] {'fsdp'}, dimensions={0}, use_global_device_ids=true | all-gather | bytes 737280 | tf_op jit(solution)/shard_map/all_gather | solution.py:476
  47.3 7.4 all-gather.3
  55.6 1.6 copy.55
  57.2 7.8 %all-gather.4 = bf16[4,1,768]{2,1,0:T(2,128)(2,1)S(1)} all-gather(bf16[1,1,768]{2,1,0:T(2,128)(2,1)S(1)} %reshape.46), channel_id=3, replica_groups=mesh['dp'=8,'fsdp'=4] {'fsdp'}, dimensions={0}, use_global_device_ids=true | all-gather | bytes 7680 | tf_op jit(solution)/shard_map/all_gather | solution.py:476
  66.3 22.4 %all-gather.10.cloned.1.call-done.qw.kw.vw.ow = bf16[4,768,768]{2,1,0:T(8,128)(2,1)} async-done(((bf16[4,96,768]{2,1,0:T(8,128)(2,1)}), bf16[4,768,768]{2,1,0:T(8,128)(2,1)}) %all-gather.10.cloned.1.call-update) | async-done | bytes 4718608 | tf_op jit(solution)/shard_map/all_gather | solution.py:476
  88.7 24.1 %attend.1 = (bf16[1024,768]{1,0:T(8,128)(2,1)}, bf16[1024,768]{1,0:T(8,128)(2,1)}, bf16[1024,768]{1,0:T(8,128)(2,1)}, bf16[1024,768]{1,0:T(8,128)(2,1)}, f32[128,1024]{1,0:T(8,128)}) custom-call(s32[1]{0:T(128)S(6)} %copy.68.bucket, s32[8]{0:T(128)} %bitcast.77, bf16[1024,768]{1,0:T(8,128)(2,1)} %x.3, ...), custom_call_target="tpu_custom_call" | custom-call | flops 15000000512 | bytes 12000000 | tf_op jit(solution)/shard_map/attend/pallas_call | solution.py:145
  112.8 33.7 %all-gather.14.cloned.1.call-done = bf16[3072,768]{1,0:T(8,128)(2,1)} async-done(((bf16[768,768]{1,0:T(8,128)(2,1)}), bf16[3072,768]{1,0:T(8,128)(2,1)}) %all-gather.14.cloned.1.call-update) | async-done | bytes 4718608 | tf_op jit(solution)/shard_map/all_gather | solution.py:476
  146.5 23.4 %up.1 = (f32[1024,768]{1,0:T(8,128)}, f32[1024,128]{1,0:T(8,128)}, bf16[1024,768]{1,0:T(8,128)(2,1)}, bf16[8,1024,384]{2,1,0:T(8,128)(2,1)}, bf16[8,1024,384]{2,1,0:T(8,128)(2,1)}) custom-call(bf16[1024,768]{1,0:T(8,128)(2,1)} %x.3, bf16[1024,768]{1,0:T(8,128)(2,1)} %get-tuple-element.51.context, ...), custom_call_target="tpu_custom_call" | custom-call | flops 12000000000 | bytes 26000000 | tf_op jit(solution)/shard_map/up/pallas_call | solution.py:281
  169.9 2.6 copy.56
  172.5 27.2 %all-gather.16.cloned.1.call-done = bf16[6144,384]{1,0:T(8,128)(2,1)} async-done(((bf16[768,384]{1,0:T(8,128)(2,1)}), bf16[6144,384]{1,0:T(8,128)(2,1)}) %all-gather.16.cloned.1.call-update) | async-done | bytes 4718608 | tf_op jit(solution)/shard_map/all_gather | solution.py:476
  199.7 28.0 %down.1 = (bf16[1024,768]{1,0:T(8,128)(2,1)}, f32[8,768]{1,0:T(8,128)}, f32[1024,768]{1,0:T(8,128)}, bf16[1024,768]{1,0:T(8,128)(2,1)}, f32[1,768]{1,0:T(1,128)}...) custom-call(s32[1]{0:T(128)S(6)} %copy.68.bucket, s32[8]{0:T(128)} %bitcast.78, ...), custom_call_target="tpu_custom_call" | custom-call | flops 12000000000 | bytes 30000000 | tf_op jit(solution)/shard_map/down/pallas_call | solution.py:367
  227.7 39.8 %feed_back.1 = (bf16[4,768,768]{2,1,0:T(8,128)(2,1)}, f32[4,1,768]{2,1,0:T(1,128)}, f32[1024,768]{1,0:T(8,128)}, f32[1,768]{1,0:T(1,128)}, f32[1,768]{1,0:T(1,12...) custom-call(bf16[1024,768]{1,0:T(8,128)(2,1)} %get-tuple-element.59.branch, ...), custom_call_target="tpu_custom_call" | custom-call | flops 17999998976 | bytes 45000000 | tf_op jit(solution)/shard_map/feed_back/pallas_call | solution.py:451
  267.5 37.7 %attend_back.1 = (bf16[768,768]{1,0:T(8,128)(2,1)}, bf16[768,768]{1,0:T(8,128)(2,1)}, bf16[768,768]{1,0:T(8,128)(2,1)}, f32[1,768]{1,0:T(1,128)}, f32[1,768]{1,0:T(1,128)}, /*index=5*/f32[1024,768]{1,0:T(8,128)}) custom-call(s32[1]{0:T(128)S(6)} %copy.68.bucket, s32[8]{0:T(128)} %bitcast.79, bf16[768,1024]{1,0:T(8,128)(2,1)} %bitcast.43, ...), custom_call_target="tpu_custom_call" | custom-call | flops 30000001024 | bytes 25000000 | tf_op jit(solution)/shard_map/attend_back/pallas_call | solution.py:221
  305.9 0.7 reduce-scatter.30.cloned.1.call-update
  306.7 0.7 reduce-scatter.32.cloned.1.call-update
  307.4 0.7 reduce-scatter.36.cloned.1.call-update
  309.0 0.9 copy.59
  310.0 27.2 %reduce-scatter.26.cloned.1.call-done = bf16[96,768]{1,0:T(8,128)(2,1)} async-done(((bf16[768,768]{1,0:T(8,128)(2,1)}), bf16[96,768]{1,0:T(8,128)(2,1)}) %reduce-scatter.26.cloned.1.call-update) | async-done | bytes 147472 | tf_op jit(solution)/shard_map/reduce_scatter | solution.py:500
  337.2 1.7 copy.57
  339.0 31.1 %reduce-scatter.28.cloned.1.call-done = bf16[96,768]{1,0:T(8,128)(2,1)} async-done(((bf16[768,768]{1,0:T(8,128)(2,1)}), bf16[96,768]{1,0:T(8,128)(2,1)}) %reduce-scatter.28.cloned.1.call-update) | async-done | bytes 147472 | tf_op jit(solution)/shard_map/reduce_scatter | solution.py:500
  370.1 1.7 copy.61
  371.9 31.5 %reduce-scatter.30.cloned.1.call-done = bf16[96,768]{1,0:T(8,128)(2,1)} async-done(((bf16[768,768]{1,0:T(8,128)(2,1)}), bf16[96,768]{1,0:T(8,128)(2,1)}) %reduce-scatter.30.cloned.1.call-update) | async-done | bytes 147472 | tf_op jit(solution)/shard_map/reduce_scatter | solution.py:500
  403.4 1.7 copy.63
  405.2 31.4 %reduce-scatter.32.cloned.1.call-done = bf16[96,768]{1,0:T(8,128)(2,1)} async-done(((bf16[768,768]{1,0:T(8,128)(2,1)}), bf16[96,768]{1,0:T(8,128)(2,1)}) %reduce-scatter.32.cloned.1.call-update) | async-done | bytes 147472 | tf_op jit(solution)/shard_map/reduce_scatter | solution.py:500
  436.5 1.7 copy.65
  438.3 53.8 %reduce-scatter.36.cloned.1.call-done = bf16[1,768,384]{2,1,0:T(8,128)(2,1)} async-done(((bf16[8,768,384]{2,1,0:T(8,128)(2,1)}), bf16[1,768,384]{2,1,0:T(8,128)(2,1)}) %reduce-scatter.36.cloned.1.call-update) | async-done | bytes 589840 | tf_op jit(solution)/shard_map/reduce_scatter | solution.py:500
  492.2 58.2 %reduce-scatter.50.cloned.1.call-done = bf16[1,768,768]{2,1,0:T(8,128)(2,1)} async-done(((bf16[4,768,768]{2,1,0:T(8,128)(2,1)}), bf16[1,768,768]{2,1,0:T(8,128)(2,1)}) %reduce-scatter.50.cloned.1.call-update) | async-done | bytes 1179664
  551.7 15.0 %all-reduce.1 = f32[3072]{0:T(1024)S(1)} all-reduce(f32[3072]{0:T(1024)S(1)} %bitcast.64), channel_id=16, replica_groups=mesh['dp'=8,'fsdp'=4] {'fsdp'}, use_global_device_ids=true, to_apply=%region_12.0.clone | all-reduce | flops 3072 | bytes 24576
  566.8 10.9 %reduce-scatter.42.cloned.1.call-done = f32[192,8]{1,0:T(8,128)} async-done(((f32[768,8]{1,0:T(8,128)}), f32[192,8]{1,0:T(8,128)}) %reduce-scatter.42.cloned.1.call-update) | async-done | bytes 6160
  577.7 0.9 copy.60
  578.7 28.2 %all-reduce.2 = (f32[8,192]{1,0:T(8,128)S(1)}, f32[768]{0:T(1024)}) all-reduce(f32[8,192]{1,0:T(8,128)S(1)} %copy.60, f32[768]{0:T(1024)S(1)} %dynamic-slice.3), channel_id=1, replica_groups=mesh['dp'=8,'fsdp'=4] {'dp'}, use_global_device_ids=true, to_apply=%region_3.0 | all-reduce | flops 2304 | bytes 18432 | tf_op jit(solution)/shard_map/psum | solution.py:506
  607.5 0.9 copy.58
  609.0 23.2 %reduce-scatter.44.cloned.1.call-done = bf16[192,96]{1,0:T(8,128)(2,1)} async-done(((bf16[768,96]{1,0:T(8,128)(2,1)}), bf16[192,96]{1,0:T(8,128)(2,1)}) %reduce-scatter.44.cloned.1.call-update) | async-done | bytes 36880
  632.3 0.9 copy.62
  633.8 25.1 %reduce-scatter.46.cloned.1.call-done = bf16[192,96]{1,0:T(8,128)(2,1)} async-done(((bf16[768,96]{1,0:T(8,128)(2,1)}), bf16[192,96]{1,0:T(8,128)(2,1)}) %reduce-scatter.46.cloned.1.call-update) | async-done | bytes 36880
  658.9 0.9 copy.64
  659.8 0.6 convert_element_type.31
  660.4 25.1 %reduce-scatter.48.cloned.1.call-done = bf16[192,96]{1,0:T(8,128)(2,1)} async-done(((bf16[768,96]{1,0:T(8,128)(2,1)}), bf16[192,96]{1,0:T(8,128)(2,1)}) %reduce-scatter.48.cloned.1.call-update) | async-done | bytes 36880
  685.5 0.9 copy.66
  687.0 26.3 %reduce-scatter.38.cloned.1.call-done = bf16[192,384]{1,0:T(8,128)(2,1)} async-done(((bf16[768,384]{1,0:T(8,128)(2,1)}), bf16[192,384]{1,0:T(8,128)(2,1)}) %reduce-scatter.38.cloned.1.call-update) | async-done | bytes 147472 | tf_op jit(solution)/shard_map/reduce_scatter | solution.py:500
  713.3 1.6 convert_bitcast_fusion
  715.0 33.2 %reduce-scatter.34.cloned.1.call-done = bf16[96,768]{1,0:T(8,128)(2,1)} async-done(((bf16[768,768]{1,0:T(8,128)(2,1)}), bf16[96,768]{1,0:T(8,128)(2,1)}) %reduce-scatter.34.cloned.1.call-update) | async-done | bytes 147472 | tf_op jit(solution)/shard_map/reduce_scatter | solution.py:500
  748.2 1.6 convert_element_type.33
  (95 shorter events, 6.9 us)
Async XLA Ops:
  7.2 27.9 %all-gather.12.cloned.1.call-start = ((), (), s32[]{:S(2)}) async-start(), calls=%async_computation.14 | async-start | bytes 1327104 | tf_op jit(solution)/shard_map/all_gather | solution.py:476
  7.9 80.8 %all-gather.10.cloned.1.call-start = ((), (), s32[]{:S(2)}) async-start(), calls=%async_computation.13 | async-start | bytes 5308416 | tf_op jit(solution)/shard_map/all_gather | solution.py:476
  21.7 13.4 %copy-start.1 = (bf16[384,192]{0,1:T(8,128)(2,1)S(1)}, bf16[384,192]{0,1:T(8,128)(2,1)}, u32[]{:S(2)}) copy-start(bf16[384,192]{0,1:T(8,128)(2,1)} %param.34) | copy-start | bytes 442372
  22.9 24.2 %copy-start.12 = (bf16[192]{0:T(256)(128)(2,1)S(1)}, bf16[192]{0:T(256)(128)(2,1)}, u32[]{:S(2)}) copy-start(bf16[192]{0:T(256)(128)(2,1)} %param.24) | copy-start | bytes 1156
  22.9 24.2 %copy-start.13 = (bf16[192]{0:T(256)(128)(2,1)S(1)}, bf16[192]{0:T(256)(128)(2,1)}, u32[]{:S(2)}) copy-start(bf16[192]{0:T(256)(128)(2,1)} %param.27) | copy-start | bytes 1156
  22.9 24.2 %copy-start.14 = (bf16[192]{0:T(256)(128)(2,1)S(1)}, bf16[192]{0:T(256)(128)(2,1)}, u32[]{:S(2)}) copy-start(bf16[192]{0:T(256)(128)(2,1)} %param.29) | copy-start | bytes 1156
  22.9 24.3 %copy-start.15 = (bf16[192]{0:T(256)(128)(2,1)S(1)}, bf16[192]{0:T(256)(128)(2,1)}, u32[]{:S(2)}) copy-start(bf16[192]{0:T(256)(128)(2,1)} %param.30) | copy-start | bytes 1156
  22.9 24.3 %copy-start.16 = (bf16[192]{0:T(256)(128)(2,1)S(1)}, bf16[192]{0:T(256)(128)(2,1)}, u32[]{:S(2)}) copy-start(bf16[192]{0:T(256)(128)(2,1)} %param.31) | copy-start | bytes 1156
  23.0 24.3 %copy-start.17 = (bf16[192]{0:T(256)(128)(2,1)S(1)}, bf16[192]{0:T(256)(128)(2,1)}, u32[]{:S(2)}) copy-start(bf16[192]{0:T(256)(128)(2,1)} %param.35) | copy-start | bytes 1156
  23.0 24.3 %copy-start.18 = (bf16[192]{0:T(256)(128)(2,1)S(1)}, bf16[192]{0:T(256)(128)(2,1)}, u32[]{:S(2)}) copy-start(bf16[192]{0:T(256)(128)(2,1)} %param.36) | copy-start | bytes 1156
  23.0 24.3 %copy-start.19 = (bf16[192]{0:T(256)(128)(2,1)S(1)}, bf16[192]{0:T(256)(128)(2,1)}, u32[]{:S(2)}) copy-start(bf16[192]{0:T(256)(128)(2,1)} %param.37) | copy-start | bytes 1156
  23.0 32.5 %copy-start.11 = (bf16[768]{0:T(1024)(128)(2,1)S(1)}, bf16[768]{0:T(1024)(128)(2,1)}, u32[]{:S(2)}) copy-start(bf16[768]{0:T(1024)(128)(2,1)} %param.33) | copy-start | bytes 4612
  23.0 32.6 %copy-start = (bf16[1024,768]{1,0:T(8,128)(2,1)S(1)}, bf16[1024,768]{1,0:T(8,128)(2,1)}, u32[]{:S(2)}) copy-start(bf16[1024,768]{1,0:T(8,128)(2,1)} %x.3) | copy-start | bytes 4718596
  23.0 123.5 %all-gather.14.cloned.1.call-start = ((), (), s32[]{:S(2)}) async-start(), calls=%async_computation.22 | async-start | bytes 5898240 | tf_op jit(solution)/shard_map/all_gather | solution.py:476
  35.1 164.7 %all-gather.16.cloned.1.call-start = ((), (), s32[]{:S(2)}) async-start(), calls=%async_computation.23 | async-start | bytes 5308416 | tf_op jit(solution)/shard_map/all_gather | solution.py:476
  47.1 290.1 %reduce-scatter.26.cloned.1.call-start = ((), (), s32[]{:S(2)}) async-start(), calls=%async_computation.15 | async-start | bytes 1327104 | tf_op jit(solution)/shard_map/reduce_scatter | solution.py:500
  305.3 64.7 %reduce-scatter.28.cloned.1.call-start = ((), (), s32[]{:S(2)}) async-start(), calls=%async_computation.16 | async-start | bytes 1327104 | tf_op jit(solution)/shard_map/reduce_scatter | solution.py:500
  305.9 97.5 %reduce-scatter.30.cloned.1.call-start = ((), (), s32[]{:S(2)}) async-start(), calls=%async_computation.17 | async-start | bytes 1327104 | tf_op jit(solution)/shard_map/reduce_scatter | solution.py:500
  306.6 129.9 %reduce-scatter.32.cloned.1.call-start = ((), (), s32[]{:S(2)}) async-start(), calls=%async_computation.18 | async-start | bytes 1327104 | tf_op jit(solution)/shard_map/reduce_scatter | solution.py:500
  307.4 184.7 %reduce-scatter.36.cloned.1.call-start = ((), (), s32[]{:S(2)}) async-start(), calls=%async_computation.20 | async-start | bytes 5308416 | tf_op jit(solution)/shard_map/reduce_scatter | solution.py:500
  308.1 242.3 %reduce-scatter.50.cloned.1.call-start = ((), (), s32[]{:S(2)}) async-start(), calls=%async_computation.29 | async-start | bytes 5898240
  308.2 0.7 copy-start.3
  308.2 0.7 copy-start.4
  308.2 0.7 copy-start.5
  308.2 0.7 copy-start.6
  308.2 0.7 copy-start.7
  308.2 0.7 copy-start.8
  308.2 0.7 copy-start.9
  308.3 0.7 copy-start.10
  308.7 269.0 %reduce-scatter.42.cloned.1.call-start = ((), (), s32[]{:S(2)}) async-start(), calls=%async_computation.25 | async-start | bytes 491520
  310.0 297.5 %reduce-scatter.40.cloned.1.call-start = ((), (), s32[]{:S(2)}) async-start(), calls=%async_computation.24 | async-start | bytes 245760
  338.9 293.3 %reduce-scatter.44.cloned.1.call-start = ((), (), s32[]{:S(2)}) async-start(), calls=%async_computation.26 | async-start | bytes 245760
  371.8 178.7 %copy-start.20 = (u32[32]{0:T(128)S(1)}, u32[32]{0:T(128)}, u32[]{:S(2)}) copy-start(u32[32]{0:T(128)} %constant.4) | copy-start | bytes 388
  371.8 179.9 %copy-start.2 = (f32[4,1,768]{2,1,0:T(1,128)S(1)}, f32[4,1,768]{2,1,0:T(1,128)}, u32[]{:S(2)}) copy-start(f32[4,1,768]{2,1,0:T(1,128)} %get-tuple-element.82) | copy-start | bytes 36868
  371.8 287.1 %reduce-scatter.46.cloned.1.call-start = ((), (), s32[]{:S(2)}) async-start(), calls=%async_computation.27 | async-start | bytes 245760
  405.1 280.4 %reduce-scatter.48.cloned.1.call-start = ((), (), s32[]{:S(2)}) async-start(), calls=%async_computation.28 | async-start | bytes 245760
  438.3 275.0 %reduce-scatter.38.cloned.1.call-start = ((), (), s32[]{:S(2)}) async-start(), calls=%async_computation.21 | async-start | bytes 737280 | tf_op jit(solution)/shard_map/reduce_scatter | solution.py:500
  492.1 256.1 %reduce-scatter.34.cloned.1.call-start = ((), (), s32[]{:S(2)}) async-start(), calls=%async_computation.19 | async-start | bytes 1327104 | tf_op jit(solution)/shard_map/reduce_scatter | solution.py:500
Sparse Core Ops, SparseCore 0:
  9.7 25.3 all-gather.11
  37.2 51.4 all-gather.9
  90.5 55.9 all-gather.13
  148.0 51.6 all-gather.15
  305.4 31.6 reduce-scatter.25
  339.3 30.6 reduce-scatter.27
  372.3 30.9 reduce-scatter.29
  405.7 30.8 reduce-scatter.31
  438.8 53.2 reduce-scatter.35
  494.9 55.4 reduce-scatter.49
  553.2 24.4 reduce-scatter.41
  580.9 23.9 reduce-scatter.39
  608.3 23.9 reduce-scatter.43
  634.9 23.9 reduce-scatter.45
  661.5 23.9 reduce-scatter.47
  688.2 25.0 reduce-scatter.37
  715.5 32.6 reduce-scatter.33

commit v2 on v1

--- a/solution.py
+++ b/solution.py
@@ -62,6 +62,190 @@
 
 def guess(flops, nbytes):
     return pl.CostEstimate(flops=int(flops), bytes_accessed=int(nbytes), transcendentals=0)
+
+
+def reverse(s, bits):
+    return sum(((s >> b) & 1) << (bits - 1 - b) for b in range(bits))
+
+
+def axis_facts():
+    dp, fsdp = lax.axis_size("dp"), lax.axis_size("fsdp")
+    return dp, fsdp, dp // 2, fsdp.bit_length() - 1
+
+
+def along_z(hop):
+    dp = lax.axis_size("dp")
+    return [(d, (d + 2 * hop) % dp) for d in range(dp)]
+
+
+def across_cores():
+    return [(d, d ^ 1) for d in range(lax.axis_size("dp"))]
+
+
+def along_bit(r):
+    dp, fsdp, _, bits = axis_facts()
+    pairs = []
+    for d in range(dp):
+        flip = 1 << (r if d % 2 == 0 else bits - 1 - r)
+        pairs += [(d * fsdp + f, d * fsdp + (f ^ flip)) for f in range(fsdp)]
+    return pairs
+
+
+def gather_blocks(block):
+    _, _, depth, bits = axis_facts()
+    parts = [block] + [lax.ppermute(block, "dp", along_z(s)) for s in range(1, depth)]
+    held = jnp.stack(parts)[None]
+    for r in range(bits):
+        got = lax.ppermute(held, ("dp", "fsdp"), along_bit(r))
+        if r < bits - 1:
+            held = jnp.concatenate([held, got])
+    own = [held, got]
+    return own + [lax.ppermute(v, "dp", across_cores()) for v in own]
+
+
+def add(left, right):
+    return (left.astype(f32) + right.astype(f32)).astype(bf16)
+
+
+def scatter_blocks(keep, send):
+    _, _, depth, bits = axis_facts()
+    got = lax.ppermute(send, "dp", across_cores())
+    for r in reversed(range(bits)):
+        half = keep.shape[0] // 2
+        upper = add(keep[half:], got[half:])
+        keep = add(keep[:half], got[:half])
+        got = lax.ppermute(upper, ("dp", "fsdp"), along_bit(r))
+    mine = [add(keep[0, s], got[0, s]) for s in range(1, depth)]
+    total = keep[0, 0].astype(f32) + got[0, 0].astype(f32)
+    for s in range(1, depth):
+        total = total + lax.ppermute(mine[s - 1], "dp", along_z(-s)).astype(f32)
+    return total
+
+
+def places():
+    dp, fsdp, depth, bits = axis_facts()
+    d, f = lax.axis_index("dp"), lax.axis_index("fsdp")
+    z, core = d // 2, d % 2
+    slot = jnp.arange(depth, dtype=jnp.int32)
+    index = jnp.arange(fsdp, dtype=jnp.int32)
+    mirror = sum((((index >> b) & 1) << (bits - 1 - b) for b in range(bits)), jnp.zeros_like(index))
+    rows, slots, columns = [], [], []
+    for n in range(2):
+        there = core ^ n
+        rows.append(2 * ((z - slot) % depth) + there)
+        away = index ^ f
+        mirrored = sum((((away >> b) & 1) << (bits - 1 - b) for b in range(bits)), jnp.zeros_like(index))
+        slots.append(jnp.where(there == 0, away, mirrored))
+        columns.append(f ^ jnp.where(there == 0, index, mirror))
+    return jnp.concatenate(rows + slots + columns).astype(jnp.int32)
+
+
+def row_of(place, n, slot, depth):
+    return place[n * depth + slot]
+
+
+def slot_of(place, n, j, depth, fsdp):
+    return place[2 * depth + n * fsdp + j]
+
+
+def column_of(place, n, s, depth, fsdp):
+    return place[2 * depth + 2 * fsdp + n * fsdp + s]
+
+
+def block_copies(place, arrays, target, sems):
+    half, depth = arrays[0].shape[:2]
+    fsdp = 2 * half
+    copies = []
+    for a, array in enumerate(arrays):
+        for q in range(half):
+            for slot in range(depth):
+                i = row_of(place, a // 2, slot, depth)
+                j = column_of(place, a // 2, (a % 2) * half + q, depth, fsdp)
+                copies.append(pltpu.make_async_copy(array.at[q, slot], target(i, j), sems.at[len(copies)]))
+    return copies
+
+
+def assemble_kernel(place, own_low, own_high, other_low, other_high, weights, vectors, ub):
+    step = pl.program_id(0)
+    half, _, height, width = own_low.shape
+    fsdp, depth, tall = 2 * half, pl.num_programs(0) // 2, height - 16
+    narrow = width // 4
+
+    def fill(n, low, high):
+        pieces = []
+        for j in range(fsdp):
+            slot = slot_of(place, n, j, depth, fsdp)
+            upper, q = slot >= half, lax.rem(slot, half)
+            pieces.append(jnp.where(upper, high[q, 0].astype(f32), low[q, 0].astype(f32)))
+        for m in range(4):
+            row = jnp.concatenate([p[:, m * narrow:(m + 1) * narrow] for p in pieces], axis=1)
+            weights[m] = row[:tall].astype(bf16)
+            vectors[m] = row[tall:]
+        for j in range(fsdp):
+            ub[j] = pieces[j][tall:]
+
+    @pl.when(step < depth)
+    def _():
+        fill(0, own_low, own_high)
+
+    @pl.when(step >= depth)
+    def _():
+        fill(1, other_low, other_high)
+
+
+def assemble(place, arrays):
+    half, depth, height, width = arrays[0].shape
+    fsdp, tall, d = 2 * half, height - 16, half * width // 2
+    own = pl.BlockSpec((half, 1, height, width), lambda s, place: (0, jnp.minimum(s, depth - 1), 0, 0))
+    other = pl.BlockSpec((half, 1, height, width), lambda s, place: (0, jnp.maximum(s - depth, 0), 0, 0))
+    return call(
+        assemble_kernel, "assemble", (2 * depth,),
+        [own, own, other, other],
+        [pl.BlockSpec((4, tall, d), lambda s, place: (0, place[s], 0)), whole((4, 16, d)), whole((fsdp, 16, width))],
+        [sds((4, 2 * depth * tall, d), bf16), sds((4, 16, d), f32), sds((fsdp, 16, width), f32)],
+        prefetch=1, cost=guess(1e9, 11e6),
+    )(place, *arrays)
+
+
+def pack_kernel(place, gq, gk, gv, go, vectors, gub, send, keep):
+    step = pl.program_id(0)
+    fsdp, _, height, width = send.shape
+    depth, tall, narrow = pl.num_programs(0) // 2, height - 16, width // 4
+
+    def fill(n, out):
+        for j in range(fsdp):
+            slot = slot_of(place, n, j, depth, fsdp)
+            columns = slice(j * narrow, (j + 1) * narrow)
+            out[slot, 0, :tall, :] = jnp.concatenate(
+                [g[:, columns].astype(f32) for g in (gq, gk, gv, go)], axis=1
+            ).astype(bf16)
+            slab = jnp.concatenate([vectors[m, :, columns] for m in range(4)], axis=1)
+            third = lax.broadcasted_iota(jnp.int32, slab.shape, 0) == 2
+            out[slot, 0, tall:, :] = jnp.where(third, gub[j], slab).astype(bf16)
+
+    @pl.when(step < depth)
+    def _():
+        fill(1, send)
+
+    @pl.when(step >= depth)
+    def _():
+        fill(0, keep)
+
+
+def pack(place, grads, vectors, gub):
+    d = grads[0].shape[0]
+    dp, fsdp, depth, _ = axis_facts()
+    tall, width = d // dp, 4 * d // fsdp
+    rows = pl.BlockSpec((tall, d), lambda s, place: (place[(s + depth) % (2 * depth)], 0))
+    sent = pl.BlockSpec((fsdp, 1, tall + 16, width), lambda s, place: (0, jnp.minimum(s, depth - 1), 0, 0))
+    kept = pl.BlockSpec((fsdp, 1, tall + 16, width), lambda s, place: (0, jnp.maximum(s - depth, 0), 0, 0))
+    return call(
+        pack_kernel, "pack", (2 * depth,),
+        [rows, rows, rows, rows, whole((4, 16, d)), whole((fsdp, 1, width))],
+        [sent, kept],
+        [sds((fsdp, depth, tall + 16, width), bf16)] * 2,
+        prefetch=1, cost=guess(1e9, 11e6),
+    )(place, *grads, vectors, gub)
 
 
 def segment_lanes(bucket, lengths, queries_ext, keys_ext):
@@ -254,14 +438,33 @@
     return u * phi, phi + u * bell * 0.3989422804014327
 
 
-def up_kernel(x, context, ow, ob, g1, b1, uw, ub, n1_out, r1_out, low_out, act_out, slope_out):
-    parts, _, wide = act_out.shape
+def up_kernel(
+    place, x, context, ow, ob, g1, b1, ub, u0, u1, u2, u3,
+    n1_out, r1_out, low_out, act_out, slope_out, uw, sems,
+):
+    wide = act_out.shape[2]
+    tall = u0.shape[2]
+    copies = block_copies(
+        place, (u0, u1, u2, u3), lambda i, j: uw.at[j, pl.ds(pl.multiple_of(i * tall, 16), tall), :], sems
+    )
+
+    @pl.when(pl.program_id(0) == 0)
+    def _():
+        for copy in copies:
+            copy.start()
+
     attended = dot(context[...], ow[0]) + ob[...]
     n1, r1 = normed(x[...].astype(f32) + attended)
     n1_out[...] = n1
     r1_out[...] = jnp.broadcast_to(r1, r1_out.shape)
     low = (n1 * g1[...] + b1[...]).astype(bf16)
     low_out[...] = low
+
+    @pl.when(pl.program_id(0) == 0)
+    def _():
+        for copy in copies:
+            copy.wait()
+
     each = uw.shape[2] // wide
     for j in range(uw.shape[0]):
         hidden = dot(low, uw[j]) + ub[j:j + 1, :]
@@ -272,39 +475,50 @@
             slope_out[j * each + c] = slope[:, c * wide:(c + 1) * wide]
 
 
-def up(x, context, weights, ob, g1, b1, uw, ub, parts):
+def up(place, x, context, weights, ob, g1, b1, ub, blocks):
     t, d = x.shape
-    f, _, wide = uw.shape
+    half, depth, tall, wide = blocks[0].shape
+    f, parts = 2 * half, 2 * depth
     narrow = f * wide // parts
-    rows = pl.BlockSpec((ROWS, d), lambda r: (r, 0))
-    tall = pl.BlockSpec((parts, ROWS, narrow), lambda r: (0, r, 0))
+    rows = pl.BlockSpec((ROWS, d), lambda r, *_: (r, 0))
+    high = pl.BlockSpec((parts, ROWS, narrow), lambda r, *_: (0, r, 0))
     return call(
         up_kernel, "up", (t // ROWS,),
-        [rows, rows, pl.BlockSpec((1, d, d), lambda r: (3, 0, 0)), whole((1, d)), whole((1, d)), whole((1, d)),
-         whole(uw.shape), whole(ub.shape)],
-        [rows, pl.BlockSpec((ROWS, 128), lambda r: (r, 0)), rows, tall, tall],
+        [rows, rows, pl.BlockSpec((1, d, d), lambda r, *_: (3, 0, 0)), whole((1, d)), whole((1, d)), whole((1, d)),
+         whole(ub.shape)] + [pl.BlockSpec(memory_space=pl.ANY)] * 4,
+        [rows, pl.BlockSpec((ROWS, 128), lambda r, *_: (r, 0)), rows, high, high, whole((f, d, wide))],
         [sds((t, d), f32), sds((t, 128), f32), sds((t, d), bf16), sds((parts, t, narrow), bf16),
-         sds((parts, t, narrow), bf16)],
-        cost=guess(12e9, 26e6),
-    )(x, context, weights, ob, g1, b1, uw, ub)
+         sds((parts, t, narrow), bf16), sds((f, d, wide), bf16)],
+        [pltpu.SemaphoreType.DMA((f * parts,))],
+        prefetch=1, cost=guess(12e9, 31e6),
+    )(place, x, context, weights, ob, g1, b1, ub, *blocks)
 
 
 def down_kernel(
-    bucket, lengths, act_rows, n1, g1, b1, dw, db, g2, b2, cotangent, act_part,
-    out, pooled, mixed_out, branch_out, gdb, gg2, gb2, gdw,
-    branch_t, counts,
+    place, bucket, lengths, act_rows, n1, g1, b1, db, g2, b2, cotangent, act_part, d0, d1, d2, d3,
+    out, pooled, mixed_out, branch_out, gdb, gg2, gb2, send, keep, dw,
+    branch_t, counts, sems,
 ):
     step = pl.program_id(0)
     tiles = branch_t.shape[1] // ROWS
     parts = dw.shape[0]
+    f, _, tall, _ = send.shape
+    depth = parts // 2
+    copies = block_copies(
+        place, (d0, d1, d2, d3), lambda i, j: dw.at[i, pl.ds(pl.multiple_of(j * tall, 16), tall), :], sems
+    )
 
     @pl.when(step == 0)
     def _():
+        for copy in copies:
+            copy.start()
         pooled[...] = jnp.zeros_like(pooled)
         counts[...] = jnp.zeros_like(counts)
         gdb[...] = jnp.zeros_like(gdb)
         gg2[...] = jnp.zeros_like(gg2)
         gb2[...] = jnp.zeros_like(gb2)
+        for copy in copies:
+            copy.wait()
 
     @pl.when(step < tiles)
     def _():
@@ -350,40 +564,56 @@
     def _():
         pooled[...] = pooled[...] / jnp.maximum(counts[...], 1.0)[:, :1]
 
-    @pl.when(step >= tiles)
-    def _():
-        gdw[0] = dot(branch_t[...], act_part[0]).astype(bf16)
-
-
-def down(bucket, lengths, active, n1, g1, b1, dw, db, g2, b2, cotangent):
+    def part(n, target):
+        found = dot(branch_t[...], act_part[0]).astype(bf16)
+        for j in range(f):
+            target[slot_of(place, n, j, depth, f), 0] = found[j * tall:(j + 1) * tall]
+
+    @pl.when((step >= tiles) & (step < tiles + depth))
+    def _():
+        part(1, send)
+
+    @pl.when(step >= tiles + depth)
+    def _():
+        part(0, keep)
+
+
+def down(place, bucket, lengths, active, n1, g1, b1, db, g2, b2, cotangent, blocks):
     parts, t, narrow = active.shape
     d = n1.shape[1]
     tiles = t // ROWS
     slots = lengths.shape[0]
+    half, depth, tall, _ = blocks[0].shape
+    f = 2 * half
     early = lambda s: jnp.minimum(s, tiles - 1)
-    late = lambda s: jnp.maximum(s - tiles, 0)
+    late = lambda s, place: place[(jnp.maximum(s - tiles, 0) + depth) % parts]
+    made = lambda first: pl.BlockSpec(
+        (f, 1, tall, narrow), lambda s, *_: (0, jnp.clip(s - tiles - first, 0, depth - 1), 0, 0)
+    )
     rows = pl.BlockSpec((ROWS, d), lambda s, *_: (early(s), 0))
     vector = whole((1, d))
     return call(
         down_kernel, "down", (tiles + parts,),
         [pl.BlockSpec((parts, ROWS, narrow), lambda s, *_: (0, early(s), 0)), rows, vector, vector,
-         whole(dw.shape), vector, vector, vector, rows,
-         pl.BlockSpec((1, t, narrow), lambda s, *_: (late(s), 0, 0))],
-        [rows, whole((slots, d)), rows, rows, vector, vector, vector,
-         pl.BlockSpec((1, d, narrow), lambda s, *_: (late(s), 0, 0))],
+         vector, vector, vector, rows,
+         pl.BlockSpec((1, t, narrow), lambda s, place, *_: (late(s, place), 0, 0))]
+        + [pl.BlockSpec(memory_space=pl.ANY)] * 4,
+        [rows, whole((slots, d)), rows, rows, vector, vector, vector, made(0), made(depth),
+         whole((parts, d, narrow))],
         [sds((t, d), bf16), sds((slots, d), f32), sds((t, d), f32), sds((t, d), bf16)]
-        + [sds((1, d), f32)] * 3 + [sds((parts, d, narrow), bf16)],
-        [pltpu.VMEM((d, t), bf16), pltpu.VMEM((slots, 128), f32)],
-        prefetch=2, cost=guess(12e9, 30e6),
-    )(bucket, lengths, active, n1, g1, b1, dw, db, g2, b2, cotangent, active)
+        + [sds((1, d), f32)] * 3 + [sds((f, depth, tall, narrow), bf16)] * 2 + [sds((parts, d, narrow), bf16)],
+        [pltpu.VMEM((d, t), bf16), pltpu.VMEM((slots, 128), f32), pltpu.SemaphoreType.DMA((f * parts,))],
+        prefetch=3, cost=guess(12e9, 35e6),
+    )(place, bucket, lengths, active, n1, g1, b1, db, g2, b2, cotangent, active, *blocks)
 
 
 def feed_back_kernel(
-    branch, slope, dw, uw, low_t, mixed, n1, r1, g1, context, ow,
-    guw, gub, inner_out, gg1, gb1, gob, gow, grad_context, delta_out,
-    hidden, grad_normed, attended,
+    place, branch, slope, dw, uw, low_t, mixed, n1, r1, g1, context, ow,
+    send, keep, gub, inner_out, gg1, gb1, gob, gow, grad_context, delta_out,
+    hidden, grad_normed, attended, found,
 ):
     j = pl.program_id(0)
+    _, depth, tall, _ = send.shape
     each, t, narrow = slope.shape
     d = branch.shape[1]
     tiles = t // ROWS
@@ -400,7 +630,11 @@
     sums = lax.fori_loop(0, tiles, gelu_rows, (jnp.zeros((1, narrow), f32),) * each)
     for c in range(each):
         gub[0, :, c * narrow:(c + 1) * narrow] = sums[c]
-    guw[0] = dot(low_t[...], hidden[...]).astype(bf16)
+    found[...] = dot(low_t[...], hidden[...]).astype(bf16)
+    for n, target in ((1, send), (0, keep)):
+        for slot in range(depth):
+            i = row_of(place, n, slot, depth)
+            target[0, slot] = found[pl.ds(pl.multiple_of(i * tall, 16), tall), :]
 
     @pl.when(j == 0)
     def _():
@@ -443,24 +677,27 @@
         gow[...] = dot_tn(context[...], attended[...]).astype(bf16)
 
 
-def feed_back(branch, slope, dw, uw, low_t, mixed, n1, r1, g1, context, weights):
+def feed_back(place, branch, slope, dw, uw, low_t, mixed, n1, r1, g1, context, weights):
     parts, t, narrow = slope.shape
     f, d, wide = uw.shape
-    each = parts // f
+    each, depth, tall = parts // f, parts // 2, d // parts
+    made = lambda n: pl.BlockSpec(
+        (1, depth, tall, wide), lambda j, place: (slot_of(place, n, j, depth, f), 0, 0, 0)
+    )
     vector = whole((1, d))
     return call(
         feed_back_kernel, "feed_back", (f,),
-        [whole((t, d)), pl.BlockSpec((each, t, narrow), lambda j: (j, 0, 0)),
-         pl.BlockSpec((each, d, narrow), lambda j: (j, 0, 0)), pl.BlockSpec((1, d, wide), lambda j: (j, 0, 0)),
+        [whole((t, d)), pl.BlockSpec((each, t, narrow), lambda j, *_: (j, 0, 0)),
+         pl.BlockSpec((each, d, narrow), lambda j, *_: (j, 0, 0)), pl.BlockSpec((1, d, wide), lambda j, *_: (j, 0, 0)),
          whole((d, t)), whole((t, d)), whole((t, d)), whole((t, 128)), vector, whole((t, d)),
-         pl.BlockSpec((1, d, d), lambda j: (3, 0, 0))],
-        [pl.BlockSpec((1, d, wide), lambda j: (j, 0, 0)), pl.BlockSpec((1, 1, wide), lambda j: (j, 0, 0)),
+         pl.BlockSpec((1, d, d), lambda j, *_: (3, 0, 0))],
+        [made(1), made(0), pl.BlockSpec((1, 1, wide), lambda j, *_: (j, 0, 0)),
          whole((t, d)), vector, vector, vector, whole((d, d)), whole((t, d)), whole((128, t))],
-        [sds((f, d, wide), bf16), sds((f, 1, wide), f32), sds((t, d), f32)] + [sds((1, d), f32)] * 3
+        [sds((f, depth, tall, wide), bf16)] * 2 + [sds((f, 1, wide), f32), sds((t, d), f32)] + [sds((1, d), f32)] * 3
         + [sds((d, d), bf16), sds((t, d), bf16), sds((128, t), f32)],
-        [pltpu.VMEM((t, wide), bf16), pltpu.VMEM((t, d), f32), pltpu.VMEM((t, d), bf16)],
-        cost=guess(18e9, 45e6),
-    )(branch, slope, dw, uw, low_t, mixed, n1, r1, g1, context, weights)
+        [pltpu.VMEM((t, wide), bf16), pltpu.VMEM((t, d), f32), pltpu.VMEM((t, d), bf16), pltpu.VMEM((d, wide), bf16)],
+        prefetch=1, cost=guess(18e9, 45e6),
+    )(place, branch, slope, dw, uw, low_t, mixed, n1, r1, g1, context, weights)
 
 
 def shards(
@@ -472,42 +709,49 @@
     dp, fsdp = lax.axis_size("dp"), lax.axis_size("fsdp")
     lengths = lengths[0]
 
-    def gather(v, axis, dim, tiled=True):
-        return lax.all_gather(v, axis, axis=dim, tiled=tiled)
-
-    stack = jnp.stack([query_weight, key_weight, value_weight, out_weight])
-    weights = gather(gather(stack, "fsdp", 2), "dp", 1)
-    uw = gather(gather(up_weight, "dp", 0), "fsdp", 0, False)
-    dw = gather(gather(down_weight.T, "fsdp", 0), "dp", 0, False)
-    vectors = jnp.stack([query_bias, value_bias, out_bias, norm1_gain, norm1_bias, down_bias, norm2_gain, norm2_bias])
-    vectors = gather(vectors, "fsdp", 1).astype(f32)
-    qb, vb, ob, g1, b1, db, g2, b2 = (vectors[n:n + 1] for n in range(8))
-    ub = gather(up_bias, "fsdp", 0, False).astype(f32)
+    place = places()
+    spare = jnp.zeros((13, 4 * d // fsdp), bf16)
+    block = jnp.concatenate([
+        jnp.concatenate([query_weight, key_weight, value_weight, out_weight], axis=1),
+        jnp.concatenate([query_bias, value_bias, out_bias, norm1_gain])[None],
+        jnp.concatenate([norm1_bias, down_bias, norm2_gain, norm2_bias])[None],
+        up_bias[None],
+        spare,
+    ])
+    attention_blocks = gather_blocks(block)
+    up_blocks = gather_blocks(up_weight)
+    down_blocks = gather_blocks(down_weight.T)
+
+    weights, vectors, ub = assemble(place, attention_blocks)
+    qb, vb, ob, g1 = (vectors[m, 0:1] for m in range(4))
+    b1, db, g2, b2 = (vectors[m, 1:2] for m in range(4))
+    ub = ub[:, 2]
 
     q, k, v, context, lse = attend(bucket, lengths, tokens, weights, qb, vb)
-    n1, r1, low, active, slope = up(tokens, context, weights, ob, g1, b1, uw, ub, dp)
-    out, pooled, mixed, branch, gdb, gg2, gb2, gdw = down(
-        bucket, lengths, active, n1, g1, b1, dw, db, g2, b2, cotangent
-    )
-    guw, gub, inner, gg1, gb1, gob, gow, grad_context, delta = feed_back(
-        branch, slope, dw, uw, low.T, mixed, n1, r1, g1, context, weights
-    )
+    n1, r1, low, active, slope, uw = up(place, tokens, context, weights, ob, g1, b1, ub, up_blocks)
+    out, pooled, mixed, branch, gdb, gg2, gb2, send_d, keep_d, dw = down(
+        place, bucket, lengths, active, n1, g1, b1, db, g2, b2, cotangent, down_blocks
+    )
+    made_d = scatter_blocks(keep_d, send_d)
+    send_u, keep_u, gub, inner, gg1, gb1, gob, gow, grad_context, delta = feed_back(
+        place, branch, slope, dw, uw, low.T, mixed, n1, r1, g1, context, weights
+    )
+    made_u = scatter_blocks(keep_u, send_u)
     gqw, gkw, gvw, gqb, gvb, input_grad = attend_back(
         bucket, lengths, tokens.T, q, k, v, grad_context, lse, delta, weights, inner
     )
-
-    def scatter(g, axis, dim, tiled=True):
-        return lax.psum_scatter(g, axis, scatter_dimension=dim, tiled=tiled)
-
-    made_u = scatter(scatter(guw, "fsdp", 0, False), "dp", 0).astype(f32)
-    made_d = scatter(scatter(gdw, "dp", 0, False), "fsdp", 0).T.astype(f32)
-    made = [scatter(scatter(g, "dp", 0), "fsdp", 1).astype(f32) for g in (gqw, gkw, gvw, gow)]
-    rows = jnp.concatenate([gqb, gvb, gob, gg1, gb1, gdb, gg2, gb2], axis=0)
-    rows = lax.psum(scatter(rows, "fsdp", 1), "dp")
-    gub = lax.psum(scatter(gub.reshape(-1), "fsdp", 0), "dp")
+    firsts = jnp.stack([gqb, gvb, gob, gg1])
+    seconds = jnp.stack([gb1, gdb, gg2, gb2])
+    vectors = jnp.concatenate([firsts, seconds, jnp.zeros((4, 14, d), f32)], axis=1)
+    send_a, keep_a = pack(place, (gqw, gkw, gvw, gow), vectors, gub)
+    made_a = scatter_blocks(keep_a, send_a)
+
+    tall, narrow = d // dp, d // fsdp
+    made = [made_a[:tall, m * narrow:(m + 1) * narrow] for m in range(4)]
+    rows = [made_a[tall + n, m * narrow:(m + 1) * narrow] for n in range(2) for m in range(4)]
     return (
         out, pooled, input_grad, made[0], rows[0], made[1], made[2], rows[1], made[3], rows[2], rows[3], rows[4],
-        made_u, gub, made_d, rows[5], rows[6], rows[7],
+        made_u, made_a[tall + 2], made_d.T, rows[5], rows[6], rows[7],
     )
 
 

time: 757 us -> 393 us (0.52)
  waiting for transfers between devices: 476 us -> 129 us
  blocking collectives: 83.1 us -> 0 us
  starting transfers between devices: 0.68 us -> 56.2 us
  Pallas kernels: 153 us -> 178 us
  between operations: 15.7 us -> 1.67 us
  local copies, waits for them, and re-layouts: 20.3 us -> 12.5 us
    reduce_scatter x7 -> x0, waiting for transfers between devices: 234 us -> none  [scatter(): return lax.psum_scatter(g, axis, scatter_dimension=dim, tiled=tiled)]
    unnamed x23 -> x0, waiting for transfers between devices: 146 us -> none
    ppermute x0 -> x39, waiting for transfers between devices: none -> 129 us  [the longest x6 41.4 us: scatter_blocks(): got = lax.ppermute(upper, ('dp', 'fsdp'), along_bit(r))]
    all_gather x4 -> x0, waiting for transfers between devices: 95.4 us -> none  [gather(): return lax.all_gather(v, axis, axis=dim, tiled=tiled)]
    ppermute x0 -> x39, starting transfers between devices: none -> 56.2 us  [the longest x9 27.5 us: gather_blocks(): lax.ppermute(block, 'dp', along_z(s))]
    all_gather x4 -> x0, blocking collectives: 39.9 us -> none  [gather(): return lax.all_gather(v, axis, axis=dim, tiled=tiled)]
    psum x1 -> x0, blocking collectives: 28.2 us -> none  [shards(): rows = lax.psum(scatter(rows, 'fsdp', 1), 'dp')]
    pallas_call x0 -> x2, Pallas kernels: none -> 17.8 us  [the longest x1 9.04 us: pack(): call(pack_kernel, 'pack', (2 * depth,), [rows, rows, rows, rows, whole((4...]
  transfers between devices with their start and end apart: 17 -> 39, of which waited for: 16 -> 19; matrix products, arithmetic and copies ran while one was open for 3% -> 5% of each run, Pallas kernels for 6% -> 37%
where the time goes in v2:
time: 393 us; the launch traced here: 392 us
  Pallas kernels  178 us (45%)
  waiting for transfers between devices  129 us (33%)
  starting transfers between devices  56.2 us (14%)
  other arithmetic  13.8 us (4%)
  local copies, waits for them, and re-layouts  12.5 us (3%)
    ppermute x6, waiting for transfers between devices, scatter_blocks(): got = lax.ppermute(upper, ('dp', 'fsdp'), along_bit(r))  41.4 us
    pallas_call x1, Pallas kernels, feed_back(): call(feed_back_kernel, 'feed_back', (f,), [whole((t, d)), pl.BlockSpec((e...  40.7 us
    ppermute x6, waiting for transfers between devices, gather_blocks(): got = lax.ppermute(held, ('dp', 'fsdp'), along_bit(r))  40.2 us
    pallas_call x1, Pallas kernels, attend_back(): call(attend_back_kernel, 'attend_back', (pairs,), [whole((d, t)), tall, t...  38 us
    pallas_call x1, Pallas kernels, down(): call(down_kernel, 'down', (tiles + parts,), [pl.BlockSpec((parts, ROWS, n...  31.7 us
    ppermute x9, starting transfers between devices, gather_blocks(): lax.ppermute(block, 'dp', along_z(s))  27.5 us
    pallas_call x1, Pallas kernels, up(): call(up_kernel, 'up', (t // ROWS,), [rows, rows, pl.BlockSpec((1, d, d),...  26.2 us
    ppermute x9, waiting for transfers between devices, scatter_blocks(): total = total + lax.ppermute(mine[s - 1], 'dp', along_z(-s)).astype(f32)  26.1 us
  transfers between devices with their start and end apart: 39, of which 19 were waited for; matrix products, arithmetic and copies ran while one was open for 5% of the time, Pallas kernels for 37%

profile of v2, /device:TPU:0, one launch (start us, length us, event | category | flops | bytes accessed | tf_op | source)
XLA Modules:
  0.0 391.7 jit_solution(3129126843742503878)
XLA Ops:
  4.2 3.1 collective-permute-start
  7.3 2.6 collective-permute-start.1
  9.8 1.3 collective-permute-start.2
  11.2 3.4 collective-permute-done
  14.6 6.5 %collective-permute-done.1 = bf16[112,768]{1,0:T(8,128)(2,1)S(1)} collective-permute-done((bf16[112,768]{1,0:T(8,128)(2,1)S(1)}, bf16[112,768]{1,0:T(8,128)(2,1)S(1)}, u32[]{:S(2)}, u32[]{:S(2)}) %collective-permute-start.1) | collective-permute-done | bytes 172064 | tf_op jit(solution)/shard_map/ppermute | solution.py:96
  21.2 1.6 collective-permute-start.3
  22.8 9.4 %collective-permute-done.3 = bf16[1,4,112,768]{3,2,1,0:T(8,128)(2,1)S(1)} collective-permute-done((bf16[1,4,112,768]{3,2,1,0:T(8,128)(2,1)S(1)}, bf16[1,4,112,768]{3,2,1,0:T(8,128)(2,1)S(1)}, u32[]{:S(2)}, u32[]{:S(2)}) %collective-permute-start.3) | collective-permute-done | bytes 688160 | tf_op jit(solution)/shard_map/ppermute | solution.py:99
  32.4 1.6 collective-permute-start.4
  34.0 4.2 %collective-permute-start.7 = (bf16[96,768]{1,0:T(8,128)(2,1)S(1)}, bf16[96,768]{1,0:T(8,128)(2,1)S(1)}, u32[]{:S(2)}, u32[]{:S(2)}) collective-permute-start(bf16[96,768]{1,0:T(8,128)(2,1)S(1)} %copy-done.6), channel_id=1, source_target_pairs={{0,8},{4,12},{8,16},{12,20},{16,24},{20,28},{24,0},{28,4},{1,9},{5... | collective-permute-start | bytes 442376 | tf_op jit(solution)/shard_map/ppermute | solution.py:96
  38.1 1.6 collective-permute-start.8
  40.5 1.3 collective-permute-start.14
  41.8 2.2 collective-permute-done.7
  44.0 5.2 %collective-permute-start.15 = (bf16[192,384]{1,0:T(8,128)(2,1)S(1)}, bf16[192,384]{1,0:T(8,128)(2,1)S(1)}, u32[]{:S(2)}, u32[]{:S(2)}) collective-permute-start(bf16[192,384]{1,0:T(8,128)(2,1)S(1)} %bitcast.105), channel_id=1, source_target_pairs={{0,16},{4,20},{8,24},{12,28},{16,0},{20,4},{24,8},{28,12},{1,17},{... | collective-permute-start | bytes 442376 | tf_op jit(solution)/shard_map/ppermute | solution.py:96
  49.2 2.9 collective-permute-done.8
  52.1 7.4 %collective-permute-start.16 = (bf16[192,384]{1,0:T(8,128)(2,1)S(1)}, bf16[192,384]{1,0:T(8,128)(2,1)S(1)}, u32[]{:S(2)}, u32[]{:S(2)}) collective-permute-start(bf16[192,384]{1,0:T(8,128)(2,1)S(1)} %bitcast.106), channel_id=1, source_target_pairs={{0,24},{4,28},{8,0},{12,4},{16,8},{20,12},{24,16},{28,20},{1,25},{... | collective-permute-start | bytes 442376 | tf_op jit(solution)/shard_map/ppermute | solution.py:96
  59.6 1.5 collective-permute-start.10
  62.2 1.5 collective-permute-start.17
  64.3 6.4 %collective-permute-done.10 = bf16[1,4,96,768]{3,2,1,0:T(8,128)(2,1)S(1)} collective-permute-done((bf16[1,4,96,768]{3,2,1,0:T(8,128)(2,1)S(1)}, bf16[1,4,96,768]{3,2,1,0:T(8,128)(2,1)S(1)}, u32[]{:S(2)}, u32[]{:S(2)}) %collective-permute-start.10) | collective-permute-done | bytes 589856 | tf_op jit(solution)/shard_map/ppermute | solution.py:99
  72.0 11.4 %collective-permute-done.17 = bf16[1,4,192,384]{3,2,1,0:T(8,128)(2,1)S(1)} collective-permute-done((bf16[1,4,192,384]{3,2,1,0:T(8,128)(2,1)S(1)}, bf16[1,4,192,384]{3,2,1,0:T(8,128)(2,1)S(1)}, u32[]{:S(2)}, u32[]{:S(2)}) %collective-permute-start.17) | collective-permute-done | bytes 589856 | tf_op jit(solution)/shard_map/ppermute | solution.py:99
  85.3 1.7 copy.38
  88.7 12.3 %collective-permute-done.18.d1 = bf16[2,4,192,384]{3,2,1,0:T(8,128)(2,1)} collective-permute-done((bf16[2,4,192,384]{3,2,1,0:T(8,128)(2,1)}, bf16[2,4,192,384]{3,2,1,0:T(8,128)(2,1)}, u32[]{:S(2)}, u32[]{:S(2)}) %collective-permute-start.18) | collective-permute-done | bytes 1179680 | tf_op jit(solution)/shard_map/ppermute | solution.py:99
  101.5 8.8 %assemble.1 = (bf16[4,768,768]{2,1,0:T(8,128)(2,1)}, f32[4,16,768]{2,1,0:T(8,128)}, f32[4,16,768]{2,1,0:T(8,128)}) custom-call(s32[24]{0:T(128)} %concatenate.27.place, bf16[2,4,112,768]{3,2,1,0:T(8,128)(2,1)} %copy-done, bf16[2,4,112,768]{3,2,1,0:T(8,128)(2,1)} %collective-permute-done.4.own_high, ...), custom_call_target="tpu_custom_call" | custom-call | flops 1000000000 | bytes 11000000 | tf_op jit(solution)/shard_map/assemble/pallas_call | solution.py:201
  110.3 1.5 slice_bitcast_fusion.1
  112.9 24.1 %attend.1 = (bf16[1024,768]{1,0:T(8,128)(2,1)}, bf16[1024,768]{1,0:T(8,128)(2,1)}, bf16[1024,768]{1,0:T(8,128)(2,1)}, bf16[1024,768]{1,0:T(8,128)(2,1)}, f32[128,1024]{1,0:T(8,128)}) custom-call(s32[1]{0:T(128)S(6)} %copy.40.bucket, s32[8]{0:T(128)} %bitcast.130, bf16[1024,768]{1,0:T(8,128)(2,1)} %x.3, bf16[4,768,768]{2,1,0:T(8,128)(2,1)} %get-tuple-element.60.qw.kw.vw.ow, ...), custom_call_target="tpu_custom_call" | custom-call | flops 15000000512 | bytes 12000000 | tf_op jit(solution)/shard_map/attend/pallas_call | solution.py:329
  137.6 26.2 %up.1 = (f32[1024,768]{1,0:T(8,128)}, f32[1024,128]{1,0:T(8,128)}, bf16[1024,768]{1,0:T(8,128)(2,1)}, bf16[8,1024,384]{2,1,0:T(8,128)(2,1)}, bf16[8,1024,384]{2,...) custom-call(s32[24]{0:T(128)} %concatenate.27.place, bf16[1024,768]{1,0:T(8,128)(2,1)} %x.3, ...), custom_call_target="tpu_custom_call" | custom-call | flops 12000000000 | bytes 31000000 | tf_op jit(solution)/shard_map/up/pallas_call | solution.py:485
  165.2 31.7 %down.1 = (bf16[1024,768]{1,0:T(8,128)(2,1)}, f32[8,768]{1,0:T(8,128)}, f32[1024,768]{1,0:T(8,128)}, bf16[1024,768]{1,0:T(8,128)(2,1)}, f32[1,768]{1,0:T(1,128)}...) custom-call(s32[24]{0:T(128)} %concatenate.27.place, ...), custom_call_target="tpu_custom_call" | custom-call | flops 12000000000 | bytes 35000000 | tf_op jit(solution)/shard_map/down/pallas_call | solution.py:595
  197.1 1.6 copy.39
  198.7 40.7 %feed_back.1 = (bf16[4,4,96,768]{3,2,1,0:T(8,128)(2,1)}, bf16[4,4,96,768]{3,2,1,0:T(8,128)(2,1)}, f32[4,1,768]{2,1,0:T(1,128)}, f32[1024,768]{1,0:T(8,128)}, f32...) custom-call(s32[24]{0:T(128)} %concatenate.27.place, ...), custom_call_target="tpu_custom_call" | custom-call | flops 17999998976 | bytes 45000000 | tf_op jit(solution)/shard_map/feed_back/pallas_call | solution.py:688
  239.5 38.0 %attend_back.1 = (bf16[768,768]{1,0:T(8,128)(2,1)}, bf16[768,768]{1,0:T(8,128)(2,1)}, bf16[768,768]{1,0:T(8,128)(2,1)}, f32[1,768]{1,0:T(1,128)}, f32[1,768]{1,0:T(1,128)}, /*index=5*/f32[1024,768]{1,0:T(8,128)}) custom-call(s32[1]{0:T(128)S(6)} %copy.40.bucket, s32[8]{0:T(128)} %bitcast.132, bf16[768,1024]{1,0:T(8,128)(2,1)} %bitcast.97, ...), custom_call_target="tpu_custom_call" | custom-call | flops 30000001024 | bytes 25000000 | tf_op jit(solution)/shard_map/attend_back/pallas_call | solution.py:405
  277.5 1.4 maximum_maximum_fusion.vectors
  278.9 9.0 %pack.1 = (bf16[4,4,112,768]{3,2,1,0:T(8,128)(2,1)}, bf16[4,4,112,768]{3,2,1,0:T(8,128)(2,1)}) custom-call(s32[24]{0:T(128)} %concatenate.27.place, bf16[768,768]{1,0:T(8,128)(2,1)} %get-tuple-element.83.gq, bf16[768,768]{1,0:T(8,128)(2,1)} %get-tuple-element.84.gk, bf16[768,768]{1,0:T(8,128)(2,1)} %get-tuple-element.85.gv, ...), custom_call_target="tpu_custom_call" | custom-call | flops 1000000000 | bytes 11000000 | tf_op jit(solution)/shard_map/pack/pallas_call | solution.py:242
  288.5 2.5 add_convert_fusion.3
  291.2 5.5 %collective-permute-done.27 = bf16[4,4,96,768]{3,2,1,0:T(8,128)(2,1)S(1)} collective-permute-done((bf16[4,4,96,768]{3,2,1,0:T(8,128)(2,1)}, bf16[4,4,96,768]{3,2,1,0:T(8,128)(2,1)S(1)}, u32[]{:S(2)}, u32[]{:S(2)}) %collective-permute-start.27) | collective-permute-done | bytes 2359328 | tf_op jit(solution)/shard_map/ppermute | solution.py:112
  300.4 6.9 %collective-permute-done.34 = bf16[2,4,192,384]{3,2,1,0:T(8,128)(2,1)S(1)} collective-permute-done((bf16[2,4,192,384]{3,2,1,0:T(8,128)(2,1)S(1)}, bf16[2,4,192,384]{3,2,1,0:T(8,128)(2,1)S(1)}, u32[]{:S(2)}, u32[]{:S(2)}) %collective-permute-start.34) | collective-permute-done | bytes 1179680 | tf_op jit(solution)/shard_map/ppermute | solution.py:117
  307.6 2.5 collective-permute-start.35
  310.1 16.2 %collective-permute-done.28 = bf16[2,4,96,768]{3,2,1,0:T(8,128)(2,1)S(1)} collective-permute-done((bf16[2,4,96,768]{3,2,1,0:T(8,128)(2,1)S(1)}, bf16[2,4,96,768]{3,2,1,0:T(8,128)(2,1)S(1)}, u32[]{:S(2)}, u32[]{:S(2)}) %collective-permute-start.28) | collective-permute-done | bytes 1179680 | tf_op jit(solution)/shard_map/ppermute | solution.py:117
  326.5 2.5 collective-permute-start.29
  329.0 18.3 %collective-permute-done.22 = bf16[2,4,112,768]{3,2,1,0:T(8,128)(2,1)S(1)} collective-permute-done((bf16[2,4,112,768]{3,2,1,0:T(8,128)(2,1)S(1)}, bf16[2,4,112,768]{3,2,1,0:T(8,128)(2,1)S(1)}, u32[]{:S(2)}, u32[]{:S(2)}) %collective-permute-start.22) | collective-permute-done | bytes 1376288 | tf_op jit(solution)/shard_map/ppermute | solution.py:117
  347.7 2.5 collective-permute-start.23
  350.4 1.9 collective-permute-start.38
  352.5 2.4 collective-permute-start.30
  354.9 3.8 collective-permute-done.36
  358.7 7.5 %collective-permute-done.37 = bf16[192,384]{1,0:T(8,128)(2,1)S(1)} collective-permute-done((bf16[192,384]{1,0:T(8,128)(2,1)S(1)}, bf16[192,384]{1,0:T(8,128)(2,1)S(1)}, u32[]{:S(2)}, u32[]{:S(2)}) %collective-permute-start.37) | collective-permute-done | bytes 147488 | tf_op jit(solution)/shard_map/ppermute | solution.py:121
  367.2 3.9 collective-permute-start.24
  372.1 1.9 collective-permute-start.26
  374.0 1.7 collective-permute-done.31
  376.6 1.7 collective-permute-done.24
  378.3 11.2 %collective-permute-done.25 = bf16[112,768]{1,0:T(8,128)(2,1)S(1)} collective-permute-done((bf16[112,768]{1,0:T(8,128)(2,1)S(1)}, bf16[112,768]{1,0:T(8,128)(2,1)S(1)}, u32[]{:S(2)}, u32[]{:S(2)}) %collective-permute-start.25) | collective-permute-done | bytes 172064 | tf_op jit(solution)/shard_map/ppermute | solution.py:121
  (110 shorter events, 24.9 us)
Async XLA Ops:
  4.2 10.4 %collective-permute-start = (bf16[112,768]{1,0:T(8,128)(2,1)S(1)}, bf16[112,768]{1,0:T(8,128)(2,1)S(1)}, u32[]{:S(2)}, u32[]{:S(2)}) collective-permute-start(bf16[112,768]{1,0:T(8,128)(2,1)S(1)} %concatenate.31), channel_id=1, source_target_pairs={{0,8},{4,12},{8,16},{12,20},{16,24},{20,28},{24,0},{28,4},{1,9},{5... | collective-permute-start | bytes 516104 | tf_op jit(solution)/shard_map/ppermute | solution.py:96
  7.3 13.9 %collective-permute-start.1 = (bf16[112,768]{1,0:T(8,128)(2,1)S(1)}, bf16[112,768]{1,0:T(8,128)(2,1)S(1)}, u32[]{:S(2)}, u32[]{:S(2)}) collective-permute-start(bf16[112,768]{1,0:T(8,128)(2,1)S(1)} %concatenate.31), channel_id=1, source_target_pairs={{0,16},{4,20},{8,24},{12,28},{16,0},{20,4},{24,8},{28,12},{1,17},{... | collective-permute-start | bytes 516104 | tf_op jit(solution)/shard_map/ppermute | solution.py:96
  9.8 11.3 %collective-permute-start.2 = (bf16[112,768]{1,0:T(8,128)(2,1)S(1)}, bf16[112,768]{1,0:T(8,128)(2,1)S(1)}, u32[]{:S(2)}, u32[]{:S(2)}) collective-permute-start(bf16[112,768]{1,0:T(8,128)(2,1)S(1)} %concatenate.31), channel_id=1, source_target_pairs={{0,24},{4,28},{8,0},{12,4},{16,8},{20,12},{24,16},{28,20},{1,25},{... | collective-permute-start | bytes 516104 | tf_op jit(solution)/shard_map/ppermute | solution.py:96
  21.2 19.3 %copy-start.7 = (bf16[384,192]{0,1:T(8,128)(2,1)S(1)}, bf16[384,192]{0,1:T(8,128)(2,1)}, u32[]{:S(2)}) copy-start(bf16[384,192]{0,1:T(8,128)(2,1)} %param.34) | copy-start | bytes 442372
  21.2 11.0 %collective-permute-start.3 = (bf16[1,4,112,768]{3,2,1,0:T(8,128)(2,1)S(1)}, bf16[1,4,112,768]{3,2,1,0:T(8,128)(2,1)S(1)}, u32[]{:S(2)}, u32[]{:S(2)}) collective-permute-start(bf16[1,4,112,768]{3,2,1,0:T(8,128)(2,1)S(1)} %maximum_bitcast_fusion), channel_id=1, source_target_pairs={{0,1},{1,0},{2,3},{3,2},{4,6},{5,7},{6,4},{7,5},{8,9},{9,8},{10,11... | collective-permute-start | bytes 2064392 | tf_op jit(solution)/shard_map/ppermute | solution.py:99
  32.4 39.4 %copy-start = (bf16[2,4,112,768]{3,2,1,0:T(8,128)(2,1)}, bf16[2,4,112,768]{3,2,1,0:T(8,128)(2,1)S(1)}, u32[]{:S(2)}) copy-start(bf16[2,4,112,768]{3,2,1,0:T(8,128)(2,1)S(1)} %pad_maximum_fusion.own_low) | copy-start | bytes 4128772
  32.4 31.4 %collective-permute-start.4 = (bf16[2,4,112,768]{3,2,1,0:T(8,128)(2,1)S(1)}, bf16[2,4,112,768]{3,2,1,0:T(8,128)(2,1)}, u32[]{:S(2)}, u32[]{:S(2)}) collective-permute-start(bf16[2,4,112,768]{3,2,1,0:T(8,128)(2,1)S(1)} %pad_maximum_fusion.own_low), channel_id=1, source_target_pairs={{0,2},{1,3},{2,0},{3,1},{4,5},{5,4},{6,7},{7,6},{8,10},{9,11},{10,... | collective-permute-start | bytes 4128776 | tf_op jit(solution)/shard_map/ppermute | solution.py:99
  34.0 10.0 %collective-permute-start.7 = (bf16[96,768]{1,0:T(8,128)(2,1)S(1)}, bf16[96,768]{1,0:T(8,128)(2,1)S(1)}, u32[]{:S(2)}, u32[]{:S(2)}) collective-permute-start(bf16[96,768]{1,0:T(8,128)(2,1)S(1)} %copy-done.6), channel_id=1, source_target_pairs={{0,8},{4,12},{8,16},{12,20},{16,24},{20,28},{24,0},{28,4},{1,9},{5... | collective-permute-start | bytes 442376 | tf_op jit(solution)/shard_map/ppermute | solution.py:96
  38.1 13.9 %collective-permute-start.8 = (bf16[96,768]{1,0:T(8,128)(2,1)S(1)}, bf16[96,768]{1,0:T(8,128)(2,1)S(1)}, u32[]{:S(2)}, u32[]{:S(2)}) collective-permute-start(bf16[96,768]{1,0:T(8,128)(2,1)S(1)} %copy-done.6), channel_id=1, source_target_pairs={{0,16},{4,20},{8,24},{12,28},{16,0},{20,4},{24,8},{28,12},{1,17},{... | collective-permute-start | bytes 442376 | tf_op jit(solution)/shard_map/ppermute | solution.py:96
  39.8 19.7 %collective-permute-start.9 = (bf16[96,768]{1,0:T(8,128)(2,1)S(1)}, bf16[96,768]{1,0:T(8,128)(2,1)S(1)}, u32[]{:S(2)}, u32[]{:S(2)}) collective-permute-start(bf16[96,768]{1,0:T(8,128)(2,1)S(1)} %copy-done.6), channel_id=1, source_target_pairs={{0,24},{4,28},{8,0},{12,4},{16,8},{20,12},{24,16},{28,20},{1,25},{... | collective-permute-start | bytes 442376 | tf_op jit(solution)/shard_map/ppermute | solution.py:96
  40.5 20.6 %collective-permute-start.14 = (bf16[192,384]{1,0:T(8,128)(2,1)S(1)}, bf16[192,384]{1,0:T(8,128)(2,1)S(1)}, u32[]{:S(2)}, u32[]{:S(2)}) collective-permute-start(bf16[192,384]{1,0:T(8,128)(2,1)S(1)} %bitcast.104), channel_id=1, source_target_pairs={{0,8},{4,12},{8,16},{12,20},{16,24},{20,28},{24,0},{28,4},{1,9},{5... | collective-permute-start | bytes 442376 | tf_op jit(solution)/shard_map/ppermute | solution.py:96
  44.0 17.1 %collective-permute-start.15 = (bf16[192,384]{1,0:T(8,128)(2,1)S(1)}, bf16[192,384]{1,0:T(8,128)(2,1)S(1)}, u32[]{:S(2)}, u32[]{:S(2)}) collective-permute-start(bf16[192,384]{1,0:T(8,128)(2,1)S(1)} %bitcast.105), channel_id=1, source_target_pairs={{0,16},{4,20},{8,24},{12,28},{16,0},{20,4},{24,8},{28,12},{1,17},{... | collective-permute-start | bytes 442376 | tf_op jit(solution)/shard_map/ppermute | solution.py:96
  52.1 10.1 %collective-permute-start.16 = (bf16[192,384]{1,0:T(8,128)(2,1)S(1)}, bf16[192,384]{1,0:T(8,128)(2,1)S(1)}, u32[]{:S(2)}, u32[]{:S(2)}) collective-permute-start(bf16[192,384]{1,0:T(8,128)(2,1)S(1)} %bitcast.106), channel_id=1, source_target_pairs={{0,24},{4,28},{8,0},{12,4},{16,8},{20,12},{24,16},{28,20},{1,25},{... | collective-permute-start | bytes 442376 | tf_op jit(solution)/shard_map/ppermute | solution.py:96
  59.6 11.1 %collective-permute-start.10 = (bf16[1,4,96,768]{3,2,1,0:T(8,128)(2,1)S(1)}, bf16[1,4,96,768]{3,2,1,0:T(8,128)(2,1)S(1)}, u32[]{:S(2)}, u32[]{:S(2)}) collective-permute-start(bf16[1,4,96,768]{3,2,1,0:T(8,128)(2,1)S(1)} %maximum_bitcast_fusion.1), channel_id=1, source_target_pairs={{0,1},{1,0},{2,3},{3,2},{4,6},{5,7},{6,4},{7,5},{8,9},{9,8},{10,11... | collective-permute-start | bytes 1769480 | tf_op jit(solution)/shard_map/ppermute | solution.py:99
  62.2 21.1 %collective-permute-start.17 = (bf16[1,4,192,384]{3,2,1,0:T(8,128)(2,1)S(1)}, bf16[1,4,192,384]{3,2,1,0:T(8,128)(2,1)S(1)}, u32[]{:S(2)}, u32[]{:S(2)}) collective-permute-start(bf16[1,4,192,384]{3,2,1,0:T(8,128)(2,1)S(1)} %maximum_bitcast_fusion.2), channel_id=1, source_target_pairs={{0,1},{1,0},{2,3},{3,2},{4,6},{5,7},{6,4},{7,5},{8,9},{9,8},{10,11... | collective-permute-start | bytes 1769480 | tf_op jit(solution)/shard_map/ppermute | solution.py:99
  63.8 37.3 %collective-permute-start.5 = (bf16[2,4,112,768]{3,2,1,0:T(8,128)(2,1)S(1)}, bf16[2,4,112,768]{3,2,1,0:T(8,128)(2,1)}, u32[]{:S(2)}, u32[]{:S(2)}) collective-permute-start(bf16[2,4,112,768]{3,2,1,0:T(8,128)(2,1)S(1)} %pad_maximum_fusion.own_low), channel_id=1, source_target_pairs={{0,4},{4,0},{8,12},{12,8},{16,20},{20,16},{24,28},{28,24},{1,5},{5... | collective-permute-start | bytes 4128776 | tf_op jit(solution)/shard_map/ppermute | solution.py:103
  63.8 37.7 %collective-permute-start.6 = (bf16[2,4,112,768]{3,2,1,0:T(8,128)(2,1)}, bf16[2,4,112,768]{3,2,1,0:T(8,128)(2,1)}, u32[]{:S(2)}, u32[]{:S(2)}) collective-permute-start(bf16[2,4,112,768]{3,2,1,0:T(8,128)(2,1)} %collective-permute-done.4.own_high), channel_id=1, source_target_pairs={{0,4},{4,0},{8,12},{12,8},{16,20},{20,16},{24,28},{28,24},{1,5},{5... | collective-permute-start | bytes 4128776 | tf_op jit(solution)/shard_map/ppermute | solution.py:103
  71.8 16.5 %collective-permute-start.11 = (bf16[2,4,96,768]{3,2,1,0:T(8,128)(2,1)}, bf16[2,4,96,768]{3,2,1,0:T(8,128)(2,1)}, u32[]{:S(2)}, u32[]{:S(2)}) collective-permute-start(bf16[2,4,96,768]{3,2,1,0:T(8,128)(2,1)} %pad_maximum_fusion.1.u0), channel_id=1, source_target_pairs={{0,2},{1,3},{2,0},{3,1},{4,5},{5,4},{6,7},{7,6},{8,10},{9,11},{10,... | collective-permute-start | bytes 3538952 | tf_op jit(solution)/shard_map/ppermute | solution.py:99
  84.5 16.5 %collective-permute-start.18 = (bf16[2,4,192,384]{3,2,1,0:T(8,128)(2,1)}, bf16[2,4,192,384]{3,2,1,0:T(8,128)(2,1)}, u32[]{:S(2)}, u32[]{:S(2)}) collective-permute-start(bf16[2,4,192,384]{3,2,1,0:T(8,128)(2,1)} %pad_maximum_fusion.2.d0), channel_id=1, source_target_pairs={{0,2},{1,3},{2,0},{3,1},{4,5},{5,4},{6,7},{7,6},{8,10},{9,11},{10,... | collective-permute-start | bytes 3538952 | tf_op jit(solution)/shard_map/ppermute | solution.py:99
  87.6 49.9 %collective-permute-start.12 = (bf16[2,4,96,768]{3,2,1,0:T(8,128)(2,1)}, bf16[2,4,96,768]{3,2,1,0:T(8,128)(2,1)}, u32[]{:S(2)}, u32[]{:S(2)}) collective-permute-start(bf16[2,4,96,768]{3,2,1,0:T(8,128)(2,1)} %pad_maximum_fusion.1.u0), channel_id=1, source_target_pairs={{0,4},{4,0},{8,12},{12,8},{16,20},{20,16},{24,28},{28,24},{1,5},{5... | collective-permute-start | bytes 3538952 | tf_op jit(solution)/shard_map/ppermute | solution.py:103
  88.3 75.5 %collective-permute-start.19 = (bf16[2,4,192,384]{3,2,1,0:T(8,128)(2,1)}, bf16[2,4,192,384]{3,2,1,0:T(8,128)(2,1)S(1)}, u32[]{:S(2)}, u32[]{:S(2)}) collective-permute-start(bf16[2,4,192,384]{3,2,1,0:T(8,128)(2,1)} %pad_maximum_fusion.2.d0), channel_id=1, source_target_pairs={{0,4},{4,0},{8,12},{12,8},{16,20},{20,16},{24,28},{28,24},{1,5},{5... | collective-permute-start | bytes 3538952 | tf_op jit(solution)/shard_map/ppermute | solution.py:103
  101.0 36.6 %collective-permute-start.13 = (bf16[2,4,96,768]{3,2,1,0:T(8,128)(2,1)}, bf16[2,4,96,768]{3,2,1,0:T(8,128)(2,1)}, u32[]{:S(2)}, u32[]{:S(2)}) collective-permute-start(bf16[2,4,96,768]{3,2,1,0:T(8,128)(2,1)} %collective-permute-done.11.u1), channel_id=1, source_target_pairs={{0,4},{4,0},{8,12},{12,8},{16,20},{20,16},{24,28},{28,24},{1,5},{5... | collective-permute-start | bytes 3538952 | tf_op jit(solution)/shard_map/ppermute | solution.py:103
  101.1 62.7 %collective-permute-start.20 = (bf16[2,4,192,384]{3,2,1,0:T(8,128)(2,1)}, bf16[2,4,192,384]{3,2,1,0:T(8,128)(2,1)S(1)}, u32[]{:S(2)}, u32[]{:S(2)}) collective-permute-start(bf16[2,4,192,384]{3,2,1,0:T(8,128)(2,1)} %collective-permute-done.18.d1), channel_id=1, source_target_pairs={{0,4},{4,0},{8,12},{12,8},{16,20},{20,16},{24,28},{28,24},{1,5},{5... | collective-permute-start | bytes 3538952 | tf_op jit(solution)/shard_map/ppermute | solution.py:103
  165.2 31.9 %copy-start.5 = (bf16[1024,768]{1,0:T(8,128)(2,1)S(1)}, bf16[1024,768]{1,0:T(8,128)(2,1)}, u32[]{:S(2)}) copy-start(bf16[1024,768]{1,0:T(8,128)(2,1)} %get-tuple-element.75) | copy-start | bytes 4718596
  196.9 91.6 %collective-permute-start.33 = (bf16[4,4,192,384]{3,2,1,0:T(8,128)(2,1)}, bf16[4,4,192,384]{3,2,1,0:T(8,128)(2,1)}, u32[]{:S(2)}, u32[]{:S(2)}) collective-permute-start(bf16[4,4,192,384]{3,2,1,0:T(8,128)(2,1)} %get-tuple-element.101), channel_id=1, source_target_pairs={{0,4},{4,0},{8,12},{12,8},{16,20},{20,16},{24,28},{28,24},{1,5},{5... | collective-permute-start | bytes 7077896 | tf_op jit(solution)/shard_map/ppermute | solution.py:112
  239.4 38.0 %copy-start.8 = (f32[1,768]{1,0:T(1,128)S(1)}, f32[1,768]{1,0:T(1,128)}, u32[]{:S(2)}) copy-start(f32[1,768]{1,0:T(1,128)} %get-tuple-element.92) | copy-start | bytes 9220
  239.4 38.0 %copy-start.9 = (f32[1,768]{1,0:T(1,128)S(1)}, f32[1,768]{1,0:T(1,128)}, u32[]{:S(2)}) copy-start(f32[1,768]{1,0:T(1,128)} %get-tuple-element.93) | copy-start | bytes 9220
  239.4 38.0 %copy-start.10 = (f32[1,768]{1,0:T(1,128)S(1)}, f32[1,768]{1,0:T(1,128)}, u32[]{:S(2)}) copy-start(f32[1,768]{1,0:T(1,128)} %get-tuple-element.94) | copy-start | bytes 9220
  239.4 38.0 %copy-start.11 = (f32[1,768]{1,0:T(1,128)S(1)}, f32[1,768]{1,0:T(1,128)}, u32[]{:S(2)}) copy-start(f32[1,768]{1,0:T(1,128)} %get-tuple-element.90) | copy-start | bytes 9220
  239.4 38.0 %copy-start.12 = (f32[1,768]{1,0:T(1,128)S(1)}, f32[1,768]{1,0:T(1,128)}, u32[]{:S(2)}) copy-start(f32[1,768]{1,0:T(1,128)} %get-tuple-element.91) | copy-start | bytes 9220
  239.4 38.0 %copy-start.13 = (f32[1,768]{1,0:T(1,128)S(1)}, f32[1,768]{1,0:T(1,128)}, u32[]{:S(2)}) copy-start(f32[1,768]{1,0:T(1,128)} %get-tuple-element.89) | copy-start | bytes 9220
  288.0 9.7 %collective-permute-start.21 = (bf16[4,4,112,768]{3,2,1,0:T(8,128)(2,1)}, bf16[4,4,112,768]{3,2,1,0:T(8,128)(2,1)S(1)}, u32[]{:S(2)}, u32[]{:S(2)}) collective-permute-start(bf16[4,4,112,768]{3,2,1,0:T(8,128)(2,1)} %get-tuple-element.97), channel_id=1, source_target_pairs={{0,4},{4,0},{8,12},{12,8},{16,20},{20,16},{24,28},{28,24},{1,5},{5... | collective-permute-start | bytes 8257544 | tf_op jit(solution)/shard_map/ppermute | solution.py:112
  288.4 8.3 %collective-permute-start.27 = (bf16[4,4,96,768]{3,2,1,0:T(8,128)(2,1)}, bf16[4,4,96,768]{3,2,1,0:T(8,128)(2,1)S(1)}, u32[]{:S(2)}, u32[]{:S(2)}) collective-permute-start(bf16[4,4,96,768]{3,2,1,0:T(8,128)(2,1)} %get-tuple-element.99), channel_id=1, source_target_pairs={{0,4},{4,0},{8,12},{12,8},{16,20},{20,16},{24,28},{28,24},{1,5},{5... | collective-permute-start | bytes 7077896 | tf_op jit(solution)/shard_map/ppermute | solution.py:112
  291.0 16.3 %collective-permute-start.34 = (bf16[2,4,192,384]{3,2,1,0:T(8,128)(2,1)S(1)}, bf16[2,4,192,384]{3,2,1,0:T(8,128)(2,1)S(1)}, u32[]{:S(2)}, u32[]{:S(2)}) collective-permute-start(bf16[2,4,192,384]{3,2,1,0:T(8,128)(2,1)S(1)} %get-tuple-element.105), channel_id=1, source_target_pairs={{0,2},{1,3},{2,0},{3,1},{4,5},{5,4},{6,7},{7,6},{8,10},{9,11},{10,... | collective-permute-start | bytes 3538952 | tf_op jit(solution)/shard_map/ppermute | solution.py:117
  297.4 28.8 %collective-permute-start.28 = (bf16[2,4,96,768]{3,2,1,0:T(8,128)(2,1)S(1)}, bf16[2,4,96,768]{3,2,1,0:T(8,128)(2,1)S(1)}, u32[]{:S(2)}, u32[]{:S(2)}) collective-permute-start(bf16[2,4,96,768]{3,2,1,0:T(8,128)(2,1)S(1)} %get-tuple-element.107), channel_id=1, source_target_pairs={{0,2},{1,3},{2,0},{3,1},{4,5},{5,4},{6,7},{7,6},{8,10},{9,11},{10,... | collective-permute-start | bytes 3538952 | tf_op jit(solution)/shard_map/ppermute | solution.py:117
  299.3 48.0 %collective-permute-start.22 = (bf16[2,4,112,768]{3,2,1,0:T(8,128)(2,1)S(1)}, bf16[2,4,112,768]{3,2,1,0:T(8,128)(2,1)S(1)}, u32[]{:S(2)}, u32[]{:S(2)}) collective-permute-start(bf16[2,4,112,768]{3,2,1,0:T(8,128)(2,1)S(1)} %get-tuple-element.103), channel_id=1, source_target_pairs={{0,2},{1,3},{2,0},{3,1},{4,5},{5,4},{6,7},{7,6},{8,10},{9,11},{10,... | collective-permute-start | bytes 4128776 | tf_op jit(solution)/shard_map/ppermute | solution.py:117
  307.6 42.5 %collective-permute-start.35 = (bf16[1,4,192,384]{3,2,1,0:T(8,128)(2,1)S(1)}, bf16[1,4,192,384]{3,2,1,0:T(8,128)(2,1)S(1)}, u32[]{:S(2)}, u32[]{:S(2)}) collective-permute-start(bf16[1,4,192,384]{3,2,1,0:T(8,128)(2,1)S(1)} %get-tuple-element.111), channel_id=1, source_target_pairs={{0,1},{1,0},{2,3},{3,2},{4,6},{5,7},{6,4},{7,5},{8,9},{9,8},{10,11... | collective-permute-start | bytes 1769480 | tf_op jit(solution)/shard_map/ppermute | solution.py:117
  326.5 25.8 %collective-permute-start.29 = (bf16[1,4,96,768]{3,2,1,0:T(8,128)(2,1)S(1)}, bf16[1,4,96,768]{3,2,1,0:T(8,128)(2,1)S(1)}, u32[]{:S(2)}, u32[]{:S(2)}) collective-permute-start(bf16[1,4,96,768]{3,2,1,0:T(8,128)(2,1)S(1)} %get-tuple-element.113), channel_id=1, source_target_pairs={{0,1},{1,0},{2,3},{3,2},{4,6},{5,7},{6,4},{7,5},{8,9},{9,8},{10,11... | collective-permute-start | bytes 1769480 | tf_op jit(solution)/shard_map/ppermute | solution.py:117
  347.7 19.4 %collective-permute-start.23 = (bf16[1,4,112,768]{3,2,1,0:T(8,128)(2,1)S(1)}, bf16[1,4,112,768]{3,2,1,0:T(8,128)(2,1)S(1)}, u32[]{:S(2)}, u32[]{:S(2)}) collective-permute-start(bf16[1,4,112,768]{3,2,1,0:T(8,128)(2,1)S(1)} %get-tuple-element.109), channel_id=1, source_target_pairs={{0,1},{1,0},{2,3},{3,2},{4,6},{5,7},{6,4},{7,5},{8,9},{9,8},{10,11... | collective-permute-start | bytes 2064392 | tf_op jit(solution)/shard_map/ppermute | solution.py:117
  350.3 8.4 %collective-permute-start.36 = (bf16[192,384]{1,0:T(8,128)(2,1)S(1)}, bf16[192,384]{1,0:T(8,128)(2,1)S(1)}, u32[]{:S(2)}, u32[]{:S(2)}) collective-permute-start(bf16[192,384]{1,0:T(8,128)(2,1)S(1)} %get-tuple-element.117), channel_id=1, source_target_pairs={{0,24},{4,28},{8,0},{12,4},{16,8},{20,12},{24,16},{28,20},{1,25},{... | collective-permute-start | bytes 442376 | tf_op jit(solution)/shard_map/ppermute | solution.py:121
  350.3 15.9 %collective-permute-start.37 = (bf16[192,384]{1,0:T(8,128)(2,1)S(1)}, bf16[192,384]{1,0:T(8,128)(2,1)S(1)}, u32[]{:S(2)}, u32[]{:S(2)}) collective-permute-start(bf16[192,384]{1,0:T(8,128)(2,1)S(1)} %get-tuple-element.119), channel_id=1, source_target_pairs={{0,16},{4,20},{8,24},{12,28},{16,0},{20,4},{24,8},{28,12},{1,17},{... | collective-permute-start | bytes 442376 | tf_op jit(solution)/shard_map/ppermute | solution.py:121
  350.4 15.8 %collective-permute-start.38 = (bf16[192,384]{1,0:T(8,128)(2,1)S(1)}, bf16[192,384]{1,0:T(8,128)(2,1)S(1)}, u32[]{:S(2)}, u32[]{:S(2)}) collective-permute-start(bf16[192,384]{1,0:T(8,128)(2,1)S(1)} %get-tuple-element.118), channel_id=1, source_target_pairs={{0,8},{4,12},{8,16},{12,20},{16,24},{20,28},{24,0},{28,4},{1,9},{5... | collective-permute-start | bytes 442376 | tf_op jit(solution)/shard_map/ppermute | solution.py:121
  352.5 19.6 %collective-permute-start.30 = (bf16[96,768]{1,0:T(8,128)(2,1)S(1)}, bf16[96,768]{1,0:T(8,128)(2,1)S(1)}, u32[]{:S(2)}, u32[]{:S(2)}) collective-permute-start(bf16[96,768]{1,0:T(8,128)(2,1)S(1)} %get-tuple-element.120), channel_id=1, source_target_pairs={{0,24},{4,28},{8,0},{12,4},{16,8},{20,12},{24,16},{28,20},{1,25},{... | collective-permute-start | bytes 442376 | tf_op jit(solution)/shard_map/ppermute | solution.py:121
  358.7 17.1 %collective-permute-start.31 = (bf16[96,768]{1,0:T(8,128)(2,1)S(1)}, bf16[96,768]{1,0:T(8,128)(2,1)S(1)}, u32[]{:S(2)}, u32[]{:S(2)}) collective-permute-start(bf16[96,768]{1,0:T(8,128)(2,1)S(1)} %get-tuple-element.122), channel_id=1, source_target_pairs={{0,16},{4,20},{8,24},{12,28},{16,0},{20,4},{24,8},{28,12},{1,17},{... | collective-permute-start | bytes 442376 | tf_op jit(solution)/shard_map/ppermute | solution.py:121
  366.2 9.5 %collective-permute-start.32 = (bf16[96,768]{1,0:T(8,128)(2,1)S(1)}, bf16[96,768]{1,0:T(8,128)(2,1)S(1)}, u32[]{:S(2)}, u32[]{:S(2)}) collective-permute-start(bf16[96,768]{1,0:T(8,128)(2,1)S(1)} %get-tuple-element.121), channel_id=1, source_target_pairs={{0,8},{4,12},{8,16},{12,20},{16,24},{20,28},{24,0},{28,4},{1,9},{5... | collective-permute-start | bytes 442376 | tf_op jit(solution)/shard_map/ppermute | solution.py:121
  367.2 11.1 %collective-permute-start.24 = (bf16[112,768]{1,0:T(8,128)(2,1)S(1)}, bf16[112,768]{1,0:T(8,128)(2,1)S(1)}, u32[]{:S(2)}, u32[]{:S(2)}) collective-permute-start(bf16[112,768]{1,0:T(8,128)(2,1)S(1)} %get-tuple-element.114), channel_id=1, source_target_pairs={{0,24},{4,28},{8,0},{12,4},{16,8},{20,12},{24,16},{28,20},{1,25},{... | collective-permute-start | bytes 516104 | tf_op jit(solution)/shard_map/ppermute | solution.py:121
  371.1 18.4 %collective-permute-start.25 = (bf16[112,768]{1,0:T(8,128)(2,1)S(1)}, bf16[112,768]{1,0:T(8,128)(2,1)S(1)}, u32[]{:S(2)}, u32[]{:S(2)}) collective-permute-start(bf16[112,768]{1,0:T(8,128)(2,1)S(1)} %get-tuple-element.116), channel_id=1, source_target_pairs={{0,16},{4,20},{8,24},{12,28},{16,0},{20,4},{24,8},{28,12},{1,17},{... | collective-permute-start | bytes 516104 | tf_op jit(solution)/shard_map/ppermute | solution.py:121
  372.1 17.5 %collective-permute-start.26 = (bf16[112,768]{1,0:T(8,128)(2,1)S(1)}, bf16[112,768]{1,0:T(8,128)(2,1)S(1)}, u32[]{:S(2)}, u32[]{:S(2)}) collective-permute-start(bf16[112,768]{1,0:T(8,128)(2,1)S(1)} %get-tuple-element.115), channel_id=1, source_target_pairs={{0,8},{4,12},{8,16},{12,20},{16,24},{20,28},{24,0},{28,4},{1,9},{5... | collective-permute-start | bytes 516104 | tf_op jit(solution)/shard_map/ppermute | solution.py:121
  (7 other events, 48.1 us)

commit v3 on v2

--- a/solution.py
+++ b/solution.py
@@ -91,35 +91,88 @@
     return pairs
 
 
-def gather_blocks(block):
-    _, _, depth, bits = axis_facts()
-    parts = [block] + [lax.ppermute(block, "dp", along_z(s)) for s in range(1, depth)]
-    held = jnp.stack(parts)[None]
-    for r in range(bits):
-        got = lax.ppermute(held, ("dp", "fsdp"), along_bit(r))
-        if r < bits - 1:
-            held = jnp.concatenate([held, got])
-    own = [held, got]
-    return own + [lax.ppermute(v, "dp", across_cores()) for v in own]
+class Gather:
+    def __init__(self, block):
+        self.block, self.round, self.blocks = block, -1, None
+
+    def stage(self):
+        _, _, depth, bits = axis_facts()
+        if self.round < 0:
+            return [(self.block, "dp", along_z(s)) for s in range(1, depth)]
+        if self.round < bits:
+            return [(self.held, ("dp", "fsdp"), along_bit(self.round))]
+        return [(v, "dp", across_cores()) for v in self.own]
+
+    def take(self, got):
+        bits = axis_facts()[3]
+        if self.round < 0:
+            self.held = jnp.stack([self.block] + got)[None]
+        elif self.round < bits - 1:
+            self.held = jnp.concatenate([self.held] + got)
+        elif self.round < bits:
+            self.own = [self.held] + got
+        else:
+            self.blocks = self.own + got
+        self.round += 1
+
+    def done(self):
+        return self.blocks is not None
 
 
 def add(left, right):
     return (left.astype(f32) + right.astype(f32)).astype(bf16)
 
 
-def scatter_blocks(keep, send):
-    _, _, depth, bits = axis_facts()
-    got = lax.ppermute(send, "dp", across_cores())
-    for r in reversed(range(bits)):
-        half = keep.shape[0] // 2
-        upper = add(keep[half:], got[half:])
-        keep = add(keep[:half], got[:half])
-        got = lax.ppermute(upper, ("dp", "fsdp"), along_bit(r))
-    mine = [add(keep[0, s], got[0, s]) for s in range(1, depth)]
-    total = keep[0, 0].astype(f32) + got[0, 0].astype(f32)
-    for s in range(1, depth):
-        total = total + lax.ppermute(mine[s - 1], "dp", along_z(-s)).astype(f32)
-    return total
+class Scatter:
+    def __init__(self, keep, send):
+        self.keep, self.send, self.round, self.total = keep, [send], axis_facts()[3], None
+
+    def stage(self):
+        _, _, depth, bits = axis_facts()
+        if self.round == bits:
+            return [(self.send[0], "dp", across_cores())]
+        if self.round >= 0:
+            return [(self.send[0], ("dp", "fsdp"), along_bit(self.round))]
+        return [(self.send[s - 1], "dp", along_z(-s)) for s in range(1, depth)]
+
+    def take(self, got):
+        depth = axis_facts()[2]
+        keep = self.keep
+        if self.round > 0:
+            half = keep.shape[0] // 2
+            self.send = [add(keep[half:], got[0][half:])]
+            self.keep = add(keep[:half], got[0][:half])
+        elif self.round == 0:
+            self.send = [add(keep[0, s], got[0][0, s]) for s in range(1, depth)]
+            self.keep = keep[0, 0].astype(f32) + got[0][0, 0].astype(f32)
+        else:
+            for part in got:
+                keep = keep + part.astype(f32)
+            self.total = keep
+        self.round -= 1
+
+    def done(self):
+        return self.total is not None
+
+
+def beside(moves, compute=None, args=()):
+    moves = [move for move in moves if not move.done()]
+    stages = [move.stage() for move in moves]
+    args, arrays = lax.optimization_barrier((args, [[v for v, _, _ in stage] for stage in stages]))
+    results = compute(*args) if compute else ()
+    got = [
+        [lax.ppermute(v, axis, perm) for v, (_, axis, perm) in zip(held, stage)]
+        for held, stage in zip(arrays, stages)
+    ]
+    results, got = lax.optimization_barrier((results, got))
+    for move, parts in zip(moves, got):
+        move.take(parts)
+    return results
+
+
+def finish(move):
+    while not move.done():
+        beside([move])
 
 
 def places():
@@ -608,24 +661,23 @@
 
 
 def feed_back_kernel(
-    place, branch, slope, dw, uw, low_t, mixed, n1, r1, g1, context, ow,
-    send, keep, gub, inner_out, gg1, gb1, gob, gow, grad_context, delta_out,
-    hidden, grad_normed, attended, found,
+    place, branch, slope, dw, uw, low_t, mixed,
+    send, keep, gub, grad_normed,
+    hidden, found,
 ):
     j = pl.program_id(0)
     _, depth, tall, _ = send.shape
     each, t, narrow = slope.shape
-    d = branch.shape[1]
     tiles = t // ROWS
 
     def gelu_rows(r, sums):
         rows = pl.ds(pl.multiple_of(r * ROWS, ROWS), ROWS)
-        found = []
+        sums_now = []
         for c in range(each):
             grad = (slope[c, rows, :].astype(f32) * dot(branch[rows, :], dw[c])).astype(bf16)
             hidden[rows, c * narrow:(c + 1) * narrow] = grad
-            found.append(sums[c] + jnp.sum(grad.astype(f32), axis=0, keepdims=True))
-        return tuple(found)
+            sums_now.append(sums[c] + jnp.sum(grad.astype(f32), axis=0, keepdims=True))
+        return tuple(sums_now)
 
     sums = lax.fori_loop(0, tiles, gelu_rows, (jnp.zeros((1, narrow), f32),) * each)
     for c in range(each):
@@ -647,57 +699,79 @@
 
     lax.fori_loop(0, tiles, normed_rows, 0)
 
-    @pl.when(j == pl.num_programs(0) - 1)
-    def _():
-        feature = lax.broadcasted_iota(jnp.int32, (128, d), 1)
-        slot = lax.broadcasted_iota(jnp.int32, (128, d), 0)
-        head = jnp.where(slot < HD, 2 * slot, 2 * (slot - HD) + 1)
-        pick = jnp.where(feature // HD == head, 1.0, 0.0).astype(bf16)
-
-        def inner_rows(r, sums):
-            rows = pl.ds(pl.multiple_of(r * ROWS, ROWS), ROWS)
-            dy, n = grad_normed[rows, :], n1[rows, :]
-            inner = norm_back(dy, n, r1[rows, :1], g1[...])
-            inner_out[rows, :] = inner
-            low = inner.astype(bf16)
-            attended[rows, :] = low
-            grad_ctx = dot_nt(low, ow[0]).astype(bf16)
-            grad_context[rows, :] = grad_ctx
-            both = grad_ctx.astype(f32) * context[rows, :].astype(f32)
-            high = both.astype(bf16)
-            rest = (both - high.astype(f32)).astype(bf16)
-            delta_out[:, rows] = dot_nt(pick, high) + dot_nt(pick, rest)
-            return (
-                sums[0] + jnp.sum(dy * n, axis=0, keepdims=True),
-                sums[1] + jnp.sum(dy, axis=0, keepdims=True),
-                sums[2] + jnp.sum(low.astype(f32), axis=0, keepdims=True),
-            )
-
-        gg1[...], gb1[...], gob[...] = lax.fori_loop(0, tiles, inner_rows, (jnp.zeros((1, d), f32),) * 3)
-        gow[...] = dot_tn(context[...], attended[...]).astype(bf16)
-
-
-def feed_back(place, branch, slope, dw, uw, low_t, mixed, n1, r1, g1, context, weights):
+
+def feed_back(place, branch, slope, dw, uw, low_t, mixed):
     parts, t, narrow = slope.shape
     f, d, wide = uw.shape
     each, depth, tall = parts // f, parts // 2, d // parts
     made = lambda n: pl.BlockSpec(
         (1, depth, tall, wide), lambda j, place: (slot_of(place, n, j, depth, f), 0, 0, 0)
     )
-    vector = whole((1, d))
     return call(
         feed_back_kernel, "feed_back", (f,),
         [whole((t, d)), pl.BlockSpec((each, t, narrow), lambda j, *_: (j, 0, 0)),
          pl.BlockSpec((each, d, narrow), lambda j, *_: (j, 0, 0)), pl.BlockSpec((1, d, wide), lambda j, *_: (j, 0, 0)),
-         whole((d, t)), whole((t, d)), whole((t, d)), whole((t, 128)), vector, whole((t, d)),
-         pl.BlockSpec((1, d, d), lambda j, *_: (3, 0, 0))],
-        [made(1), made(0), pl.BlockSpec((1, 1, wide), lambda j, *_: (j, 0, 0)),
-         whole((t, d)), vector, vector, vector, whole((d, d)), whole((t, d)), whole((128, t))],
-        [sds((f, depth, tall, wide), bf16)] * 2 + [sds((f, 1, wide), f32), sds((t, d), f32)] + [sds((1, d), f32)] * 3
+         whole((d, t)), whole((t, d))],
+        [made(1), made(0), pl.BlockSpec((1, 1, wide), lambda j, *_: (j, 0, 0)), whole((t, d))],
+        [sds((f, depth, tall, wide), bf16)] * 2 + [sds((f, 1, wide), f32), sds((t, d), f32)],
+        [pltpu.VMEM((t, wide), bf16), pltpu.VMEM((d, wide), bf16)],
+        prefetch=1, cost=guess(15e9, 35e6),
+    )(place, branch, slope, dw, uw, low_t, mixed)
+
+
+def inner_kernel(
+    grad_normed, n1, r1, g1, context, ow,
+    inner_out, gg1, gb1, gob, gow, grad_context, delta_out,
+    weight_grad,
+):
+    step = pl.program_id(0)
+    d = n1.shape[1]
+
+    @pl.when(step == 0)
+    def _():
+        weight_grad[...] = jnp.zeros_like(weight_grad)
+        gg1[...] = jnp.zeros_like(gg1)
+        gb1[...] = jnp.zeros_like(gb1)
+        gob[...] = jnp.zeros_like(gob)
+
+    feature = lax.broadcasted_iota(jnp.int32, (128, d), 1)
+    slot = lax.broadcasted_iota(jnp.int32, (128, d), 0)
+    head = jnp.where(slot < HD, 2 * slot, 2 * (slot - HD) + 1)
+    pick = jnp.where(feature // HD == head, 1.0, 0.0).astype(bf16)
+    dy, n = grad_normed[...], n1[...]
+    inner = norm_back(dy, n, r1[:, :1], g1[...])
+    inner_out[...] = inner
+    low = inner.astype(bf16)
+    grad_ctx = dot_nt(low, ow[0]).astype(bf16)
+    grad_context[...] = grad_ctx
+    both = grad_ctx.astype(f32) * context[...].astype(f32)
+    high = both.astype(bf16)
+    rest = (both - high.astype(f32)).astype(bf16)
+    delta_out[...] = dot_nt(pick, high) + dot_nt(pick, rest)
+    gg1[...] += jnp.sum(dy * n, axis=0, keepdims=True)
+    gb1[...] += jnp.sum(dy, axis=0, keepdims=True)
+    gob[...] += jnp.sum(low.astype(f32), axis=0, keepdims=True)
+    weight_grad[...] += dot_tn(context[...], low)
+
+    @pl.when(step == pl.num_programs(0) - 1)
+    def _():
+        gow[...] = weight_grad[...].astype(bf16)
+
+
+def inner_back(grad_normed, n1, r1, g1, context, weights):
+    t, d = n1.shape
+    rows = pl.BlockSpec((ROWS, d), lambda r: (r, 0))
+    vector = whole((1, d))
+    return call(
+        inner_kernel, "inner_back", (t // ROWS,),
+        [rows, rows, pl.BlockSpec((ROWS, 128), lambda r: (r, 0)), vector, rows,
+         pl.BlockSpec((1, d, d), lambda r: (3, 0, 0))],
+        [rows, vector, vector, vector, whole((d, d)), rows, pl.BlockSpec((128, ROWS), lambda r: (0, r))],
+        [sds((t, d), f32)] + [sds((1, d), f32)] * 3
         + [sds((d, d), bf16), sds((t, d), bf16), sds((128, t), f32)],
-        [pltpu.VMEM((t, wide), bf16), pltpu.VMEM((t, d), f32), pltpu.VMEM((t, d), bf16), pltpu.VMEM((d, wide), bf16)],
-        prefetch=1, cost=guess(18e9, 45e6),
-    )(place, branch, slope, dw, uw, low_t, mixed, n1, r1, g1, context, weights)
+        [pltpu.VMEM((d, d), f32)],
+        cost=guess(4e9, 20e6),
+    )(grad_normed, n1, r1, g1, context, weights)
 
 
 def shards(
@@ -718,33 +792,46 @@
         up_bias[None],
         spare,
     ])
-    attention_blocks = gather_blocks(block)
-    up_blocks = gather_blocks(up_weight)
-    down_blocks = gather_blocks(down_weight.T)
-
-    weights, vectors, ub = assemble(place, attention_blocks)
+    to_a, to_u, to_d = Gather(block), Gather(up_weight), Gather(down_weight.T)
+    beside([to_a])
+    beside([to_a, to_u])
+    while to_a.round < axis_facts()[3]:
+        beside([to_a, to_d] if to_d.round < 0 else [to_a])
+    beside([to_a, to_u])
+    weights, vectors, ub = beside([to_u], assemble, (place, to_a.blocks))
     qb, vb, ob, g1 = (vectors[m, 0:1] for m in range(4))
     b1, db, g2, b2 = (vectors[m, 1:2] for m in range(4))
     ub = ub[:, 2]
 
-    q, k, v, context, lse = attend(bucket, lengths, tokens, weights, qb, vb)
-    n1, r1, low, active, slope, uw = up(place, tokens, context, weights, ob, g1, b1, ub, up_blocks)
+    q, k, v, context, lse = beside([to_u, to_d], attend, (bucket, lengths, tokens, weights, qb, vb))
+    finish(to_u)
+    n1, r1, low, active, slope, uw = beside(
+        [to_d], up, (place, tokens, context, weights, ob, g1, b1, ub, to_u.blocks)
+    )
+    finish(to_d)
     out, pooled, mixed, branch, gdb, gg2, gb2, send_d, keep_d, dw = down(
-        place, bucket, lengths, active, n1, g1, b1, db, g2, b2, cotangent, down_blocks
-    )
-    made_d = scatter_blocks(keep_d, send_d)
-    send_u, keep_u, gub, inner, gg1, gb1, gob, gow, grad_context, delta = feed_back(
-        place, branch, slope, dw, uw, low.T, mixed, n1, r1, g1, context, weights
-    )
-    made_u = scatter_blocks(keep_u, send_u)
-    gqw, gkw, gvw, gqb, gvb, input_grad = attend_back(
-        bucket, lengths, tokens.T, q, k, v, grad_context, lse, delta, weights, inner
+        place, bucket, lengths, active, n1, g1, b1, db, g2, b2, cotangent, to_d.blocks
+    )
+    of_d = Scatter(keep_d, send_d)
+    send_u, keep_u, gub, grad_normed = beside(
+        [of_d], feed_back, (place, branch, slope, dw, uw, low.T, mixed)
+    )
+    of_u = Scatter(keep_u, send_u)
+    inner, gg1, gb1, gob, gow, grad_context, delta = beside(
+        [of_d, of_u], inner_back, (grad_normed, n1, r1, g1, context, weights)
+    )
+    gqw, gkw, gvw, gqb, gvb, input_grad = beside(
+        [of_d, of_u], attend_back,
+        (bucket, lengths, tokens.T, q, k, v, grad_context, lse, delta, weights, inner),
     )
     firsts = jnp.stack([gqb, gvb, gob, gg1])
     seconds = jnp.stack([gb1, gdb, gg2, gb2])
     vectors = jnp.concatenate([firsts, seconds, jnp.zeros((4, 14, d), f32)], axis=1)
-    send_a, keep_a = pack(place, (gqw, gkw, gvw, gow), vectors, gub)
-    made_a = scatter_blocks(keep_a, send_a)
+    send_a, keep_a = beside([of_d, of_u], pack, (place, (gqw, gkw, gvw, gow), vectors, gub))
+    of_a = Scatter(keep_a, send_a)
+    while not (of_a.done() and of_u.done() and of_d.done()):
+        beside([of_a, of_u, of_d])
+    made_a, made_u, made_d = of_a.total, of_u.total, of_d.total
 
     tall, narrow = d // dp, d // fsdp
     made = [made_a[:tall, m * narrow:(m + 1) * narrow] for m in range(4)]

time: 393 us -> 367 us (0.934)
  waiting for transfers between devices: 129 us -> 99.9 us
  starting transfers between devices: 56.2 us -> 46.4 us
  other arithmetic: 13.8 us -> 23.3 us
    ppermute x39, waiting for transfers between devices: 129 us -> 99.9 us  [beside(): lax.ppermute(v, axis, perm)]
    pallas_call x0 -> x1, Pallas kernels: none -> 10.7 us  [inner_back(): call(inner_kernel, 'inner_back', (t // ROWS,), [rows, rows, pl.BlockSpec(...]
    ppermute x39, starting transfers between devices: 56.2 us -> 46.4 us  [beside(): lax.ppermute(v, axis, perm)]
    pallas_call x1, Pallas kernels: 40.7 us -> 31.1 us  [feed_back(): call(feed_back_kernel, 'feed_back', (f,), [whole((t, d)), pl.BlockSpec((e...]
    convert_element_type x9, other arithmetic: 5.37 us -> 14.6 us  [add(): return (left.astype(f32) + right.astype(f32)).astype(bf16)]
  transfers between devices with their start and end apart: 39 -> 39, of which waited for: 19 -> 19; matrix products, arithmetic and copies ran while one was open for 5% -> 3% of each run, Pallas kernels for 37% -> 40%
where the time goes in v3:
time: 367 us; the launch traced here: 366 us
  Pallas kernels  179 us (49%)
  waiting for transfers between devices  99.9 us (27%)
  starting transfers between devices  46.4 us (13%)
  other arithmetic  23.3 us (6%)
  local copies, waits for them, and re-layouts  15.3 us (4%)
    ppermute x39, waiting for transfers between devices, beside(): lax.ppermute(v, axis, perm)  99.9 us
    ppermute x39, starting transfers between devices, beside(): lax.ppermute(v, axis, perm)  46.4 us
    pallas_call x1, Pallas kernels, attend_back(): call(attend_back_kernel, 'attend_back', (pairs,), [whole((d, t)), tall, t...  37.9 us
    pallas_call x1, Pallas kernels, down(): call(down_kernel, 'down', (tiles + parts,), [pl.BlockSpec((parts, ROWS, n...  31.6 us
    pallas_call x1, Pallas kernels, feed_back(): call(feed_back_kernel, 'feed_back', (f,), [whole((t, d)), pl.BlockSpec((e...  31.1 us
    pallas_call x1, Pallas kernels, up(): call(up_kernel, 'up', (t // ROWS,), [rows, rows, pl.BlockSpec((1, d, d),...  26.2 us
    pallas_call x1, Pallas kernels, attend(): call(attend_kernel, 'attend', (pairs,), [whole((t, d)), column(0), column...  24.1 us
    convert_element_type x9, other arithmetic, add(): return (left.astype(f32) + right.astype(f32)).astype(bf16)  14.6 us
  transfers between devices with their start and end apart: 39, of which 19 were waited for; matrix products, arithmetic and copies ran while one was open for 3% of the time, Pallas kernels for 40%

profile of v3, /device:TPU:0, one launch (start us, length us, event | category | flops | bytes accessed | tf_op | source)
XLA Modules:
  0.0 365.9 jit_solution(12287202089273612672)
XLA Ops:
  4.2 3.1 collective-permute-start
  7.3 2.6 collective-permute-start.1
  9.9 1.3 collective-permute-start.2
  11.2 3.4 collective-permute-done
  14.6 6.5 %collective-permute-done.1 = bf16[112,768]{1,0:T(8,128)(2,1)S(1)} collective-permute-done((bf16[112,768]{1,0:T(8,128)(2,1)S(1)}, bf16[112,768]{1,0:T(8,128)(2,1)S(1)}, u32[]{:S(2)}, u32[]{:S(2)}) %collective-permute-start.1) | collective-permute-done | bytes 172064 | tf_op jit(solution)/shard_map/ppermute | solution.py:164
  21.3 1.6 collective-permute-start.3
  22.8 4.2 %collective-permute-start.4 = (bf16[96,768]{1,0:T(8,128)(2,1)S(1)}, bf16[96,768]{1,0:T(8,128)(2,1)S(1)}, u32[]{:S(2)}, u32[]{:S(2)}) collective-permute-start(bf16[96,768]{1,0:T(8,128)(2,1)S(1)} %copy-done.7), channel_id=1, source_target_pairs={{0,8},{4,12},{8,16},{12,20},{16,24},{20,28},{24,0},{28,4},{1,9},{5... | collective-permute-start | bytes 442376 | tf_op jit(solution)/shard_map/ppermute | solution.py:164
  27.0 1.6 collective-permute-start.5
  29.4 3.4 collective-permute-done.4
  32.8 4.8 %collective-permute-done.5 = bf16[96,768]{1,0:T(8,128)(2,1)S(1)} collective-permute-done((bf16[96,768]{1,0:T(8,128)(2,1)S(1)}, bf16[96,768]{1,0:T(8,128)(2,1)S(1)}, u32[]{:S(2)}, u32[]{:S(2)}) %collective-permute-start.5) | collective-permute-done | bytes 147488 | tf_op jit(solution)/shard_map/ppermute | solution.py:164
  38.6 4.7 %collective-permute-start.10 = (bf16[192,384]{1,0:T(8,128)(2,1)S(1)}, bf16[192,384]{1,0:T(8,128)(2,1)S(1)}, u32[]{:S(2)}, u32[]{:S(2)}) collective-permute-start(bf16[192,384]{1,0:T(8,128)(2,1)S(1)} %bitcast.104), channel_id=1, source_target_pairs={{0,24},{4,28},{8,0},{12,4},{16,8},{20,12},{24,16},{28,20},{1,25},{... | collective-permute-start | bytes 442376 | tf_op jit(solution)/shard_map/ppermute | solution.py:164
  44.0 3.6 collective-permute-done.10
  47.6 4.3 %collective-permute-done.8 = bf16[192,384]{1,0:T(8,128)(2,1)S(1)} collective-permute-done((bf16[192,384]{1,0:T(8,128)(2,1)S(1)}, bf16[192,384]{1,0:T(8,128)(2,1)S(1)}, u32[]{:S(2)}, u32[]{:S(2)}) %collective-permute-start.8) | collective-permute-done | bytes 147488 | tf_op jit(solution)/shard_map/ppermute | solution.py:164
  51.9 5.1 %collective-permute-done.9 = bf16[192,384]{1,0:T(8,128)(2,1)S(1)} collective-permute-done((bf16[192,384]{1,0:T(8,128)(2,1)S(1)}, bf16[192,384]{1,0:T(8,128)(2,1)S(1)}, u32[]{:S(2)}, u32[]{:S(2)}) %collective-permute-start.9) | collective-permute-done | bytes 147488 | tf_op jit(solution)/shard_map/ppermute | solution.py:164
  59.1 8.5 %collective-permute-done.13 = bf16[1,4,96,768]{3,2,1,0:T(8,128)(2,1)} collective-permute-done((bf16[1,4,96,768]{3,2,1,0:T(8,128)(2,1)S(1)}, bf16[1,4,96,768]{3,2,1,0:T(8,128)(2,1)}, u32[]{:S(2)}, u32[]{:S(2)}) %collective-permute-start.13) | collective-permute-done | bytes 589856 | tf_op jit(solution)/shard_map/ppermute | solution.py:164
  67.6 2.2 pad_maximum_fusion.1.u0
  71.5 8.7 %assemble.1 = (bf16[4,768,768]{2,1,0:T(8,128)(2,1)}, f32[4,16,768]{2,1,0:T(8,128)}, f32[4,16,768]{2,1,0:T(8,128)}) custom-call(s32[24]{0:T(128)} %concatenate.27.place, bf16[2,4,112,768]{3,2,1,0:T(8,128)(2,1)} %copy-done, bf16[2,4,112,768]{3,2,1,0:T(8,128)(2,1)} %copy-done.3, bf16[2,4,112,768]{3,2,1,0:T(8,128)(2,1)} %collective-permute-done.11.other_low, ...), custom_call_target="tpu_custom_call" | custom-call | flops 1000000000 | bytes 11000000 | tf_op jit(solution)/shard_map/assemble/pallas_call | solution.py:254
  80.2 6.1 %collective-permute-done.14.u1 = bf16[2,4,96,768]{3,2,1,0:T(8,128)(2,1)} collective-permute-done((bf16[2,4,96,768]{3,2,1,0:T(8,128)(2,1)}, bf16[2,4,96,768]{3,2,1,0:T(8,128)(2,1)}, u32[]{:S(2)}, u32[]{:S(2)}) %collective-permute-start.14) | collective-permute-done | bytes 1179680 | tf_op jit(solution)/shard_map/ppermute | solution.py:164
  86.3 1.5 slice_bitcast_fusion.1
  89.3 24.1 %attend.1 = (bf16[1024,768]{1,0:T(8,128)(2,1)}, bf16[1024,768]{1,0:T(8,128)(2,1)}, bf16[1024,768]{1,0:T(8,128)(2,1)}, bf16[1024,768]{1,0:T(8,128)(2,1)}, f32[128,1024]{1,0:T(8,128)}) custom-call(s32[1]{0:T(128)S(6)} %copy.40.bucket, s32[8]{0:T(128)} %bitcast.130, bf16[1024,768]{1,0:T(8,128)(2,1)} %x.1, bf16[4,768,768]{2,1,0:T(8,128)(2,1)} %get-tuple-element.367.qw.kw.vw.ow, ...), custom_call_target="tpu_custom_call" | custom-call | flops 15000000512 | bytes 12000000 | tf_op jit(solution)/shard_map/attend/pallas_call | solution.py:382
  115.8 26.2 %up.1 = (f32[1024,768]{1,0:T(8,128)}, f32[1024,128]{1,0:T(8,128)}, bf16[1024,768]{1,0:T(8,128)(2,1)}, bf16[8,1024,384]{2,1,0:T(8,128)(2,1)}, bf16[8,1024,384]{2,...) custom-call(s32[24]{0:T(128)} %concatenate.27.place, bf16[1024,768]{1,0:T(8,128)(2,1)} %x.1, ...), custom_call_target="tpu_custom_call" | custom-call | flops 12000000000 | bytes 31000000 | tf_op jit(solution)/shard_map/up/pallas_call | solution.py:538
  142.6 2.6 copy.39
  146.9 31.6 %down.1 = (bf16[1024,768]{1,0:T(8,128)(2,1)}, f32[8,768]{1,0:T(8,128)}, f32[1024,768]{1,0:T(8,128)}, bf16[1024,768]{1,0:T(8,128)(2,1)}, f32[1,768]{1,0:T(1,128)}...) custom-call(s32[24]{0:T(128)} %concatenate.27.place, ...), custom_call_target="tpu_custom_call" | custom-call | flops 12000000000 | bytes 35000000 | tf_op jit(solution)/shard_map/down/pallas_call | solution.py:648
  178.7 31.1 %feed_back.1 = (bf16[4,4,96,768]{3,2,1,0:T(8,128)(2,1)}, bf16[4,4,96,768]{3,2,1,0:T(8,128)(2,1)}, f32[4,1,768]{2,1,0:T(1,128)}, f32[1024,768]{1,0:T(8,128)}) custom-call(s32[24]{0:T(128)} %concatenate.27.place, bf16[1024,768]{1,0:T(8,128)(2,1)} %get-tuple-element.320.branch, bf16[8,1024,384]{2,1,0:T(8,128)(2,1)} %get-tuple-element.321.slope, ...), custom_call_target="tpu_custom_call" | custom-call | flops 15000000512 | bytes 35000000 | tf_op jit(solution)/shard_map/feed_back/pallas_call | solution.py:710
  209.8 3.3 add_convert_fusion.4
  213.5 1.5 collective-permute-start.22
  215.0 2.6 copy.38
  218.2 10.7 %inner_back.1 = (f32[1024,768]{1,0:T(8,128)}, f32[1,768]{1,0:T(1,128)}, f32[1,768]{1,0:T(1,128)}, f32[1,768]{1,0:T(1,128)}, bf16[768,768]{1,0:T(8,128)(2,1)}, /*...) custom-call(f32[1024,768]{1,0:T(8,128)} %get-tuple-element.336.grad_normed, f32[1024,768]{1,0:T(8,128)} %get-tuple-element.337.n1, ...), custom_call_target="tpu_custom_call" | custom-call | flops 4000000000 | bytes 20000000 | tf_op jit(solution)/shard_map/inner_back/pallas_call | solution.py:765
  230.0 1.4 copy-done.2
  231.4 3.0 add_convert_fusion.2
  234.4 2.3 add_convert_fusion.10
  236.8 1.5 collective-permute-start.25
  239.5 37.9 %attend_back.1 = (bf16[768,768]{1,0:T(8,128)(2,1)}, bf16[768,768]{1,0:T(8,128)(2,1)}, bf16[768,768]{1,0:T(8,128)(2,1)}, f32[1,768]{1,0:T(1,128)}, f32[1,768]{1,0:T(1,128)}, /*index=5*/f32[1024,768]{1,0:T(8,128)}) custom-call(s32[1]{0:T(128)S(6)} %copy.40.bucket, s32[8]{0:T(128)} %bitcast.132, bf16[768,1024]{1,0:T(8,128)(2,1)} %bitcast.97, ...), custom_call_target="tpu_custom_call" | custom-call | flops 30000001024 | bytes 25000000 | tf_op jit(solution)/shard_map/attend_back/pallas_call | solution.py:458
  278.6 1.6 add_convert_fusion.8
  283.0 4.7 %collective-permute-start.26 = (bf16[192,384]{1,0:T(8,128)(2,1)S(1)}, bf16[192,384]{1,0:T(8,128)(2,1)S(1)}, u32[]{:S(2)}, u32[]{:S(2)}) collective-permute-start(bf16[192,384]{1,0:T(8,128)(2,1)S(1)} %get-tuple-element.402), channel_id=1, source_target_pairs={{0,24},{4,28},{8,0},{12,4},{16,8},{20,12},{24,16},{28,20},{1,25},{... | collective-permute-start | bytes 442376 | tf_op jit(solution)/shard_map/ppermute | solution.py:164
  288.3 8.8 %pack.1 = (bf16[4,4,112,768]{3,2,1,0:T(8,128)(2,1)}, bf16[4,4,112,768]{3,2,1,0:T(8,128)(2,1)}) custom-call(s32[24]{0:T(128)} %concatenate.27.place, bf16[768,768]{1,0:T(8,128)(2,1)} %get-tuple-element.394.gq, bf16[768,768]{1,0:T(8,128)(2,1)} %get-tuple-element.395.gk, bf16[768,768]{1,0:T(8,128)(2,1)} %get-tuple-element.396.gv, ...), custom_call_target="tpu_custom_call" | custom-call | flops 1000000000 | bytes 11000000 | tf_op jit(solution)/shard_map/pack/pallas_call | solution.py:295
  297.1 1.5 collective-permute-done.27
  298.9 1.8 collective-permute-start.31
  302.7 2.4 collective-permute-done.31
  305.1 10.3 %collective-permute-done.32 = bf16[96,768]{1,0:T(8,128)(2,1)S(1)} collective-permute-done((bf16[96,768]{1,0:T(8,128)(2,1)S(1)}, bf16[96,768]{1,0:T(8,128)(2,1)S(1)}, u32[]{:S(2)}, u32[]{:S(2)}) %collective-permute-start.32) | collective-permute-done | bytes 147488 | tf_op jit(solution)/shard_map/ppermute | solution.py:164
  315.5 2.5 add_convert_fusion.1
  318.8 17.6 %collective-permute-done.34 = bf16[2,4,112,768]{3,2,1,0:T(8,128)(2,1)S(1)} collective-permute-done((bf16[2,4,112,768]{3,2,1,0:T(8,128)(2,1)S(1)}, bf16[2,4,112,768]{3,2,1,0:T(8,128)(2,1)S(1)}, u32[]{:S(2)}, u32[]{:S(2)}) %collective-permute-start.34) | collective-permute-done | bytes 1376288 | tf_op jit(solution)/shard_map/ppermute | solution.py:164
  337.5 1.7 fusion.4
  339.2 8.5 %collective-permute-done.35 = bf16[1,4,112,768]{3,2,1,0:T(8,128)(2,1)S(1)} collective-permute-done((bf16[1,4,112,768]{3,2,1,0:T(8,128)(2,1)S(1)}, bf16[1,4,112,768]{3,2,1,0:T(8,128)(2,1)S(1)}, u32[]{:S(2)}, u32[]{:S(2)}) %collective-permute-start.35) | collective-permute-done | bytes 688160 | tf_op jit(solution)/shard_map/ppermute | solution.py:164
  348.0 1.9 collective-permute-start.37
  349.9 1.9 collective-permute-start.38
  352.6 1.2 collective-permute-done.36
  353.8 9.9 %collective-permute-done.37 = bf16[112,768]{1,0:T(8,128)(2,1)S(1)} collective-permute-done((bf16[112,768]{1,0:T(8,128)(2,1)S(1)}, bf16[112,768]{1,0:T(8,128)(2,1)S(1)}, u32[]{:S(2)}, u32[]{:S(2)}) %collective-permute-start.37) | collective-permute-done | bytes 172064 | tf_op jit(solution)/shard_map/ppermute | solution.py:164
  (135 shorter events, 30.4 us)
Async XLA Ops:
  0.7 22.2 %copy-start.7 = (bf16[96,768]{1,0:T(8,128)(2,1)S(1)}, bf16[96,768]{1,0:T(8,128)(2,1)}, u32[]{:S(2)}) copy-start(bf16[96,768]{1,0:T(8,128)(2,1)} %param.32) | copy-start | bytes 442372
  4.2 10.4 %collective-permute-start = (bf16[112,768]{1,0:T(8,128)(2,1)S(1)}, bf16[112,768]{1,0:T(8,128)(2,1)S(1)}, u32[]{:S(2)}, u32[]{:S(2)}) collective-permute-start(bf16[112,768]{1,0:T(8,128)(2,1)S(1)} %concatenate.31), channel_id=1, source_target_pairs={{0,8},{4,12},{8,16},{12,20},{16,24},{20,28},{24,0},{28,4},{1,9},{5... | collective-permute-start | bytes 516104 | tf_op jit(solution)/shard_map/ppermute | solution.py:164
  7.3 13.9 %collective-permute-start.1 = (bf16[112,768]{1,0:T(8,128)(2,1)S(1)}, bf16[112,768]{1,0:T(8,128)(2,1)S(1)}, u32[]{:S(2)}, u32[]{:S(2)}) collective-permute-start(bf16[112,768]{1,0:T(8,128)(2,1)S(1)} %concatenate.31), channel_id=1, source_target_pairs={{0,16},{4,20},{8,24},{12,28},{16,0},{20,4},{24,8},{28,12},{1,17},{... | collective-permute-start | bytes 516104 | tf_op jit(solution)/shard_map/ppermute | solution.py:164
  9.9 11.3 %collective-permute-start.2 = (bf16[112,768]{1,0:T(8,128)(2,1)S(1)}, bf16[112,768]{1,0:T(8,128)(2,1)S(1)}, u32[]{:S(2)}, u32[]{:S(2)}) collective-permute-start(bf16[112,768]{1,0:T(8,128)(2,1)S(1)} %concatenate.31), channel_id=1, source_target_pairs={{0,24},{4,28},{8,0},{12,4},{16,8},{20,12},{24,16},{28,20},{1,25},{... | collective-permute-start | bytes 516104 | tf_op jit(solution)/shard_map/ppermute | solution.py:164
  21.3 17.3 %copy-start.8 = (bf16[384,192]{0,1:T(8,128)(2,1)S(1)}, bf16[384,192]{0,1:T(8,128)(2,1)}, u32[]{:S(2)}) copy-start(bf16[384,192]{0,1:T(8,128)(2,1)} %param.34) | copy-start | bytes 442372
  21.3 16.3 %collective-permute-start.3 = (bf16[1,4,112,768]{3,2,1,0:T(8,128)(2,1)S(1)}, bf16[1,4,112,768]{3,2,1,0:T(8,128)(2,1)S(1)}, u32[]{:S(2)}, u32[]{:S(2)}) collective-permute-start(bf16[1,4,112,768]{3,2,1,0:T(8,128)(2,1)S(1)} %maximum_bitcast_fusion), channel_id=1, source_target_pairs={{0,1},{1,0},{2,3},{3,2},{4,6},{5,7},{6,4},{7,5},{8,9},{9,8},{10,11... | collective-permute-start | bytes 2064392 | tf_op jit(solution)/shard_map/ppermute | solution.py:164
  22.8 9.9 %collective-permute-start.4 = (bf16[96,768]{1,0:T(8,128)(2,1)S(1)}, bf16[96,768]{1,0:T(8,128)(2,1)S(1)}, u32[]{:S(2)}, u32[]{:S(2)}) collective-permute-start(bf16[96,768]{1,0:T(8,128)(2,1)S(1)} %copy-done.7), channel_id=1, source_target_pairs={{0,8},{4,12},{8,16},{12,20},{16,24},{20,28},{24,0},{28,4},{1,9},{5... | collective-permute-start | bytes 442376 | tf_op jit(solution)/shard_map/ppermute | solution.py:164
  27.0 10.6 %collective-permute-start.5 = (bf16[96,768]{1,0:T(8,128)(2,1)S(1)}, bf16[96,768]{1,0:T(8,128)(2,1)S(1)}, u32[]{:S(2)}, u32[]{:S(2)}) collective-permute-start(bf16[96,768]{1,0:T(8,128)(2,1)S(1)} %copy-done.7), channel_id=1, source_target_pairs={{0,16},{4,20},{8,24},{12,28},{16,0},{20,4},{24,8},{28,12},{1,17},{... | collective-permute-start | bytes 442376 | tf_op jit(solution)/shard_map/ppermute | solution.py:164
  28.6 9.0 %collective-permute-start.6 = (bf16[96,768]{1,0:T(8,128)(2,1)S(1)}, bf16[96,768]{1,0:T(8,128)(2,1)S(1)}, u32[]{:S(2)}, u32[]{:S(2)}) collective-permute-start(bf16[96,768]{1,0:T(8,128)(2,1)S(1)} %copy-done.7), channel_id=1, source_target_pairs={{0,24},{4,28},{8,0},{12,4},{16,8},{20,12},{24,16},{28,20},{1,25},{... | collective-permute-start | bytes 442376 | tf_op jit(solution)/shard_map/ppermute | solution.py:164
  37.7 32.0 %copy-start = (bf16[2,4,112,768]{3,2,1,0:T(8,128)(2,1)}, bf16[2,4,112,768]{3,2,1,0:T(8,128)(2,1)S(1)}, u32[]{:S(2)}) copy-start(bf16[2,4,112,768]{3,2,1,0:T(8,128)(2,1)S(1)} %pad_maximum_fusion.own_low) | copy-start | bytes 4128772
  37.7 19.2 %collective-permute-start.7 = (bf16[2,4,112,768]{3,2,1,0:T(8,128)(2,1)S(1)}, bf16[2,4,112,768]{3,2,1,0:T(8,128)(2,1)S(1)}, u32[]{:S(2)}, u32[]{:S(2)}) collective-permute-start(bf16[2,4,112,768]{3,2,1,0:T(8,128)(2,1)S(1)} %pad_maximum_fusion.own_low), channel_id=1, source_target_pairs={{0,2},{1,3},{2,0},{3,1},{4,5},{5,4},{6,7},{7,6},{8,10},{9,11},{10,... | collective-permute-start | bytes 4128776 | tf_op jit(solution)/shard_map/ppermute | solution.py:164
  38.6 9.0 %collective-permute-start.10 = (bf16[192,384]{1,0:T(8,128)(2,1)S(1)}, bf16[192,384]{1,0:T(8,128)(2,1)S(1)}, u32[]{:S(2)}, u32[]{:S(2)}) collective-permute-start(bf16[192,384]{1,0:T(8,128)(2,1)S(1)} %bitcast.104), channel_id=1, source_target_pairs={{0,24},{4,28},{8,0},{12,4},{16,8},{20,12},{24,16},{28,20},{1,25},{... | collective-permute-start | bytes 442376 | tf_op jit(solution)/shard_map/ppermute | solution.py:164
  43.3 8.5 %collective-permute-start.8 = (bf16[192,384]{1,0:T(8,128)(2,1)S(1)}, bf16[192,384]{1,0:T(8,128)(2,1)S(1)}, u32[]{:S(2)}, u32[]{:S(2)}) collective-permute-start(bf16[192,384]{1,0:T(8,128)(2,1)S(1)} %bitcast.105), channel_id=1, source_target_pairs={{0,8},{4,12},{8,16},{12,20},{16,24},{20,28},{24,0},{28,4},{1,9},{5... | collective-permute-start | bytes 442376 | tf_op jit(solution)/shard_map/ppermute | solution.py:164
  43.3 13.6 %collective-permute-start.9 = (bf16[192,384]{1,0:T(8,128)(2,1)S(1)}, bf16[192,384]{1,0:T(8,128)(2,1)S(1)}, u32[]{:S(2)}, u32[]{:S(2)}) collective-permute-start(bf16[192,384]{1,0:T(8,128)(2,1)S(1)} %bitcast.106), channel_id=1, source_target_pairs={{0,16},{4,20},{8,24},{12,28},{16,0},{20,4},{24,8},{28,12},{1,17},{... | collective-permute-start | bytes 442376 | tf_op jit(solution)/shard_map/ppermute | solution.py:164
  44.0 27.3 %copy-start.9 = (bf16[384,192]{0,1:T(8,128)(2,1)S(1)}, bf16[384,192]{0,1:T(8,128)(2,1)}, u32[]{:S(2)}) copy-start(bf16[384,192]{0,1:T(8,128)(2,1)} %param.34) | copy-start | bytes 442372
  57.0 14.5 %copy-start.3 = (bf16[2,4,112,768]{3,2,1,0:T(8,128)(2,1)}, bf16[2,4,112,768]{3,2,1,0:T(8,128)(2,1)S(1)}, u32[]{:S(2)}) copy-start(bf16[2,4,112,768]{3,2,1,0:T(8,128)(2,1)S(1)} %collective-permute-done.7.own_high) | copy-start | bytes 4128772
  57.0 10.6 %collective-permute-start.11 = (bf16[2,4,112,768]{3,2,1,0:T(8,128)(2,1)S(1)}, bf16[2,4,112,768]{3,2,1,0:T(8,128)(2,1)}, u32[]{:S(2)}, u32[]{:S(2)}) collective-permute-start(bf16[2,4,112,768]{3,2,1,0:T(8,128)(2,1)S(1)} %pad_maximum_fusion.own_low), channel_id=1, source_target_pairs={{0,4},{4,0},{8,12},{12,8},{16,20},{20,16},{24,28},{28,24},{1,5},{5... | collective-permute-start | bytes 4128776 | tf_op jit(solution)/shard_map/ppermute | solution.py:164
  57.1 10.5 %collective-permute-start.12 = (bf16[2,4,112,768]{3,2,1,0:T(8,128)(2,1)S(1)}, bf16[2,4,112,768]{3,2,1,0:T(8,128)(2,1)}, u32[]{:S(2)}, u32[]{:S(2)}) collective-permute-start(bf16[2,4,112,768]{3,2,1,0:T(8,128)(2,1)S(1)} %collective-permute-done.7.own_high), channel_id=1, source_target_pairs={{0,4},{4,0},{8,12},{12,8},{16,20},{20,16},{24,28},{28,24},{1,5},{5... | collective-permute-start | bytes 4128776 | tf_op jit(solution)/shard_map/ppermute | solution.py:164
  57.6 10.0 %collective-permute-start.13 = (bf16[1,4,96,768]{3,2,1,0:T(8,128)(2,1)S(1)}, bf16[1,4,96,768]{3,2,1,0:T(8,128)(2,1)}, u32[]{:S(2)}, u32[]{:S(2)}) collective-permute-start(bf16[1,4,96,768]{3,2,1,0:T(8,128)(2,1)S(1)} %maximum_bitcast_fusion.1), channel_id=1, source_target_pairs={{0,1},{1,0},{2,3},{3,2},{4,6},{5,7},{6,4},{7,5},{8,9},{9,8},{10,11... | collective-permute-start | bytes 1769480 | tf_op jit(solution)/shard_map/ppermute | solution.py:164
  59.1 12.2 %copy-start.15 = (bf16[192,384]{1,0:T(8,128)(2,1)S(1)}, bf16[192,384]{1,0:T(8,128)(2,1)}, u32[]{:S(2)}) copy-start(bf16[192,384]{1,0:T(8,128)(2,1)} %copy-done.14) | copy-start | bytes 442372
  69.8 16.5 %collective-permute-start.14 = (bf16[2,4,96,768]{3,2,1,0:T(8,128)(2,1)}, bf16[2,4,96,768]{3,2,1,0:T(8,128)(2,1)}, u32[]{:S(2)}, u32[]{:S(2)}) collective-permute-start(bf16[2,4,96,768]{3,2,1,0:T(8,128)(2,1)} %pad_maximum_fusion.1.u0), channel_id=1, source_target_pairs={{0,2},{1,3},{2,0},{3,1},{4,5},{5,4},{6,7},{7,6},{8,10},{9,11},{10,... | collective-permute-start | bytes 3538952 | tf_op jit(solution)/shard_map/ppermute | solution.py:164
  87.8 25.5 %copy-start.6 = (f32[4,16,768]{2,1,0:T(8,128)S(1)}, f32[4,16,768]{2,1,0:T(8,128)}, u32[]{:S(2)}) copy-start(f32[4,16,768]{2,1,0:T(8,128)} %get-tuple-element.277) | copy-start | bytes 589828
  87.8 26.3 %collective-permute-start.15 = (bf16[2,4,96,768]{3,2,1,0:T(8,128)(2,1)}, bf16[2,4,96,768]{3,2,1,0:T(8,128)(2,1)S(1)}, u32[]{:S(2)}, u32[]{:S(2)}) collective-permute-start(bf16[2,4,96,768]{3,2,1,0:T(8,128)(2,1)} %pad_maximum_fusion.1.u0), channel_id=1, source_target_pairs={{0,4},{4,0},{8,12},{12,8},{16,20},{20,16},{24,28},{28,24},{1,5},{5... | collective-permute-start | bytes 3538952 | tf_op jit(solution)/shard_map/ppermute | solution.py:164
  87.9 26.2 %collective-permute-start.16 = (bf16[2,4,96,768]{3,2,1,0:T(8,128)(2,1)}, bf16[2,4,96,768]{3,2,1,0:T(8,128)(2,1)}, u32[]{:S(2)}, u32[]{:S(2)}) collective-permute-start(bf16[2,4,96,768]{3,2,1,0:T(8,128)(2,1)} %collective-permute-done.14.u1), channel_id=1, source_target_pairs={{0,4},{4,0},{8,12},{12,8},{16,20},{20,16},{24,28},{28,24},{1,5},{5... | collective-permute-start | bytes 3538952 | tf_op jit(solution)/shard_map/ppermute | solution.py:164
  88.4 25.7 %collective-permute-start.17 = (bf16[1,4,192,384]{3,2,1,0:T(8,128)(2,1)S(1)}, bf16[1,4,192,384]{3,2,1,0:T(8,128)(2,1)S(1)}, u32[]{:S(2)}, u32[]{:S(2)}) collective-permute-start(bf16[1,4,192,384]{3,2,1,0:T(8,128)(2,1)S(1)} %maximum_bitcast_fusion.2), channel_id=1, source_target_pairs={{0,1},{1,0},{2,3},{3,2},{4,6},{5,7},{6,4},{7,5},{8,9},{9,8},{10,11... | collective-permute-start | bytes 1769480 | tf_op jit(solution)/shard_map/ppermute | solution.py:164
  115.2 26.8 %copy-start.5 = (bf16[2,4,192,384]{3,2,1,0:T(8,128)(2,1)}, bf16[2,4,192,384]{3,2,1,0:T(8,128)(2,1)S(1)}, u32[]{:S(2)}) copy-start(bf16[2,4,192,384]{3,2,1,0:T(8,128)(2,1)S(1)} %pad_maximum_fusion.2.d0) | copy-start | bytes 3538948
  115.2 26.7 %collective-permute-start.18 = (bf16[2,4,192,384]{3,2,1,0:T(8,128)(2,1)S(1)}, bf16[2,4,192,384]{3,2,1,0:T(8,128)(2,1)S(1)}, u32[]{:S(2)}, u32[]{:S(2)}) collective-permute-start(bf16[2,4,192,384]{3,2,1,0:T(8,128)(2,1)S(1)} %pad_maximum_fusion.2.d0), channel_id=1, source_target_pairs={{0,2},{1,3},{2,0},{3,1},{4,5},{5,4},{6,7},{7,6},{8,10},{9,11},{10,... | collective-permute-start | bytes 3538952 | tf_op jit(solution)/shard_map/ppermute | solution.py:164
  142.0 3.8 %collective-permute-start.19 = (bf16[2,4,192,384]{3,2,1,0:T(8,128)(2,1)S(1)}, bf16[2,4,192,384]{3,2,1,0:T(8,128)(2,1)S(1)}, u32[]{:S(2)}, u32[]{:S(2)}) collective-permute-start(bf16[2,4,192,384]{3,2,1,0:T(8,128)(2,1)S(1)} %pad_maximum_fusion.2.d0), channel_id=1, source_target_pairs={{0,4},{4,0},{8,12},{12,8},{16,20},{20,16},{24,28},{28,24},{1,5},{5... | collective-permute-start | bytes 3538952 | tf_op jit(solution)/shard_map/ppermute | solution.py:164
  142.1 4.7 %collective-permute-start.20 = (bf16[2,4,192,384]{3,2,1,0:T(8,128)(2,1)S(1)}, bf16[2,4,192,384]{3,2,1,0:T(8,128)(2,1)}, u32[]{:S(2)}, u32[]{:S(2)}) collective-permute-start(bf16[2,4,192,384]{3,2,1,0:T(8,128)(2,1)S(1)} %collective-permute-done.18.d1), channel_id=1, source_target_pairs={{0,4},{4,0},{8,12},{12,8},{16,20},{20,16},{24,28},{28,24},{1,5},{5... | collective-permute-start | bytes 3538952 | tf_op jit(solution)/shard_map/ppermute | solution.py:164
  178.5 31.3 %collective-permute-start.21 = (bf16[4,4,192,384]{3,2,1,0:T(8,128)(2,1)}, bf16[4,4,192,384]{3,2,1,0:T(8,128)(2,1)}, u32[]{:S(2)}, u32[]{:S(2)}) collective-permute-start(bf16[4,4,192,384]{3,2,1,0:T(8,128)(2,1)} %get-tuple-element.330), channel_id=1, source_target_pairs={{0,4},{4,0},{8,12},{12,8},{16,20},{20,16},{24,28},{28,24},{1,5},{5... | collective-permute-start | bytes 7077896 | tf_op jit(solution)/shard_map/ppermute | solution.py:164
  178.7 31.1 %copy-start.1 = (bf16[4,4,192,384]{3,2,1,0:T(8,128)(2,1)S(1)}, bf16[4,4,192,384]{3,2,1,0:T(8,128)(2,1)}, u32[]{:S(2)}) copy-start(bf16[4,4,192,384]{3,2,1,0:T(8,128)(2,1)} %get-tuple-element.333) | copy-start | bytes 7077892
  213.1 16.9 %collective-permute-start.23 = (bf16[4,4,96,768]{3,2,1,0:T(8,128)(2,1)}, bf16[4,4,96,768]{3,2,1,0:T(8,128)(2,1)S(1)}, u32[]{:S(2)}, u32[]{:S(2)}) collective-permute-start(bf16[4,4,96,768]{3,2,1,0:T(8,128)(2,1)} %get-tuple-element.350), channel_id=1, source_target_pairs={{0,4},{4,0},{8,12},{12,8},{16,20},{20,16},{24,28},{28,24},{1,5},{5... | collective-permute-start | bytes 7077896 | tf_op jit(solution)/shard_map/ppermute | solution.py:164
  213.5 16.5 %collective-permute-start.22 = (bf16[2,4,192,384]{3,2,1,0:T(8,128)(2,1)}, bf16[2,4,192,384]{3,2,1,0:T(8,128)(2,1)}, u32[]{:S(2)}, u32[]{:S(2)}) collective-permute-start(bf16[2,4,192,384]{3,2,1,0:T(8,128)(2,1)} %get-tuple-element.349), channel_id=1, source_target_pairs={{0,2},{1,3},{2,0},{3,1},{4,5},{5,4},{6,7},{7,6},{8,10},{9,11},{10,... | collective-permute-start | bytes 3538952 | tf_op jit(solution)/shard_map/ppermute | solution.py:164
  236.8 40.7 %collective-permute-start.25 = (bf16[2,4,96,768]{3,2,1,0:T(8,128)(2,1)S(1)}, bf16[2,4,96,768]{3,2,1,0:T(8,128)(2,1)S(1)}, u32[]{:S(2)}, u32[]{:S(2)}) collective-permute-start(bf16[2,4,96,768]{3,2,1,0:T(8,128)(2,1)S(1)} %get-tuple-element.376), channel_id=1, source_target_pairs={{0,2},{1,3},{2,0},{3,1},{4,5},{5,4},{6,7},{7,6},{8,10},{9,11},{10,... | collective-permute-start | bytes 3538952 | tf_op jit(solution)/shard_map/ppermute | solution.py:164
  238.3 39.1 %collective-permute-start.24 = (bf16[1,4,192,384]{3,2,1,0:T(8,128)(2,1)}, bf16[1,4,192,384]{3,2,1,0:T(8,128)(2,1)}, u32[]{:S(2)}, u32[]{:S(2)}) collective-permute-start(bf16[1,4,192,384]{3,2,1,0:T(8,128)(2,1)} %get-tuple-element.375), channel_id=1, source_target_pairs={{0,1},{1,0},{2,3},{3,2},{4,6},{5,7},{6,4},{7,5},{8,9},{9,8},{10,11... | collective-permute-start | bytes 1769480 | tf_op jit(solution)/shard_map/ppermute | solution.py:164
  282.2 16.5 %collective-permute-start.29 = (bf16[1,4,96,768]{3,2,1,0:T(8,128)(2,1)S(1)}, bf16[1,4,96,768]{3,2,1,0:T(8,128)(2,1)S(1)}, u32[]{:S(2)}, u32[]{:S(2)}) collective-permute-start(bf16[1,4,96,768]{3,2,1,0:T(8,128)(2,1)S(1)} %get-tuple-element.405), channel_id=1, source_target_pairs={{0,1},{1,0},{2,3},{3,2},{4,6},{5,7},{6,4},{7,5},{8,9},{9,8},{10,11... | collective-permute-start | bytes 1769480 | tf_op jit(solution)/shard_map/ppermute | solution.py:164
  283.0 14.1 %collective-permute-start.26 = (bf16[192,384]{1,0:T(8,128)(2,1)S(1)}, bf16[192,384]{1,0:T(8,128)(2,1)S(1)}, u32[]{:S(2)}, u32[]{:S(2)}) collective-permute-start(bf16[192,384]{1,0:T(8,128)(2,1)S(1)} %get-tuple-element.402), channel_id=1, source_target_pairs={{0,24},{4,28},{8,0},{12,4},{16,8},{20,12},{24,16},{28,20},{1,25},{... | collective-permute-start | bytes 442376 | tf_op jit(solution)/shard_map/ppermute | solution.py:164
  287.7 11.0 %collective-permute-start.27 = (bf16[192,384]{1,0:T(8,128)(2,1)S(1)}, bf16[192,384]{1,0:T(8,128)(2,1)S(1)}, u32[]{:S(2)}, u32[]{:S(2)}) collective-permute-start(bf16[192,384]{1,0:T(8,128)(2,1)S(1)} %get-tuple-element.403), channel_id=1, source_target_pairs={{0,16},{4,20},{8,24},{12,28},{16,0},{20,4},{24,8},{28,12},{1,17},{... | collective-permute-start | bytes 442376 | tf_op jit(solution)/shard_map/ppermute | solution.py:164
  287.7 11.0 %collective-permute-start.28 = (bf16[192,384]{1,0:T(8,128)(2,1)S(1)}, bf16[192,384]{1,0:T(8,128)(2,1)S(1)}, u32[]{:S(2)}, u32[]{:S(2)}) collective-permute-start(bf16[192,384]{1,0:T(8,128)(2,1)S(1)} %get-tuple-element.404), channel_id=1, source_target_pairs={{0,8},{4,12},{8,16},{12,20},{16,24},{20,28},{24,0},{28,4},{1,9},{5... | collective-permute-start | bytes 442376 | tf_op jit(solution)/shard_map/ppermute | solution.py:164
  298.8 16.7 %collective-permute-start.30 = (bf16[4,4,112,768]{3,2,1,0:T(8,128)(2,1)}, bf16[4,4,112,768]{3,2,1,0:T(8,128)(2,1)S(1)}, u32[]{:S(2)}, u32[]{:S(2)}) collective-permute-start(bf16[4,4,112,768]{3,2,1,0:T(8,128)(2,1)} %get-tuple-element.409), channel_id=1, source_target_pairs={{0,4},{4,0},{8,12},{12,8},{16,20},{20,16},{24,28},{28,24},{1,5},{5... | collective-permute-start | bytes 8257544 | tf_op jit(solution)/shard_map/ppermute | solution.py:164
  298.9 6.3 %collective-permute-start.31 = (bf16[96,768]{1,0:T(8,128)(2,1)S(1)}, bf16[96,768]{1,0:T(8,128)(2,1)S(1)}, u32[]{:S(2)}, u32[]{:S(2)}) collective-permute-start(bf16[96,768]{1,0:T(8,128)(2,1)S(1)} %get-tuple-element.410), channel_id=1, source_target_pairs={{0,24},{4,28},{8,0},{12,4},{16,8},{20,12},{24,16},{28,20},{1,25},{... | collective-permute-start | bytes 442376 | tf_op jit(solution)/shard_map/ppermute | solution.py:164
  300.7 14.8 %collective-permute-start.32 = (bf16[96,768]{1,0:T(8,128)(2,1)S(1)}, bf16[96,768]{1,0:T(8,128)(2,1)S(1)}, u32[]{:S(2)}, u32[]{:S(2)}) collective-permute-start(bf16[96,768]{1,0:T(8,128)(2,1)S(1)} %get-tuple-element.411), channel_id=1, source_target_pairs={{0,16},{4,20},{8,24},{12,28},{16,0},{20,4},{24,8},{28,12},{1,17},{... | collective-permute-start | bytes 442376 | tf_op jit(solution)/shard_map/ppermute | solution.py:164
  301.8 13.7 %collective-permute-start.33 = (bf16[96,768]{1,0:T(8,128)(2,1)S(1)}, bf16[96,768]{1,0:T(8,128)(2,1)S(1)}, u32[]{:S(2)}, u32[]{:S(2)}) collective-permute-start(bf16[96,768]{1,0:T(8,128)(2,1)S(1)} %get-tuple-element.412), channel_id=1, source_target_pairs={{0,8},{4,12},{8,16},{12,20},{16,24},{20,28},{24,0},{28,4},{1,9},{5... | collective-permute-start | bytes 442376 | tf_op jit(solution)/shard_map/ppermute | solution.py:164
  318.0 18.4 %collective-permute-start.34 = (bf16[2,4,112,768]{3,2,1,0:T(8,128)(2,1)S(1)}, bf16[2,4,112,768]{3,2,1,0:T(8,128)(2,1)S(1)}, u32[]{:S(2)}, u32[]{:S(2)}) collective-permute-start(bf16[2,4,112,768]{3,2,1,0:T(8,128)(2,1)S(1)} %get-tuple-element.427), channel_id=1, source_target_pairs={{0,2},{1,3},{2,0},{3,1},{4,5},{5,4},{6,7},{7,6},{8,10},{9,11},{10,... | collective-permute-start | bytes 4128776 | tf_op jit(solution)/shard_map/ppermute | solution.py:164
  336.8 11.0 %collective-permute-start.35 = (bf16[1,4,112,768]{3,2,1,0:T(8,128)(2,1)S(1)}, bf16[1,4,112,768]{3,2,1,0:T(8,128)(2,1)S(1)}, u32[]{:S(2)}, u32[]{:S(2)}) collective-permute-start(bf16[1,4,112,768]{3,2,1,0:T(8,128)(2,1)S(1)} %get-tuple-element.433), channel_id=1, source_target_pairs={{0,1},{1,0},{2,3},{3,2},{4,6},{5,7},{6,4},{7,5},{8,9},{9,8},{10,11... | collective-permute-start | bytes 2064392 | tf_op jit(solution)/shard_map/ppermute | solution.py:164
  347.9 5.9 %collective-permute-start.36 = (bf16[112,768]{1,0:T(8,128)(2,1)S(1)}, bf16[112,768]{1,0:T(8,128)(2,1)S(1)}, u32[]{:S(2)}, u32[]{:S(2)}) collective-permute-start(bf16[112,768]{1,0:T(8,128)(2,1)S(1)} %get-tuple-element.414), channel_id=1, source_target_pairs={{0,24},{4,28},{8,0},{12,4},{16,8},{20,12},{24,16},{28,20},{1,25},{... | collective-permute-start | bytes 516104 | tf_op jit(solution)/shard_map/ppermute | solution.py:164
  348.0 15.8 %collective-permute-start.37 = (bf16[112,768]{1,0:T(8,128)(2,1)S(1)}, bf16[112,768]{1,0:T(8,128)(2,1)S(1)}, u32[]{:S(2)}, u32[]{:S(2)}) collective-permute-start(bf16[112,768]{1,0:T(8,128)(2,1)S(1)} %get-tuple-element.415), channel_id=1, source_target_pairs={{0,16},{4,20},{8,24},{12,28},{16,0},{20,4},{24,8},{28,12},{1,17},{... | collective-permute-start | bytes 516104 | tf_op jit(solution)/shard_map/ppermute | solution.py:164
  349.9 13.9 %collective-permute-start.38 = (bf16[112,768]{1,0:T(8,128)(2,1)S(1)}, bf16[112,768]{1,0:T(8,128)(2,1)S(1)}, u32[]{:S(2)}, u32[]{:S(2)}) collective-permute-start(bf16[112,768]{1,0:T(8,128)(2,1)S(1)} %get-tuple-element.416), channel_id=1, source_target_pairs={{0,8},{4,12},{8,16},{12,20},{16,24},{20,28},{24,0},{28,4},{1,9},{5... | collective-permute-start | bytes 516104 | tf_op jit(solution)/shard_map/ppermute | solution.py:164
  (19 other events, 74.2 us)
